TPU v7x, 32 devices: a whole 2x2x4 slice. The times are simulated.
32 devices in a mesh: ctx: 16 (over z, x, core), fsdp: 2 (over y).
Axes of the slice: x: 2, y: 2, z: 4, core: 2. Of those that a mesh axis runs over, the one named last changes fastest.
Arguments:
- hidden: bfloat16 [2, 4096, 1024], P('fsdp', 'ctx'), may hold values from -6 to 6
- out_grad: bfloat16 [2, 4096, 1024], P('fsdp', 'ctx'), may hold values from -6 to 6
- decay_log: float32 [2, 24, 4096], P('fsdp', None, 'ctx'), may hold values from -1.2 to 0, as said below
- doc_lengths: int32 [2, 2], P('fsdp'), may hold values from 1 to 3072, 4096 in all within a row
- weights: float32 [1024, 12288], P(('ctx', 'fsdp')), may hold values from -2 to 2
- first_moment: float32 [1024, 12288], P(('ctx', 'fsdp')), may hold values from -8 to 8
- second_moment: float32 [1024, 12288], P(('ctx', 'fsdp')), may hold values from 0.5 to 50
- small_params: float32 [12568], replicated, may hold values from -2 to 2, as said below
- small_first: float32 [12568], replicated, may hold values from -8 to 8
- small_second: float32 [12568], replicated, may hold values from 1 to 1000
Outputs:
- out_hidden: bfloat16 [2, 4096, 1024], P('fsdp', 'ctx')
- grad_hidden: float32 [2, 4096, 1024], P('fsdp', 'ctx')
- grad_weights: float32 [1024, 12288], P(('ctx', 'fsdp'))
- new_weights: float32 [1024, 12288], P(('ctx', 'fsdp'))
- new_first: float32 [1024, 12288], P(('ctx', 'fsdp'))
- new_second: float32 [1024, 12288], P(('ctx', 'fsdp'))
- small_grads: float32 [12568], replicated
- small_step: float32 [12568], replicated
- small_first_new: float32 [12568], replicated
- small_second_new: float32 [12568], replicated
Inputs may be any that keep to these rules, and one draw needn't show every extreme that they name: `doc_lengths`: each row holds the lengths of the 2 documents of that sequence in order; they sum to 4096 and none is longer than 3072. `decay_log`: negative everywhere. `small_params`: the three gains and the skip gains are positive.
All inputs are finite; a program needn't handle non-finite values.
Results may differ from a plain program's by a relative error of at most 0.025.
Values may be sent and summed in bfloat16 or wider, within the bound.
A program may use at most 384 MiB of HBM per device.

v0:
```python
import math

import jax
import jax.numpy as jnp
from jax import lax
from jax.sharding import PartitionSpec as P

D = 1024
QUERY_HEADS = 8
KEY_VALUE_HEADS = 2
HEAD_WIDTH = 64
MH = 24
MP = 64
NS = 128
FF = 2048
CONV = 4
STEP = 3
QUERY_WIDTH = 512
KEY_WIDTH = 128
INNER = 1536
XBC = 1792
MIXIN = 4096
MIXOUT = 2048


norm_eps = 1e-05
rope_base = 100000000000.0
large_negative = -1e30
learn_rate = 0.02
beta_one = 0.9
beta_two = 0.95
adam_eps = 1e-08
decay_rate = 0.1
highest = lax.Precision.HIGHEST


def shifted(value, axis, steps):
    count = lax.axis_size(axis)
    initial, last = (max(0, -steps), min(count, count - steps))
    return lax.ppermute(value, axis, [(source, source + steps) for source in range(initial, last)])


def prefix(array, axis, join, neutral):
    place = lax.axis_index(axis)
    gathered = jax.tree.map(
        lambda a, kind: lax.all_gather(a.astype(kind), axis), array, (jnp.bfloat16, jnp.bfloat16)
    )
    state = jax.tree.map(lambda a, e: jnp.zeros_like(a) + jnp.asarray(e, a.dtype), array, neutral)

    def one(step, state):
        return join(
            state,
            jax.tree.map(
                lambda a, own: lax.dynamic_index_in_dim(a, step, 0, False).astype(own.dtype),
                gathered,
                array,
            ),
        )

    return lax.fori_loop(0, place, one, state)


def entering(array, axis, combine, identity):
    length, mine = (lax.axis_size(axis), lax.axis_index(axis))
    everything = jax.tree.map(
        lambda part, kind: lax.all_gather(part.astype(kind), axis),
        array,
        jax.tree.map(lambda a: jnp.bfloat16 if a.dtype == jnp.float32 else a.dtype, array),
    )
    start = jax.tree.map(
        lambda part, zero: jnp.broadcast_to(jnp.asarray(zero, part.dtype), part.shape),
        array,
        identity,
    )

    def step(k, before):
        at = length - 1 - k
        reached = at > mine
        new = combine(
            before, jax.tree.map(lambda part, own: part[at].astype(own.dtype), everything, array)
        )
        return jax.tree.map(lambda a, b: jnp.where(reached, a, b), new, before)

    return lax.fori_loop(0, length, step, start)


def doc_layout(lengths, token_positions):
    starts = jnp.cumsum(lengths) - lengths
    inside = token_positions[:, None] >= starts[None, :]
    document_index = jnp.sum(inside.astype(jnp.int32), axis=1) - 1
    begins = jnp.max(jnp.where(inside, starts[None, :], 0), axis=1)
    return (document_index, token_positions - begins)


def rope_tables(rel_pos):
    half_dim = HEAD_WIDTH // 2
    inv_freq = rope_base ** (-2.0 * jnp.arange(half_dim, dtype=jnp.float32) / HEAD_WIDTH)
    angles = rel_pos.astype(jnp.float32)[:, None] * inv_freq[None, :]
    return (jnp.cos(angles), jnp.sin(angles))


def apply_rotary(values, cosine_table, sine_table):
    half_dim = values.shape[-1] // 2
    lower_half = values[..., :half_dim]
    upper_half = values[..., half_dim:]
    cos_rows = cosine_table[:, None, :]
    sin_rows = sine_table[:, None, :]
    return jnp.concatenate(
        [
            lower_half * cos_rows - upper_half * sin_rows,
            upper_half * cos_rows + lower_half * sin_rows,
        ],
        axis=-1,
    )


def inverse_rotary(grads, cosine_table, sine_table):
    half_dim = grads.shape[-1] // 2
    lower_half = grads[..., :half_dim]
    upper_half = grads[..., half_dim:]
    cos_rows = cosine_table[:, None, :]
    sin_rows = sine_table[:, None, :]
    return jnp.concatenate(
        [
            lower_half * cos_rows + upper_half * sin_rows,
            upper_half * cos_rows - lower_half * sin_rows,
        ],
        axis=-1,
    )


def split_small(vector):
    widths = (D, D, INNER, CONV * XBC, XBC, MH)
    pieces = []
    offset = 0
    for span_width in widths:
        pieces.append(vector[offset : offset + span_width])
        offset += span_width
    return (pieces[0], pieces[1], pieces[2], pieces[3].reshape(CONV, XBC), pieces[4], pieces[5])


def conv_block(xbc_ext, doc_ext, document_index, conv_weights, conv_biases):
    rows_out = document_index.shape[0]
    summed = jnp.broadcast_to(conv_biases[None, :], (rows_out, conv_biases.shape[0]))
    for tap_index in range(conv_weights.shape[0]):
        same_doc = (doc_ext[tap_index : tap_index + rows_out] == document_index).astype(
            xbc_ext.dtype
        )[:, None]
        summed = (
            summed
            + conv_weights[tap_index][None, :]
            * xbc_ext[tap_index : tap_index + rows_out]
            * same_doc
        )
    return jax.nn.silu(summed)


def scan_consts(log_decay, is_start, document_index, doc_before):
    cum_decay = jnp.cumsum(log_decay, axis=1)
    steps_in = jnp.where(is_start[None, :], jnp.float32(1.0), jnp.sqrt(-jnp.expm1(2.0 * log_decay)))
    row_order = jnp.arange(document_index.shape[0], dtype=jnp.int32)
    same_mask = (document_index[:, None] == document_index[None, :]) & (
        row_order[None, :] <= row_order[:, None]
    )
    spread = jnp.minimum(cum_decay[:, :, None] - cum_decay[:, None, :], 0.0)
    decay_mat = jnp.where(same_mask[None], jnp.exp(spread), 0.0)
    decay_in = jnp.where((document_index == doc_before)[None, :], jnp.exp(cum_decay), 0.0)
    return (decay_mat, steps_in, decay_in)


def split_conv(conv_out):
    heads_x = conv_out[:, :INNER].reshape(conv_out.shape[0], MH, MP)
    return (heads_x, conv_out[:, INNER : INNER + NS], conv_out[:, INNER + NS :])


def state_local(conv_out, consts):
    decay_mat, steps_in, decay_in = consts
    heads_x, b_rows, c_rows = split_conv(conv_out)
    weight_end = decay_mat[:, -1, :] * steps_in
    return jnp.einsum("hs,shp,sn->hpn", weight_end, heads_x, b_rows, precision=highest)


def out_local(conv_out, state_vals, skip_vals, consts):
    decay_mat, steps_in, decay_in = consts
    heads_x, b_rows, c_rows = split_conv(conv_out)
    intersection = jnp.dot(c_rows, b_rows.T, precision=highest)
    mixing = decay_mat * intersection[None] * steps_in[:, None, :]
    within = jnp.einsum("hts,shp->thp", mixing, heads_x, precision=highest)
    carried = decay_in.T[:, :, None] * jnp.einsum(
        "hpn,tn->thp", state_vals, c_rows, precision=highest
    )
    result = within + carried + skip_vals[None, :, None] * heads_x
    return result.reshape(result.shape[0], INNER)


def local_mamba(conv_out, skip_vals, log_decay, is_start, document_index, doc_before):
    total_length = conv_out.shape[0]
    block_length = math.gcd(total_length, 256)
    block_count = total_length // block_length
    prev_ids = jnp.concatenate([jnp.reshape(doc_before, (1,)), document_index[:-1]])
    befores = prev_ids.reshape(block_count, block_length)[:, 0]
    scan_result = (
        conv_out.reshape(block_count, block_length, XBC),
        jnp.transpose(log_decay.reshape(MH, block_count, block_length), (1, 0, 2)),
        is_start.reshape(block_count, block_length),
        document_index.reshape(block_count, block_length),
        befores,
    )

    def advance(carried_state, blocks):
        xblock, lblock, sblock, dblock, before_doc = blocks
        consts = scan_consts(lblock, sblock, dblock, before_doc)
        result = out_local(xblock, carried_state, skip_vals, consts)
        carried_state = consts[2][:, -1][:, None, None] * carried_state + state_local(
            xblock, consts
        )
        return (carried_state, result)

    zero_state = jnp.zeros((MH, MP, NS), conv_out.dtype)
    final_state, mixed = lax.scan(advance, zero_state, scan_result)
    return (mixed.reshape(total_length, INNER), final_state)


def carry_term(conv_out, state_vals, decay_shard):
    heads_x, b_rows, c_rows = split_conv(conv_out)
    carried = decay_shard.T[:, :, None] * jnp.einsum(
        "hpn,tn->thp", state_vals, c_rows, precision=highest
    )
    return carried.reshape(carried.shape[0], INNER)


def gate_norm(mixed, gate_vals, gain_vals):
    gated = mixed * jax.nn.silu(gate_vals)
    factor = lax.rsqrt(jnp.mean(gated * gated, axis=1, keepdims=True) + norm_eps)
    return gated * factor * gain_vals


def norm_backward(grad_normed, values, factor, gain_vals):
    weighted = grad_normed * gain_vals
    grad_values = factor * (
        weighted - values * factor * factor * jnp.mean(weighted * values, axis=1, keepdims=True)
    )
    grad_gain = jnp.sum(grad_normed * values * factor, axis=0)
    return (grad_values, grad_gain)


def adamw_step(param_vals, grad_vals, first_vals, second_vals, weight_decay):
    first_new = beta_one * first_vals + (1.0 - beta_one) * grad_vals
    second_new = beta_two * second_vals + (1.0 - beta_two) * grad_vals * grad_vals
    update = (
        first_new
        / (1.0 - beta_one**STEP)
        / (jnp.sqrt(second_new / (1.0 - beta_two**STEP)) + adam_eps)
    )
    return (param_vals - learn_rate * (update + weight_decay * param_vals), first_new, second_new)


def adam_direction(grad_vals, first_vals, second_vals):
    first_new = beta_one * first_vals + (1.0 - beta_one) * grad_vals
    second_new = beta_two * second_vals + (1.0 - beta_two) * grad_vals * grad_vals
    update = (
        first_new
        / (1.0 - beta_one**STEP)
        / (jnp.sqrt(second_new / (1.0 - beta_two**STEP)) + adam_eps)
    )
    return (update, first_new, second_new)


def combine_states(earlier, later):
    return (earlier[0] * later[0], later[0][:, None, None] * earlier[1] + later[1])


def row_product(left_side, right_side):
    return lax.dot_general(
        left_side, right_side, (((0,), (0,)), ((), ())), preferred_element_type=jnp.float32
    )


def shards(
    hidden,
    out_grad,
    decay_log,
    doc_lengths,
    weights,
    first_moment,
    second_moment,
    small_params,
    small_first,
    small_second,
):
    local_rows = hidden.shape[1]
    ctx_index = lax.axis_index("ctx")
    first_pos = ctx_index * local_rows
    query_groups = QUERY_HEADS // KEY_VALUE_HEADS
    scale_qk = HEAD_WIDTH ** (-0.5)
    contract_last = (((1,), (1,)), ((), ()))
    gain_one, gain_two, gate_gain, conv_w, conv_bias, skip_gain = split_small(small_params)
    lengths = doc_lengths[0]
    token_positions = first_pos + jnp.arange(local_rows, dtype=jnp.int32)
    document_index, rel_pos = doc_layout(lengths, token_positions)
    doc_before = doc_layout(lengths, jnp.reshape(first_pos - 1, (1,)))[0][0]
    prev_ids = jnp.concatenate([jnp.reshape(doc_before, (1,)), document_index[:-1]])
    is_start = document_index != prev_ids
    cosine_table, sine_table = rope_tables(rel_pos)
    tokens = hidden[0]
    tok_f = tokens.astype(jnp.float32)
    scale_one = lax.rsqrt(jnp.mean(tok_f * tok_f, axis=1, keepdims=True) + norm_eps)
    normed_one = (tok_f * scale_one * gain_one).astype(jnp.bfloat16)
    own_b = weights.astype(jnp.bfloat16)
    mixer_w = lax.all_gather(own_b[:, : MIXIN + MIXOUT], ("ctx", "fsdp"), axis=0, tiled=True)
    projected_output = jnp.dot(normed_one, mixer_w[:, :MIXIN], preferred_element_type=jnp.float32)
    query_rows = apply_rotary(
        projected_output[:, :QUERY_WIDTH].reshape(local_rows, QUERY_HEADS, HEAD_WIDTH),
        cosine_table,
        sine_table,
    ).astype(jnp.bfloat16)
    key_row_values = (
        apply_rotary(
            projected_output[:, QUERY_WIDTH : QUERY_WIDTH + KEY_WIDTH].reshape(
                local_rows, KEY_VALUE_HEADS, HEAD_WIDTH
            ),
            cosine_table,
            sine_table,
        )
        .astype(jnp.bfloat16)
        .reshape(local_rows, KEY_WIDTH)
    )
    value_row_values = projected_output[
        :, QUERY_WIDTH + KEY_WIDTH : QUERY_WIDTH + 2 * KEY_WIDTH
    ].astype(jnp.bfloat16)
    gate_in = projected_output[:, QUERY_WIDTH + 2 * KEY_WIDTH : QUERY_WIDTH + 2 * KEY_WIDTH + INNER]
    xbc_b = projected_output[:, QUERY_WIDTH + 2 * KEY_WIDTH + INNER : MIXIN].astype(jnp.bfloat16)
    grouped_query = query_rows.reshape(local_rows, KEY_VALUE_HEADS, query_groups, HEAD_WIDTH)

    def block_scores(key_tile, key_start, block_length):
        key_pos = key_start + jnp.arange(block_length, dtype=jnp.int32)
        key_doc = doc_layout(lengths, key_pos)[0]
        allowed = (key_pos[None, :] <= token_positions[:, None]) & (
            key_doc[None, :] == document_index[:, None]
        )
        scores = (
            jnp.einsum(
                "tgqd,sgd->tgqs",
                grouped_query,
                key_tile.reshape(block_length, KEY_VALUE_HEADS, HEAD_WIDTH),
                preferred_element_type=jnp.float32,
            )
            * scale_qk
        )
        return (scores, allowed[:, None, None, :])

    initial_accumulator = jnp.zeros(
        (local_rows, KEY_VALUE_HEADS, query_groups, HEAD_WIDTH), jnp.float32
    )
    initial_maximum = jnp.full(
        (local_rows, KEY_VALUE_HEADS, query_groups), large_negative, jnp.float32
    )
    initial_sum = jnp.zeros((local_rows, KEY_VALUE_HEADS, query_groups), jnp.float32)
    key_piece = lax.all_gather(key_row_values, "ctx", axis=0, tiled=True)
    value_piece = lax.all_gather(value_row_values, "ctx", axis=0, tiled=True)
    piece_rows = key_piece.shape[0]
    block_length = math.gcd(piece_rows, 512)
    block_count = piece_rows // block_length
    starts = block_length * jnp.arange(block_count, dtype=jnp.int32)

    def absorb(running, blocks):
        accumulated, row_top, norm_sum = running
        key_tile, value_tile, key_start = blocks
        scores, allowed = block_scores(key_tile, key_start, block_length)
        new_top = jnp.maximum(row_top, jnp.max(jnp.where(allowed, scores, large_negative), axis=-1))
        weights_blk = jnp.where(allowed, jnp.exp(scores - new_top[..., None]), 0.0)
        rescale = jnp.exp(row_top - new_top)
        accumulated = accumulated * rescale[..., None] + jnp.einsum(
            "tgqs,sgd->tgqd",
            weights_blk.astype(jnp.bfloat16),
            value_tile.reshape(block_length, KEY_VALUE_HEADS, HEAD_WIDTH),
            preferred_element_type=jnp.float32,
        )
        norm_sum = norm_sum * rescale + jnp.sum(weights_blk, axis=-1)
        return ((accumulated, new_top, norm_sum), None)

    running, unused = lax.scan(
        absorb,
        (initial_accumulator, initial_maximum, initial_sum),
        (
            key_piece.reshape(block_count, block_length, KEY_WIDTH),
            value_piece.reshape(block_count, block_length, KEY_WIDTH),
            starts,
        ),
    )
    accumulated, row_top, norm_sum = running
    attention_result = (accumulated / norm_sum[..., None]).astype(jnp.bfloat16)
    log_sum_exp = row_top + jnp.log(norm_sum)
    edge_in = shifted(xbc_b[local_rows - CONV + 1 :], "ctx", 1)
    xbc_ext = jnp.concatenate([edge_in, xbc_b], axis=0).astype(jnp.float32)
    edge_pos = first_pos - CONV + 1 + jnp.arange(CONV - 1, dtype=jnp.int32)
    doc_ext = jnp.concatenate([doc_layout(lengths, edge_pos)[0], document_index])
    log_decay = decay_log[0]
    decay_shard = jnp.where(
        (document_index == doc_before)[None, :], jnp.exp(jnp.cumsum(log_decay, axis=1)), 0.0
    )

    def conv_fn(xbc_vals, conv_weights, conv_biases):
        return conv_block(xbc_vals, doc_ext, document_index, conv_weights, conv_biases)

    def local_fn(conv_vals, skip_vals):
        return local_mamba(conv_vals, skip_vals, log_decay, is_start, document_index, doc_before)

    def carry_fn(conv_vals, state_vals):
        return carry_term(conv_vals, state_vals, decay_shard)

    conv_out, conv_vjp = jax.vjp(conv_fn, xbc_ext, conv_w, conv_bias)
    (mixed_zero, state_out), local_vjp = jax.vjp(local_fn, conv_out, skip_gain)
    shard_decay = decay_shard[:, -1]
    chain_ident = (jnp.ones_like(shard_decay), jnp.zeros_like(state_out))
    state_in = prefix((shard_decay, state_out), "ctx", combine_states, chain_ident)[1]
    carried, carry_vjp = jax.vjp(carry_fn, conv_out, state_in)
    mamba_f, gate_vjp = jax.vjp(gate_norm, mixed_zero + carried, gate_in, gate_gain)
    mamba_b = mamba_f.astype(jnp.bfloat16)
    branch = jnp.concatenate([attention_result.reshape(local_rows, QUERY_WIDTH), mamba_b], axis=1)
    resid_one = tok_f + lax.dot_general(
        branch, mixer_w[:, MIXIN:], contract_last, preferred_element_type=jnp.float32
    )
    scale_two = lax.rsqrt(jnp.mean(resid_one * resid_one, axis=1, keepdims=True) + norm_eps)
    normed_two = (resid_one * scale_two * gain_two).astype(jnp.bfloat16)
    mlp_w = lax.all_gather(own_b[:, MIXIN + MIXOUT :], ("ctx", "fsdp"), axis=0, tiled=True)
    gate_up = jnp.dot(normed_two, mlp_w[:, : 2 * FF], preferred_element_type=jnp.float32)
    gate_part = gate_up[:, :FF]
    up_part = gate_up[:, FF:]
    sigma_gate = jax.nn.sigmoid(gate_part)
    silu_gate = gate_part * sigma_gate
    hidden_mid = (silu_gate * up_part).astype(jnp.bfloat16)
    block_out = resid_one + lax.dot_general(
        hidden_mid, mlp_w[:, 2 * FF :], contract_last, preferred_element_type=jnp.float32
    )
    out_hidden = block_out.astype(jnp.bfloat16)[None]
    grad_out = out_grad[0]
    grad_mid = jnp.dot(grad_out, mlp_w[:, 2 * FF :], preferred_element_type=jnp.float32)
    silu_slope = sigma_gate * (1.0 + gate_part * (1.0 - sigma_gate))
    grad_gate_up = jnp.concatenate(
        [grad_mid * up_part * silu_slope, grad_mid * silu_gate], axis=1
    ).astype(jnp.bfloat16)
    grad_normed_two = lax.dot_general(
        grad_gate_up, mlp_w[:, : 2 * FF], contract_last, preferred_element_type=jnp.float32
    )
    grad_norm_two, grad_gain_two = norm_backward(grad_normed_two, resid_one, scale_two, gain_two)
    grad_resid_one = grad_out.astype(jnp.float32) + grad_norm_two
    grad_resid_b = grad_resid_one.astype(jnp.bfloat16)
    grad_branch = jnp.dot(grad_resid_b, mixer_w[:, MIXIN:], preferred_element_type=jnp.float32)
    attention_gradient = grad_branch[:, :QUERY_WIDTH].astype(jnp.bfloat16)
    grad_mamba = grad_branch[:, QUERY_WIDTH:]
    grad_mixed, grad_gate_in, grad_gate_gain = gate_vjp(grad_mamba)
    grad_conv_c, grad_state_in = carry_vjp(grad_mixed)
    grad_state_out = entering((shard_decay, grad_state_in), "ctx", combine_states, chain_ident)[1]
    grad_conv_l, grad_skip = local_vjp((grad_mixed, grad_state_out))
    grad_ext, grad_conv_w, grad_conv_bias = conv_vjp(grad_conv_c + grad_conv_l)
    edge_back = shifted(grad_ext[: CONV - 1], "ctx", -1)
    grad_xbc = grad_ext[CONV - 1 :] + jnp.concatenate(
        [jnp.zeros((local_rows - CONV + 1, XBC), jnp.float32), edge_back], axis=0
    )
    grouped_attention_gradient = attention_gradient.reshape(
        local_rows, KEY_VALUE_HEADS, query_groups, HEAD_WIDTH
    )
    row_correction = jnp.sum(
        grouped_attention_gradient.astype(jnp.float32) * attention_result.astype(jnp.float32),
        axis=-1,
    )
    keys_all, values_all = (
        lax.all_gather(key_row_values, "ctx", axis=0, tiled=True),
        lax.all_gather(value_row_values, "ctx", axis=0, tiled=True),
    )
    total_keys = keys_all.shape[0]
    key_block_rows = math.gcd(total_keys, 512)
    nkey_blocks = total_keys // key_block_rows

    def attend_back(grad_query, blocks):
        key_tile, value_tile, key_start = blocks
        scores, allowed = block_scores(key_tile, key_start, key_block_rows)
        probs_f = jnp.where(allowed, jnp.exp(scores - log_sum_exp[..., None]), 0.0)
        value_head_rows = value_tile.reshape(key_block_rows, KEY_VALUE_HEADS, HEAD_WIDTH)
        grad_prob = jnp.einsum(
            "tgqd,sgd->tgqs",
            grouped_attention_gradient,
            value_head_rows,
            preferred_element_type=jnp.float32,
        )
        dscores = (probs_f * (grad_prob - row_correction[..., None])).astype(jnp.bfloat16)
        probs_b = probs_f.astype(jnp.bfloat16)
        grad_query = (
            grad_query
            + jnp.einsum(
                "tgqs,sgd->tgqd",
                dscores,
                key_tile.reshape(key_block_rows, KEY_VALUE_HEADS, HEAD_WIDTH),
                preferred_element_type=jnp.float32,
            )
            * scale_qk
        )
        grad_key = (
            jnp.einsum("tgqs,tgqd->sgd", dscores, grouped_query, preferred_element_type=jnp.float32)
            * scale_qk
        )
        grad_value = jnp.einsum(
            "tgqs,tgqd->sgd",
            probs_b,
            grouped_attention_gradient,
            preferred_element_type=jnp.float32,
        )
        return (
            grad_query,
            jnp.concatenate(
                [
                    grad_key.reshape(key_block_rows, KEY_WIDTH),
                    grad_value.reshape(key_block_rows, KEY_WIDTH),
                ],
                axis=1,
            ),
        )

    key_starts = key_block_rows * jnp.arange(nkey_blocks, dtype=jnp.int32)
    grad_query, stacked = lax.scan(
        attend_back,
        jnp.zeros_like(initial_accumulator),
        (
            keys_all.reshape(nkey_blocks, key_block_rows, KEY_WIDTH),
            values_all.reshape(nkey_blocks, key_block_rows, KEY_WIDTH),
            key_starts,
        ),
    )
    key_gradients = lax.psum_scatter(
        stacked.reshape(total_keys, 2 * KEY_WIDTH), "ctx", scatter_dimension=0, tiled=True
    )
    grad_q = inverse_rotary(
        grad_query.reshape(local_rows, QUERY_HEADS, HEAD_WIDTH), cosine_table, sine_table
    ).reshape(local_rows, QUERY_WIDTH)
    key_gradient = inverse_rotary(
        key_gradients[:, :KEY_WIDTH].reshape(local_rows, KEY_VALUE_HEADS, HEAD_WIDTH),
        cosine_table,
        sine_table,
    ).reshape(local_rows, KEY_WIDTH)
    grad_proj = jnp.concatenate(
        [grad_q, key_gradient, key_gradients[:, KEY_WIDTH:], grad_gate_in, grad_xbc], axis=1
    ).astype(jnp.bfloat16)
    grad_normed_one = lax.dot_general(
        grad_proj, mixer_w[:, :MIXIN], contract_last, preferred_element_type=jnp.float32
    )
    grad_norm_one, grad_gain_one = norm_backward(grad_normed_one, tok_f, scale_one, gain_one)
    grad_hidden = (grad_resid_one + grad_norm_one)[None]
    grad_weights = lax.psum_scatter(
        jnp.concatenate(
            [
                row_product(normed_one, grad_proj),
                row_product(grad_resid_b, branch),
                row_product(normed_two, grad_gate_up),
                row_product(grad_out, hidden_mid),
            ],
            axis=1,
        ),
        ("ctx", "fsdp"),
        scatter_dimension=0,
        tiled=True,
    )
    small_local = jnp.concatenate(
        [
            grad_gain_one,
            grad_gain_two,
            grad_gate_gain,
            grad_conv_w.reshape(-1),
            grad_conv_bias,
            grad_skip,
        ]
    )
    small_grads = lax.psum(small_local, ("ctx", "fsdp"))
    new_weights, new_first, new_second = adamw_step(
        weights, grad_weights, first_moment, second_moment, decay_rate
    )
    small_step, small_first_new, small_second_new = adam_direction(
        small_grads, small_first, small_second
    )
    return (
        out_hidden,
        grad_hidden,
        grad_weights,
        new_weights,
        new_first,
        new_second,
        small_grads,
        small_step,
        small_first_new,
        small_second_new,
    )


def solution(mesh):
    placed = (
        P("fsdp", "ctx", None),
        P("fsdp", "ctx", None),
        P("fsdp", None, "ctx"),
        P("fsdp", None),
        P(("ctx", "fsdp"), None),
        P(("ctx", "fsdp"), None),
        P(("ctx", "fsdp"), None),
        P(),
        P(),
        P(),
    )
    return jax.shard_map(
        shards,
        mesh=mesh,
        in_specs=placed,
        out_specs=(
            P("fsdp", "ctx", None),
            P("fsdp", "ctx", None),
            P(("ctx", "fsdp"), None),
            P(("ctx", "fsdp"), None),
            P(("ctx", "fsdp"), None),
            P(("ctx", "fsdp"), None),
            P(),
            P(),
            P(),
            P(),
        ),
        check_vma=False,
    )
```

profile of v0, /device:TPU:0, one launch (start us, length us, event | category | flops | bytes accessed | tf_op | source)
XLA Modules:
  0.0 1156.8 jit_solution(17916562093942026029)
XLA Ops:
  11.2 99.0 %all-gather.10.cloned.1.call-done = bf16[1024,6144]{1,0:T(8,128)(2,1)} async-done(((bf16[32,6144]{1,0:T(8,128)(2,1)}), bf16[1024,6144]{1,0:T(8,128)(2,1)}) %all-gather.10.cloned.1.call-update) | async-done | bytes 12582928 | tf_op jit(solution)/shard_map/all_gather | solution.py:310
  110.2 5.8 fusion.196
  143.9 32.1 %all-reduce.15 = bf16[384]{0:T(512)(128)(2,1)S(1)} all-reduce(bf16[384]{0:T(512)(128)(2,1)S(1)} %dynamic-update-slice), channel_id=2, replica_groups=mesh['ctx'=16,'fsdp'=2] {'ctx'}, use_global_device_ids=true, to_apply=%add.15 | all-reduce | flops 384 | bytes 1536
  186.3 7.6 all-gather.14.cloned.1.call-done
  196.1 94.0 %while.40 = (s32[]{:T(128)}, f32[256,2,4,64]{0,3,2,1:T(8,128)}, f32[256,2,4]{0,2,1:T(4,128)S(1)}, f32[256,2,4]{0,2,1:T(4,128)S(1)}, s32[8]{0:T(128)S(1)}, /*inde...) while((s32[]{:T(128)}, f32[256,2,4,64]{0,3,2,1:T(8,128)}, ...), condition=%wide.region_8.9_spmd.clone, body=%wide.region_4.0_spmd.clone.sunk | while | flops 280770304 | bytes 32130248 | solution.py:382
  294.3 10.0 fusion.77
  313.9 40.9 %all-gather.16.cloned.1.call-done = bf16[1024,6144]{1,0:T(8,128)(2,1)} async-done(((bf16[32,6144]{1,0:T(8,128)(2,1)}), bf16[1024,6144]{1,0:T(8,128)(2,1)}) %all-gather.16.cloned.1.call-update) | async-done | bytes 12582928 | tf_op jit(solution)/shard_map/all_gather | solution.py:426
  354.7 5.9 fusion.39
  376.2 119.3 %while.41 = (s32[]{:T(128)}, f32[256,2,4,64]{0,3,2,1:T(8,128)}, f32[8,512,256]{2,1,0:T(8,128)}, bf16[8,512,128]{1,2,0:T(8,128)(2,1)}, s32[8]{0:T(128)}, /*index=...) while((s32[]{:T(128)}, f32[256,2,4,64]{0,3,2,1:T(8,128)}, ...), condition=%wide.region_21.22_spmd.clone, body=%wide.region_19.21_spmd.clone.sunk | while | flops 682561280 | bytes 42870068 | solution.py:521
  499.5 4.6 multiply_reduce_fusion.5
  513.8 8.9 bitcast_add_fusion
  534.4 7.7 multiply_reduce_fusion
  546.3 4.6 fusion.139
  551.0 4.6 convolution_bitcast_fusion.1
  555.6 8.2 fusion.89
  573.9 56.5 %all-gather.20.cloned.1.call-done = bf16[384,64,128]{2,1,0:T(8,128)(2,1)} async-done(((bf16[24,64,128]{2,1,0:T(8,128)(2,1)}), bf16[384,64,128]{2,1,0:T(8,128)(2,1)}) %all-gather.20.cloned.1.call-update) | async-done | bytes 6291472 | tf_op jit(solution)/shard_map/all_gather | solution.py:66
  630.4 30.2 %while.42 = (s32[]{:T(128)}, f32[24,64,128]{2,1,0:T(8,128)S(1)}, s32[]{:T(128)}, bf16[16,24]{1,0:T(8,128)(2,1)}, bf16[16,24,64,128]{3,2,1,0:T(8,128)(2,1)}, /*index=5*/s32[]{:T(128)}, s32[]{:T(128)}, s32[]{:T(128)}, s32[]{:T(128)}) while((s32[]{:T(128)}, f32[24,64,128]{2,1,0:T(8,128)S(1)}, s32[]{:T(128)}, ...), condition=%wide.region_25.26_spmd.clone, body=%wide.region_24.25_spmd.clone.sunk | while | flops 983072 | bytes 1966495 | solution.py:84
  679.4 4.5 fusion.149
  683.9 27.1 %pad_maximum_fusion = f32[1024,12288]{1,0:T(8,128)} fusion(f32[1024,2048]{1,0:T(8,128)S(1)} %bitcast.300, f32[1024,4096]{1,0:T(8,128)} %fusion.89, f32[1024,2048]{1,0:T(8,128)} %fusion.139, f32[1024,4096]{1,0:T(8,128)S(1)} %fusion.149), kind=kLoop, calls=%fused_computation.59 | loop fusion | flops 37748736 | bytes 100663296 | tf_op jit(solution)/shard_map/concatenate | solution.py:550
  712.6 4.3 fusion.109
  717.0 9.6 fusion.130
  726.6 41.6 %psum.7 = f32[12568]{0:T(1024)S(1)} all-reduce(f32[12568]{0:T(1024)S(1)} %constant_dynamic-update-slice_fusion.4), channel_id=1, replica_groups=mesh['ctx'=16,'fsdp'=2] {'ctx','fsdp'}, use_global_device_ids=true, to_apply=%region_39.40 | all-reduce | flops 12568 | bytes 100544 | tf_op jit(solution)/shard_map/psum | solution.py:573
  771.8 372.4 %reduce-scatter.5.cloned.1.call-done = f32[32,12288]{1,0:T(8,128)} async-done(((f32[1024,12288]{1,0:T(8,128)}), f32[32,12288]{1,0:T(8,128)}) %reduce-scatter.5.cloned.1.call-update) | async-done | bytes 1572880 | tf_op jit(solution)/shard_map/reduce_scatter | solution.py:549
  1144.3 5.3 multiply_subtract_fusion
  (673 shorter events, 376.5 us)
Async XLA Ops:
  7.2 103.0 %all-gather.10.cloned.1.call-start = ((), (), s32[]{:S(2)}) async-start(), calls=%async_computation.2 | async-start | bytes 12976128 | tf_op jit(solution)/shard_map/all_gather | solution.py:310
  9.7 172.0 %all-gather.12.cloned.1.call-start = ((), (), s32[]{:S(2)}) async-start(), calls=%async_computation.3 | async-start | bytes 1114112 | tf_op jit(solution)/shard_map/all_gather | solution.py:359
  10.6 111.9 %copy-start.51 = (s32[1,2]{1,0:T(1,128)}, s32[1,2]{1,0:T(1,128)S(1)}, u32[]{:S(2)}) copy-start(s32[1,2]{1,0:T(1,128)S(1)} %get-tuple-element.1291) | copy-start | bytes 28
  10.9 105.1 %copy-start.70 = (f32[256]{0:T(256)}, f32[256]{0:T(256)S(1)}, u32[]{:S(2)}) copy-start(f32[256]{0:T(256)S(1)} %add_rsqrt_fusion.1) | copy-start | bytes 3076
  11.0 105.1 %copy-start.42 = (f32[1024]{0:T(1024)}, f32[1024]{0:T(1024)S(1)}, u32[]{:S(2)}) copy-start(f32[1024]{0:T(1024)S(1)} %get-tuple-element.977) | copy-start | bytes 12292
  110.2 9.9 copy-start.50
  118.8 75.0 %all-gather.14.cloned.1.call-start = ((), (), s32[]{:S(2)}) async-start(), calls=%async_computation.4 | async-start | bytes 1114112 | tf_op jit(solution)/shard_map/all_gather | solution.py:360
  123.4 169.3 %all-gather.18.cloned.1.call-start = ((), (), s32[]{:S(2)}) async-start(), calls=%async_computation.8 | async-start | bytes 6684672 | tf_op jit(solution)/shard_map/all_gather | solution.py:46
  124.9 3.0 collective-permute-start
  130.9 161.9 %copy-start.7 = (f32[256,1792]{1,0:T(8,128)}, f32[256,1792]{1,0:T(8,128)S(1)}, u32[]{:S(2)}) copy-start(f32[256,1792]{1,0:T(8,128)S(1)} %get-tuple-element.949) | copy-start | bytes 5505028
  139.0 215.7 %all-gather.16.cloned.1.call-start = ((), (), s32[]{:S(2)}) async-start(), calls=%async_computation.5 | async-start | bytes 12976128 | tf_op jit(solution)/shard_map/all_gather | solution.py:426
  139.6 426.7 %reduce-scatter.3.cloned.1.call-start = ((), (), s32[]{:S(2)}) async-start(), calls=%async_computation.6 | async-start | bytes 4456448 | tf_op jit(solution)/shard_map/reduce_scatter | solution.py:530
  184.0 12.1 %copy-start.52 = (s32[1,2]{1,0:T(1,128)S(1)}, s32[1,2]{1,0:T(1,128)}, u32[]{:S(2)}) copy-start(s32[1,2]{1,0:T(1,128)} %copy-done.51) | copy-start | bytes 28
  184.0 12.1 %copy-start.88 = (s32[8]{0:T(128)S(1)}, s32[8]{0:T(128)}, u32[]{:S(2)}) copy-start(s32[8]{0:T(128)} %iota_multiply_fusion) | copy-start | bytes 100
  313.8 54.2 %copy-start.22 = (f32[256,1024]{1,0:T(8,128)}, f32[256,1024]{1,0:T(8,128)S(1)}, u32[]{:S(2)}) copy-start(f32[256,1024]{1,0:T(8,128)S(1)} %get-tuple-element.995) | copy-start | bytes 3145732
  313.9 54.2 %copy-start.64 = (f32[256]{0:T(256)}, f32[256]{0:T(256)S(1)}, u32[]{:S(2)}) copy-start(f32[256]{0:T(256)S(1)} %add_rsqrt_fusion) | copy-start | bytes 3076
  495.6 134.8 %all-gather.20.cloned.1.call-start = ((), (), s32[]{:S(2)}) async-start(), calls=%async_computation.9 | async-start | bytes 6684672 | tf_op jit(solution)/shard_map/all_gather | solution.py:66
  510.8 633.5 %reduce-scatter.5.cloned.1.call-start = ((), (), s32[]{:S(2)}) async-start(), calls=%async_computation.7 | async-start | bytes 51904512 | tf_op jit(solution)/shard_map/reduce_scatter | solution.py:549
  534.4 11.9 %copy-start.26 = (bf16[256,1536]{1,0:T(8,128)(2,1)S(1)}, bf16[256,1536]{1,0:T(8,128)(2,1)}, u32[]{:S(2)}) copy-start(bf16[256,1536]{1,0:T(8,128)(2,1)} %copy-done.25) | copy-start | bytes 2359300
  534.4 11.9 %copy-start.37 = (bf16[256,512]{1,0:T(8,128)(2,1)S(1)}, bf16[256,512]{1,0:T(8,128)(2,1)}, u32[]{:S(2)}) copy-start(bf16[256,512]{1,0:T(8,128)(2,1)} %copy.142) | copy-start | bytes 786436
  675.1 3.1 collective-permute-start.1
  716.9 9.6 copy-start.85
  716.9 51.2 %copy-start.16 = (f32[256,1024]{1,0:T(8,128)S(1)}, f32[256,1024]{1,0:T(8,128)}, u32[]{:S(2)}) copy-start(f32[256,1024]{1,0:T(8,128)} %copy-done.14) | copy-start | bytes 3145732
  768.2 376.1 %copy-start.19 = (f32[32,12288]{1,0:T(8,128)S(1)}, f32[32,12288]{1,0:T(8,128)}, u32[]{:S(2)}) copy-start(f32[32,12288]{1,0:T(8,128)} %param.22) | copy-start | bytes 4718596
  (115 other events, 446.3 us)
Sparse Core Ops, SparseCore 0:
  11.5 98.6 all-gather.9
  119.0 35.1 all-gather.11
  156.3 37.4 all-gather.13
  196.6 60.6 all-gather.17
  260.0 94.6 all-gather.15
  495.7 70.5 reduce-scatter.2
  569.4 60.9 all-gather.19
  711.2 433.0 reduce-scatter.4
where the time goes:
time: 1170 us; the launch traced here: 1160 us
  waiting for transfers between devices  581 us (50%)
  matrix products  237 us (20%)
  other arithmetic  150 us (13%)
  local copies, waits for them, and re-layouts  92.3 us (8%)
  blocking collectives  73.7 us (6%)
  between operations  17.2 us (1%)
    reduce_scatter x1, waiting for transfers between devices, shards(): lax.psum_scatter(jnp.concatenate([row_product(normed_one, grad_proj), row...  372 us
    all_gather x1, waiting for transfers between devices, shards(): lax.all_gather(own_b[:, :MIXIN + MIXOUT], ('ctx', 'fsdp'), axis=0, tiled=...  99 us
    all_gather x1, waiting for transfers between devices, entering(): lax.all_gather(part.astype(kind), axis)  56.5 us
    psum x1, blocking collectives, shards(): small_grads = lax.psum(small_local, ('ctx', 'fsdp'))  41.6 us
    all_gather x1, waiting for transfers between devices, shards(): lax.all_gather(own_b[:, MIXIN + MIXOUT:], ('ctx', 'fsdp'), axis=0, tiled=...  40.9 us
    dynamic_slice x32, local copies, waits for them, and re-layouts, shards(): lax.scan(absorb, (initial_accumulator, initial_maximum, initial_sum), (ke...  35.4 us
    unnamed x1, blocking collectives  32.1 us
    dot_general x16, matrix products, block_scores(): jnp.einsum('tgqd,sgd->tgqs', grouped_query, key_tile.reshape(block_length...  29 us
  transfers between devices with their start and end apart: 10, of which 8 were waited for; matrix products, arithmetic and copies ran while one was open for 21% of the time, Pallas kernels for 0%

commit v1 on v0

v1 whole, which is shorter than its diff:
```python
import functools
import math

import jax
import jax.numpy as jnp
from jax import lax
from jax.experimental import pallas as pl
from jax.experimental.pallas import tpu as pltpu
from jax.sharding import PartitionSpec as P

D = 1024
QUERY_HEADS = 8
KEY_VALUE_HEADS = 2
HEAD_WIDTH = 64
MH = 24
MP = 64
NS = 128
FF = 2048
CONV = 4
STEP = 3
QUERY_WIDTH = 512
KEY_WIDTH = 128
INNER = 1536
XBC = 1792
MIXIN = 4096
MIXOUT = 2048
SMALL_ROWS = 104

norm_eps = 1e-05
rope_base = 100000000000.0
large_negative = -1e30
learn_rate = 0.02
beta_one = 0.9
beta_two = 0.95
adam_eps = 1e-08
decay_rate = 0.1

MESH = pl.DeviceIdType.MESH
BF = jnp.bfloat16
F32 = jnp.float32
VM = pl.BlockSpec(memory_space=pltpu.VMEM)
SM = pl.BlockSpec(memory_space=pltpu.SMEM)
HB = pl.BlockSpec(memory_space=pl.ANY)
DMA = pltpu.SemaphoreType.DMA


def params(collective=None):
    if collective is None:
        return pltpu.CompilerParams(vmem_limit_bytes=56 * 2**20)
    return pltpu.CompilerParams(
        collective_id=collective, has_side_effects=True, vmem_limit_bytes=56 * 2**20
    )


def nt(a, b):
    return lax.dot_general(a, b, (((1,), (1,)), ((), ())), preferred_element_type=F32)


def tn(a, b):
    return lax.dot_general(a, b, (((0,), (0,)), ((), ())), preferred_element_type=F32)


def nn(a, b):
    return lax.dot_general(a, b, (((1,), (0,)), ((), ())), preferred_element_type=F32)


class Place:
    def __init__(self, planes):
        ctx = lax.axis_index("ctx")
        self.ctx = ctx
        self.Z, self.z, self.x, self.c = planes, ctx // 4, (ctx // 2) % 2, ctx % 2
        self.y = lax.axis_index("fsdp")
        self.up, self.down = self.z + 1 < planes, self.z > 0

    def shard(self, z, x, y, c):
        return ((z * 2 + x) * 2 + c) * 2 + y

    def spot(self, z, x, c):
        return (z * 2 + x) * 2 + c

    def dev(self, z, x, y, c):
        return ((z * 2 + x) * 2 + c, y)

    def near(self, d):
        z, x, y, c = self.z, self.x, self.y, self.c
        return {
            "x": self.dev(z, 1 - x, y, c),
            "y": self.dev(z, x, 1 - y, c),
            "c": self.dev(z, x, y, 1 - c),
            "u": self.dev(z + 1, x, y, c),
            "d": self.dev(z - 1, x, y, c),
        }[d]

    def zord(self, k):
        if k == self.Z - 1:
            return self.z
        low = self.Z - 1 - k
        z = self.z
        return jnp.where(
            2 * z < self.Z, jnp.where(low > z, low, low - 1), jnp.where(k < z, k, k + 1)
        )


def greet(pc, dims="xyc", chain=True):
    bar = pltpu.get_barrier_semaphore()

    def sig(d):
        pl.semaphore_signal(bar, inc=1, device_id=pc.near(d), device_id_type=MESH)

    for d in dims:
        sig(d)
    if chain:
        pl.when(pc.up)(lambda: sig("u"))
        pl.when(pc.down)(lambda: sig("d"))
    peers = len(dims)
    if chain:
        peers = peers + pc.up.astype(jnp.int32) + pc.down.astype(jnp.int32)
    pl.semaphore_wait(bar, peers)


def greet_row(pc):
    bar = pltpu.get_barrier_semaphore()
    n = 4 * pc.Z

    @pl.loop(1, n)
    def _(d):
        pl.semaphore_signal(
            bar, inc=1, device_id=(lax.rem(pc.ctx + d, n), pc.y), device_id_type=MESH
        )

    pl.semaphore_wait(bar, n - 1)


def rcopy(pc, src, dst, ssem, rsem, d):
    return pltpu.make_async_remote_copy(
        src_ref=src,
        dst_ref=dst,
        send_sem=ssem,
        recv_sem=rsem,
        device_id=pc.near(d) if isinstance(d, str) else d,
        device_id_type=MESH,
    )


def add_into(dst, parts, width=512):
    columns = dst.shape[-1]
    step = width if columns % width == 0 else (256 if columns % 256 == 0 else 128)

    @pl.loop(0, columns // step)
    def _(i):
        sl = pl.ds(pl.multiple_of(i * step, step), step)
        total = parts[0][:, sl].astype(F32)
        for r in parts[1:]:
            total = total + r[:, sl].astype(F32)
        dst[:, sl] = total.astype(dst.dtype)


def gather_scratch(planes):
    n = 8 * planes
    return [
        DMA((2, planes, 2)),
        DMA((2, planes)),
        DMA((2, planes, 2)),
        DMA((2, planes, 4)),
        DMA((2, n)),
        DMA,
    ]


def gather_steps(pc, w_ref, out_ref, scratch):
    zs, xs, ys, cs, rs, loc = scratch
    Z, z, x, y, c = pc.Z, pc.z, pc.x, pc.y, pc.c
    half = w_ref.shape[-1] // 2
    me = pc.shard(z, x, y, c)

    def cp(p, s, sem, d, own=False):
        sl = pl.ds(p * half, half)
        src = w_ref.at[:, sl] if own else out_ref.at[s, :, sl]
        return rcopy(pc, src, out_ref.at[s, :, sl], sem, rs.at[p, s], d)

    def along(p, zz, up, own=False):
        return cp(p, pc.shard(zz, x, y, c), zs.at[p, zz, int(up)], "u" if up else "d", own)

    def first(p, zz, own=False):
        return cp(p, pc.shard(zz, x, y, c), xs.at[p, zz], "x" if p == 0 else "y", own)

    def second(p, zz, q, own=False):
        if p == 0:
            return cp(p, pc.shard(zz, x if q == 0 else 1 - x, y, c), ys.at[p, zz, q], "y", own)
        return cp(p, pc.shard(zz, x, y if q == 0 else 1 - y, c), ys.at[p, zz, q], "x", own)

    def core(p, zz, q, r, own=False):
        s = pc.shard(zz, x if q == 0 else 1 - x, y if r == 0 else 1 - y, c)
        return cp(p, s, cs.at[p, zz, q * 2 + r], "c", own)

    def arrived(p, s):
        sl = pl.ds(p * half, half)
        rcopy(pc, w_ref.at[:, sl], out_ref.at[s, :, sl], loc, rs.at[p, s], "c").wait_recv()

    keep = pltpu.make_async_copy(w_ref, out_ref.at[me], loc)
    keep.start()
    for p in (0, 1):
        pl.when(pc.up)(lambda: along(p, z, True, True).start())
        pl.when(pc.down)(lambda: along(p, z, False, True).start())
        first(p, z, True).start()
    for p in (0, 1):
        second(p, z, 0, True).start()
        core(p, z, 0, 0, True).start()
    yield
    for d in range(1, Z):
        for p in (0, 1):

            def onward(zz, up, more):
                arrived(p, pc.shard(zz, x, y, c))
                pl.when(more)(lambda: along(p, zz, up).start())
                first(p, zz).start()
                second(p, zz, 0).start()
                core(p, zz, 0, 0).start()

            pl.when(z - d >= 0)(lambda: onward(z - d, True, pc.up))
            pl.when(z + d < Z)(lambda: onward(z + d, False, pc.down))
        yield
    near = [lax.rem(z + k, Z) for k in range(Z)]
    for zz in near:
        for p in (0, 1):
            xx, yy = (1 - x, y) if p == 0 else (x, 1 - y)
            arrived(p, pc.shard(zz, xx, yy, c))
            second(p, zz, 1).start()
            core(p, zz, *((1, 0) if p == 0 else (0, 1))).start()
        yield
    for q in (0, 1):
        for zz in near:
            for p in (0, 1):
                if p == 0:
                    xx, yy, a, b = (x if q == 0 else 1 - x), 1 - y, q, 1
                else:
                    xx, yy, a, b = 1 - x, (y if q == 0 else 1 - y), 1, q
                arrived(p, pc.shard(zz, xx, yy, c))
                core(p, zz, a, b).start()
            yield
    for q in range(4):
        for zz in near:
            for p in (0, 1):
                xx = x if q < 2 else 1 - x
                yy = y if q % 2 == 0 else 1 - y
                arrived(p, pc.shard(zz, xx, yy, 1 - c))
        yield
    keep.wait()
    for p in (0, 1):
        for zz in range(Z):
            pl.when(pc.up & (zz <= z))(lambda: along(p, zz, True).wait_send())
            pl.when(pc.down & (zz >= z))(lambda: along(p, zz, False).wait_send())
            first(p, zz).wait_send()
            for q in (0, 1):
                second(p, zz, q).wait_send()
            for q in range(4):
                core(p, zz, q // 2, q % 2).wait_send()


def gather_kernel(planes, w_ref, out_ref, *scratch):
    pc = Place(planes)
    greet(pc)
    for _ in gather_steps(pc, w_ref, out_ref, scratch):
        pass


def gather_rows(w, planes, collective):
    rows, columns = w.shape
    return pl.pallas_call(
        functools.partial(gather_kernel, planes),
        out_shape=jax.ShapeDtypeStruct((8 * planes, rows, columns), w.dtype),
        in_specs=[HB],
        out_specs=HB,
        scratch_shapes=gather_scratch(planes),
        compiler_params=params(collective),
    )(w)


def scatter_scratch(planes, rows, columns):
    h = columns // 2
    return [
        pltpu.VMEM((planes, 4, rows, columns), BF),
        pltpu.VMEM((2, planes, 2, rows, h), BF),
        pltpu.VMEM((2, planes, rows, h), BF),
        pltpu.VMEM((2, 2, planes, rows, h), BF),
        DMA((planes, 4)),
        DMA((planes, 4)),
        DMA((2, planes, 2)),
        DMA((2, planes, 2)),
        DMA((2, planes)),
        DMA((2, planes)),
        DMA((2, 2, planes)),
        DMA((2, 2, planes)),
    ]


def scatter_steps(pc, make_plane, g_ref, out_ref, scratch):
    rc, r2, r3, rz, cs, cr, s2, q2, s3, q3, sz, qz = scratch
    Z, z, x, y, c = pc.Z, pc.z, pc.x, pc.y, pc.c
    h = g_ref.shape[-1] // 2

    def cols(p):
        return pl.ds(p * h, h)

    def other(q):
        return (x if q < 2 else 1 - x), (y if q % 2 == 0 else 1 - y)

    def ccopy(zz, q):
        xx, yy = other(q)
        return rcopy(
            pc, g_ref.at[pc.shard(zz, xx, yy, 1 - c)], rc.at[zz, q], cs.at[zz, q], cr.at[zz, q], "c"
        )

    def copy2(p, zz, j):
        q = (1 + 2 * j) if p == 0 else (2 + j)
        return rcopy(
            pc,
            rc.at[zz, q, :, cols(p)],
            r2.at[p, zz, j],
            s2.at[p, zz, j],
            q2.at[p, zz, j],
            "y" if p == 0 else "x",
        )

    def copy3(p, zz):
        q = 2 if p == 0 else 1
        return rcopy(
            pc, rc.at[zz, q, :, cols(p)], r3.at[p, zz], s3.at[p, zz], q3.at[p, zz], "x" if p == 0 else "y"
        )

    def copyz(p, zz, up):
        u = int(up)
        return rcopy(
            pc,
            rc.at[zz, 0, :, cols(p)],
            rz.at[p, u, zz],
            sz.at[p, u, zz],
            qz.at[p, u, zz],
            "u" if up else "d",
        )

    order = (3, 1, 2, 0)
    for k in range(Z):
        zz = pc.zord(k)
        make_plane(zz)
        for q in order:
            ccopy(zz, q).start()
        yield
    for q in order:
        for k in range(Z):
            zz = pc.zord(k)
            xx, yy = other(q)
            ccopy(zz, q).wait_recv()
            add_into(rc.at[zz, q], [g_ref.at[pc.shard(zz, xx, yy, c)], rc.at[zz, q]])
            if q == 3:
                copy2(0, zz, 1).start()
                copy2(1, zz, 1).start()
            if q == 1:
                copy2(0, zz, 0).start()
            if q == 2:
                copy2(1, zz, 0).start()
            yield
    for k in range(Z):
        zz = pc.zord(k)
        for p in (0, 1):
            copy2(p, zz, 1).wait_recv()
            a = rc.at[zz, 2 if p == 0 else 1, :, cols(p)]
            add_into(a, [a, r2.at[p, zz, 1]])
            copy3(p, zz).start()
        yield

    def own(p, zz):
        copy2(p, zz, 0).wait_recv()
        copy3(p, zz).wait_recv()
        a = rc.at[zz, 0, :, cols(p)]
        return a, [a, r2.at[p, zz, 0], r3.at[p, zz]]

    def chain(p, zz, up, more):
        a, parts = own(p, zz)
        add_into(a, parts)

        @pl.when(more)
        def _():
            copyz(p, zz, up).wait_recv()
            add_into(a, [a, rz.at[p, int(up), zz]])

        copyz(p, zz, up).start()

    for t in range(Z - 1):
        for p in (0, 1):
            below, above = t - (Z - 1 - z), Z - 1 - (t - z)
            pl.when((below >= 0) & (below < z))(lambda: chain(p, below, False, pc.up))
            pl.when((above > z) & (above < Z))(lambda: chain(p, above, True, pc.down))
        yield
    for p in (0, 1):
        a, parts = own(p, z)
        o = out_ref.at[:, cols(p)]
        add_into(o, parts)

        def last(u):
            copyz(p, z, bool(u)).wait_recv()
            add_into(o, [o, rz.at[p, u, z]])

        pl.when(pc.up)(lambda: last(0))
        pl.when(pc.down)(lambda: last(1))
        yield
    for zz in range(Z):
        for q in range(4):
            ccopy(zz, q).wait_send()
        for p in (0, 1):
            for j in (0, 1):
                copy2(p, zz, j).wait_send()
            copy3(p, zz).wait_send()
            pl.when(zz < z)(lambda: copyz(p, zz, False).wait_send())
            pl.when(zz > z)(lambda: copyz(p, zz, True).wait_send())


def plane_maker(planes, pairs, g_ref):
    rows = g_ref.shape[1]
    depth = 8 * rows

    def make_plane(zz):
        base = 0
        for left, right in pairs:
            lhs = left[pl.ds(pl.multiple_of(zz * depth, depth), depth), :]
            width = right.shape[1]

            @pl.loop(0, width // 512)
            def _(i):
                at = pl.multiple_of(i * 512, 512)
                tile = nn(lhs, right[:, pl.ds(at, 512)]).reshape(8, rows, 512).astype(BF)
                g_ref[pl.ds(zz * 8, 8), :, pl.ds(pl.multiple_of(base + at, 512), 512)] = tile

            base += width

    return make_plane


def scatter_kernel(planes, l1, r1, l2, r2, out_ref, g_ref, *scratch):
    pc = Place(planes)
    greet(pc)
    for _ in scatter_steps(
        pc, plane_maker(planes, ((l1, r1), (l2, r2)), g_ref), g_ref, out_ref, scratch
    ):
        pass


def scatter_rows(planes, l1, r1, l2, r2, collective):
    rows = l1.shape[0] // (8 * planes)
    columns = r1.shape[1] + r2.shape[1]
    return pl.pallas_call(
        functools.partial(scatter_kernel, planes),
        out_shape=jax.ShapeDtypeStruct((rows, columns), F32),
        in_specs=[VM] * 4,
        out_specs=VM,
        scratch_shapes=[pltpu.VMEM((8 * planes, rows, columns), BF)]
        + scatter_scratch(planes, rows, columns),
        compiler_params=params(collective),
    )(l1, r1, l2, r2)


def spread_scratch(planes):
    n = 4 * planes
    return [DMA((planes,)), DMA((planes,)), DMA((planes, 2)), DMA((n,)), DMA((n,)), DMA((n,)), DMA((3,))]


def spread_kernel(planes, kv_ref, edge_ref, dec_ref, all_ref, got_ref, decs_ref, *scratch):
    us, xs, cs, rs, ds, dr, one = scratch
    pc = Place(planes)
    Z, z, x, c = pc.Z, pc.z, pc.x, pc.c
    n = 4 * Z
    me = pc.ctx
    greet_row(pc)

    def cp(zz, xx, sem, d, own=False):
        s = pc.spot(zz, xx, c)
        return rcopy(pc, kv_ref if own else all_ref.at[s], all_ref.at[s], sem, rs.at[s], d)

    def arrived(s):
        rcopy(pc, kv_ref, all_ref.at[s], one.at[0], rs.at[s], "c").wait_recv()

    def decay_copy(d, to):
        return rcopy(pc, dec_ref, decs_ref.at[me], ds.at[d], dr.at[d], (lax.rem(to, n), pc.y))

    edge = rcopy(pc, edge_ref, got_ref, one.at[1], one.at[2], (lax.rem(me + 1, n), pc.y))
    keep = pltpu.make_async_copy(kv_ref, all_ref.at[me], one.at[0])
    keep.start()
    pl.when(pc.up)(lambda: cp(z, x, us.at[z], "u", True).start())
    cp(z, x, xs.at[z], "x", True).start()
    cp(z, x, cs.at[z, 0], "c", True).start()
    pl.when(me < n - 1)(lambda: edge.start())
    decs_ref[me] = dec_ref[...]

    @pl.loop(1, n)
    def _(d):
        decay_copy(d, me + d).start()

    for d in range(1, Z):

        @pl.when(z - d >= 0)
        def _():
            zz = z - d
            arrived(pc.spot(zz, x, c))
            pl.when(pc.up)(lambda: cp(zz, x, us.at[zz], "u").start())
            cp(zz, x, xs.at[zz], "x").start()
            cp(zz, x, cs.at[zz, 0], "c").start()

    for d in range(Z):

        @pl.when(z - d >= 0)
        def _():
            arrived(pc.spot(z - d, 1 - x, c))
            cp(z - d, 1 - x, cs.at[z - d, 1], "c").start()

    for d in range(Z):

        @pl.when(z - d >= 0)
        def _():
            for xx in (x, 1 - x):
                arrived(pc.spot(z - d, xx, 1 - c))

    keep.wait()
    for zz in range(Z):

        @pl.when(zz <= z)
        def _():
            pl.when(pc.up)(lambda: cp(zz, x, us.at[zz], "u").wait_send())
            cp(zz, x, xs.at[zz], "x").wait_send()
            cp(zz, x, cs.at[zz, 0], "c").wait_send()
            cp(zz, 1 - x, cs.at[zz, 1], "c").wait_send()

    @pl.when(me < n - 1)
    def _():
        edge.wait_send()

    @pl.when(me > 0)
    def _():
        edge.wait_recv()

    @pl.when(me == 0)
    def _():
        got_ref[...] = jnp.zeros_like(got_ref)

    @pl.loop(1, n)
    def _(d):
        decay_copy(d, me + d).wait()


def spread(planes, kv, edge, dec, collective):
    n = 4 * planes
    return pl.pallas_call(
        functools.partial(spread_kernel, planes),
        out_shape=(
            jax.ShapeDtypeStruct((n,) + kv.shape, kv.dtype),
            jax.ShapeDtypeStruct(edge.shape, edge.dtype),
            jax.ShapeDtypeStruct((n,) + dec.shape, dec.dtype),
        ),
        in_specs=[VM] * 3,
        out_specs=(VM,) * 3,
        scratch_shapes=spread_scratch(planes),
        compiler_params=params(collective),
    )(kv, edge, dec)


def fold_kernel(planes, g_ref, edge_ref, out_ref, got_ref, rc, rx, rz, acc, *scratch):
    cs, cr, xs, xr, zs, zr, one = scratch
    pc = Place(planes)
    Z, z, x, c = pc.Z, pc.z, pc.x, pc.c
    n = 4 * Z
    me = pc.ctx
    greet_row(pc)
    edge = rcopy(pc, edge_ref, got_ref, one.at[0], one.at[1], (lax.rem(me + n - 1, n), pc.y))
    pl.when(me > 0)(lambda: edge.start())

    def ccopy(zz, q):
        xx = x if q == 0 else 1 - x
        return rcopy(
            pc, g_ref.at[pc.spot(zz, xx, 1 - c)], rc.at[zz, q], cs.at[zz, q], cr.at[zz, q], "c"
        )

    def xcopy(zz):
        return rcopy(pc, acc.at[zz, 1], rx.at[zz], xs.at[zz], xr.at[zz], "x")

    def zcopy(zz):
        return rcopy(pc, acc.at[zz, 0], rz.at[zz], zs.at[zz], zr.at[zz], "d")

    def each(f):
        for zz in range(Z):
            pl.when(zz <= z)(functools.partial(f, zz))

    def a(zz):
        ccopy(zz, 1).start()
        ccopy(zz, 0).start()

    def b(zz):
        ccopy(zz, 1).wait_recv()
        add_into(acc.at[zz, 1], [g_ref.at[pc.spot(zz, 1 - x, c)], rc.at[zz, 1]], 128)
        xcopy(zz).start()

    def m(zz):
        ccopy(zz, 0).wait_recv()
        add_into(acc.at[zz, 0], [g_ref.at[pc.spot(zz, x, c)], rc.at[zz, 0]], 128)

    def e(zz):
        xcopy(zz).wait_recv()

        @pl.when(pc.up)
        def _():
            zcopy(zz).wait_recv()

            @pl.when(zz < z)
            def _():
                add_into(acc.at[zz, 0], [acc.at[zz, 0], rx.at[zz], rz.at[zz]], 128)
                zcopy(zz).start()

            @pl.when(zz == z)
            def _():
                add_into(out_ref, [acc.at[zz, 0], rx.at[zz], rz.at[zz]], 128)

        @pl.when(jnp.logical_not(pc.up))
        def _():
            @pl.when(zz < z)
            def _():
                add_into(acc.at[zz, 0], [acc.at[zz, 0], rx.at[zz]], 128)
                zcopy(zz).start()

            @pl.when(zz == z)
            def _():
                add_into(out_ref, [acc.at[zz, 0], rx.at[zz]], 128)

    def w(zz):
        ccopy(zz, 1).wait_send()
        ccopy(zz, 0).wait_send()
        xcopy(zz).wait_send()
        pl.when(zz < z)(lambda: zcopy(zz).wait_send())

    for f in (a, b, m, e, w):
        each(f)
    pl.when(me > 0)(lambda: edge.wait_send())
    pl.when(me < n - 1)(lambda: edge.wait_recv())

    @pl.when(me == n - 1)
    def _():
        got_ref[...] = jnp.zeros_like(got_ref)


def fold(planes, grads, edge, collective):
    n, rows, columns = grads.shape
    return pl.pallas_call(
        functools.partial(fold_kernel, planes),
        out_shape=(
            jax.ShapeDtypeStruct((rows, columns), F32),
            jax.ShapeDtypeStruct(edge.shape, edge.dtype),
        ),
        in_specs=[VM] * 2,
        out_specs=(VM,) * 2,
        scratch_shapes=[
            pltpu.VMEM((planes, 2, rows, columns), BF),
            pltpu.VMEM((planes, rows, columns), BF),
            pltpu.VMEM((planes, rows, columns), BF),
            pltpu.VMEM((planes, 2, rows, columns), BF),
            DMA((planes, 2)),
            DMA((planes, 2)),
            DMA((planes,)),
            DMA((planes,)),
            DMA((planes,)),
            DMA((planes,)),
            DMA((2,)),
        ],
        compiler_params=params(collective),
    )(grads, edge)


def relay_kernel(planes, reverse, s_ref, dec_ref, out_ref, got, part, ss, sr, bs, br):
    pc = Place(planes)
    n = 4 * planes
    me = pc.ctx
    greet_row(pc)

    def to(d):
        return lax.rem(me + d, n)

    def there(d):
        return rcopy(pc, s_ref.at[to(d)], got.at[me], ss.at[d], sr.at[d], (to(d), pc.y))

    def back(d):
        return rcopy(pc, part.at[to(d)], out_ref.at[me], bs.at[d], br.at[d], (to(d), pc.y))

    pl.loop(1, n)(lambda d: there(d).start())
    got[me] = s_ref[me]
    pl.loop(1, n)(lambda d: there(d).wait_recv())
    total = jnp.zeros(got.shape[1:], F32)
    for k in range(n):
        j = n - 1 - k if reverse else k
        part[j] = total.astype(BF)
        total = total * dec_ref[pl.ds(j, 1), :] + got[j].astype(F32)
    pl.loop(1, n)(lambda d: back(d).start())
    out_ref[me] = part[me]

    @pl.loop(1, n)
    def _(d):
        there(d).wait_send()
        back(d).wait()


def relay(planes, reverse, state, decays, collective):
    n = 4 * planes
    piece = state.reshape(n, NS // n, INNER)
    out = pl.pallas_call(
        functools.partial(relay_kernel, planes, reverse),
        out_shape=jax.ShapeDtypeStruct(piece.shape, BF),
        in_specs=[VM] * 2,
        out_specs=VM,
        scratch_shapes=[pltpu.VMEM(piece.shape, BF), pltpu.VMEM(piece.shape, BF)]
        + [DMA((n,))] * 4,
        compiler_params=params(collective),
    )(piece, decays)
    return out.reshape(NS, INNER)


def total_kernel(planes, a_ref, out_ref, rx, rz, ss, sr, zs, zr):
    pc = Place(planes)
    Z, z = pc.Z, pc.z
    bar = pltpu.get_barrier_semaphore()

    def plane(d):
        return pc.dev(lax.rem(z + d, Z), pc.x, pc.y, pc.c)

    for d in "cxy":
        pl.semaphore_signal(bar, inc=1, device_id=pc.near(d), device_id_type=MESH)
    for d in range(1, Z):
        pl.semaphore_signal(bar, inc=1, device_id=plane(d), device_id_type=MESH)
    pl.semaphore_wait(bar, 2 + Z)
    out_ref[...] = a_ref[...]
    for i, d in enumerate("cxy"):
        src = rx.at[2 * i]
        src[...] = out_ref[...]
        cp = rcopy(pc, src, rx.at[2 * i + 1], ss.at[i], sr.at[i], d)
        cp.start()
        cp.wait()
        out_ref[...] = out_ref[...] + rx[2 * i + 1]
    rz[z] = out_ref[...]
    copies = [rcopy(pc, rz.at[z], rz.at[z], zs.at[d], zr.at[d], plane(d)) for d in range(1, Z)]
    for cp in copies:
        cp.start()
    for cp in copies:
        cp.wait()
    total = rz[0]
    for k in range(1, Z):
        total = total + rz[k]
    out_ref[...] = total


def total_small(planes, a, collective):
    return pl.pallas_call(
        functools.partial(total_kernel, planes),
        out_shape=jax.ShapeDtypeStruct(a.shape, F32),
        in_specs=[VM],
        out_specs=VM,
        scratch_shapes=[
            pltpu.VMEM((6,) + a.shape, F32),
            pltpu.VMEM((planes,) + a.shape, F32),
            DMA((3,)),
            DMA((3,)),
            DMA((planes,)),
            DMA((planes,)),
        ],
        compiler_params=params(collective),
    )(a)


def visible(start, block, pos_ref):
    kpos = start + lax.broadcasted_iota(jnp.int32, (block, pos_ref.shape[1]), 0)
    return (kpos <= pos_ref[0:1, :]) & (kpos >= pos_ref[1:2, :])


def attend_kernel(block, span_ref, q_ref, kv_ref, pos_ref, o_ref, lse_ref, m_ref, l_ref, acc_ref):
    rows = pos_ref.shape[1]
    m_ref[...] = jnp.full_like(m_ref, large_negative)
    l_ref[...] = jnp.zeros_like(l_ref)
    acc_ref[...] = jnp.zeros_like(acc_ref)

    @pl.loop(span_ref[0], span_ref[1])
    def _(j):
        start = pl.multiple_of(j * block, block)
        ok = visible(start, block, pos_ref)
        for h in range(QUERY_HEADS):
            g = h // (QUERY_HEADS // KEY_VALUE_HEADS)
            keys = kv_ref[pl.ds(start, block), pl.ds(g * HEAD_WIDTH, HEAD_WIDTH)]
            vals = kv_ref[pl.ds(start, block), pl.ds(KEY_WIDTH + g * HEAD_WIDTH, HEAD_WIDTH)]
            s = jnp.where(ok, nt(keys, q_ref[pl.ds(h * rows, rows), :]), large_negative)
            m0 = m_ref[h : h + 1, :]
            m1 = jnp.maximum(m0, jnp.max(s, axis=0, keepdims=True))
            p = jnp.where(ok, jnp.exp(s - m1), 0.0)
            a = jnp.exp(m0 - m1)
            l_ref[h : h + 1, :] = l_ref[h : h + 1, :] * a + jnp.sum(p, axis=0, keepdims=True)
            m_ref[h : h + 1, :] = m1
            r = pl.ds(h * HEAD_WIDTH, HEAD_WIDTH)
            acc_ref[r, :] = acc_ref[r, :] * a + tn(vals, p.astype(BF))

    lse_ref[...] = m_ref[...] + jnp.log(l_ref[...])
    inv = 1.0 / l_ref[...]
    for h in range(QUERY_HEADS):
        r = pl.ds(h * HEAD_WIDTH, HEAD_WIDTH)
        acc_ref[r, :] = acc_ref[r, :] * inv[h : h + 1, :]
    o_ref[...] = acc_ref[...].T.astype(o_ref.dtype)


def attend(span, q, kv, pos, block):
    rows = pos.shape[1]
    return pl.pallas_call(
        functools.partial(attend_kernel, block),
        out_shape=(
            jax.ShapeDtypeStruct((rows, QUERY_WIDTH), BF),
            jax.ShapeDtypeStruct((QUERY_HEADS, rows), F32),
        ),
        in_specs=[SM, VM, VM, VM],
        out_specs=(VM, VM),
        scratch_shapes=[
            pltpu.VMEM((QUERY_HEADS, rows), F32),
            pltpu.VMEM((QUERY_HEADS, rows), F32),
            pltpu.VMEM((QUERY_WIDTH, rows), F32),
        ],
        compiler_params=params(),
    )(span, q, kv, pos)


def attend_back_kernel(
    block, span_ref, q_ref, do_ref, kv_ref, pos_ref, lse_ref, dl_ref, dq_ref, dkv_ref, acc_ref
):
    rows = pos_ref.shape[1]
    acc_ref[...] = jnp.zeros_like(acc_ref)

    def blank(j):
        dkv_ref[pl.ds(pl.multiple_of(j * block, block), block), :] = jnp.zeros((block, 256), BF)

    pl.loop(0, span_ref[0])(blank)
    pl.loop(span_ref[1], kv_ref.shape[0] // block)(blank)

    @pl.loop(span_ref[0], span_ref[1])
    def _(j):
        start = pl.multiple_of(j * block, block)
        ok = visible(start, block, pos_ref)
        at = pl.ds(start, block)
        dks, dvs = [], []
        for g in range(KEY_VALUE_HEADS):
            keys = kv_ref[at, pl.ds(g * HEAD_WIDTH, HEAD_WIDTH)]
            vals = kv_ref[at, pl.ds(KEY_WIDTH + g * HEAD_WIDTH, HEAD_WIDTH)]
            dk = dv = None
            for h in range(4 * g, 4 * g + 4):
                q = q_ref[pl.ds(h * rows, rows), :]
                do = do_ref[pl.ds(h * rows, rows), :]
                p = jnp.where(ok, jnp.exp(nt(keys, q) - lse_ref[h : h + 1, :]), 0.0)
                ds = (p * (nt(vals, do) - dl_ref[h : h + 1, :])).astype(BF)
                r = pl.ds(h * HEAD_WIDTH, HEAD_WIDTH)
                acc_ref[r, :] += tn(keys, ds)
                a, b = nn(ds, q), nn(p.astype(BF), do)
                dk = a if dk is None else dk + a
                dv = b if dv is None else dv + b
            dks.append(dk)
            dvs.append(dv)
        dkv_ref[at, :] = jnp.concatenate(dks + dvs, axis=1).astype(BF)

    dq_ref[...] = acc_ref[...].T * (HEAD_WIDTH**-0.5)


def attend_back(span, q, do, kv, pos, lse, delta, block):
    rows = pos.shape[1]
    return pl.pallas_call(
        functools.partial(attend_back_kernel, block),
        out_shape=(
            jax.ShapeDtypeStruct((rows, QUERY_WIDTH), F32),
            jax.ShapeDtypeStruct((kv.shape[0], 2 * KEY_WIDTH), BF),
        ),
        in_specs=[SM] + [VM] * 6,
        out_specs=(VM, VM),
        scratch_shapes=[pltpu.VMEM((QUERY_WIDTH, rows), F32)],
        compiler_params=params(),
    )(span, q, do, kv, pos, lse, delta)


def two(left, right, lanes):
    return jnp.where(lanes < MP, left, right)


def pair_columns(ref, p, lanes):
    return two(ref[:, 2 * p : 2 * p + 1], ref[:, 2 * p + 1 : 2 * p + 2], lanes)


def mixer_kernel(
    xe, mk, cw, cb, cum_t, cum, dt_t, we_t, skip, doc_c, doc_r, pre, xo, mix, so, xw, bias
):
    rows = pre.shape[0]
    for i in range(XBC // 256):
        sl = pl.ds(i * 256, 256)
        acc = jnp.broadcast_to(cb[:, sl], (rows, 256))
        for j in range(CONV):
            acc = acc + cw[j : j + 1, sl] * (xe[pl.ds(5 + j, rows), sl] * mk[:, j : j + 1])
        pre[:, sl] = acc
        act = acc * jax.nn.sigmoid(acc)
        xo[:, sl] = act.astype(BF)
        if i < INNER // 256:
            mix[:, sl] = skip[:, sl] * act
    b_rows, c_rows = xo[:, pl.ds(INNER, NS)], xo[:, pl.ds(INNER + NS, NS)]
    cross = nt(c_rows, b_rows)
    t_at = lax.broadcasted_iota(jnp.int32, (rows, rows), 0)
    s_at = lax.broadcasted_iota(jnp.int32, (rows, rows), 1)
    bias[...] = jnp.where((doc_c[...] == doc_r[...]) & (s_at <= t_at), 0.0, large_negative)
    lanes = lax.broadcasted_iota(jnp.int32, (rows, 2 * MP), 1)
    for p in range(MH // 2):
        sl = pl.ds(p * 2 * MP, 2 * MP)
        xd = xo[:, sl].astype(F32) * pair_columns(dt_t, p, lanes)
        xw[:, sl] = (xd * pair_columns(we_t, p, lanes)).astype(BF)
        xb = xd.astype(BF)
        outs = []
        for h in (2 * p, 2 * p + 1):
            low = jnp.exp(jnp.minimum(cum_t[:, h : h + 1] - cum[h : h + 1, :], bias[...]))
            outs.append(nn((low * cross).astype(BF), xb))
        mix[:, sl] = mix[:, sl] + two(outs[0], outs[1], lanes)
    so[...] = tn(b_rows, xw[...]).astype(BF)


def mixer(xe, mk, cw, cb, cum_t, cum, dt_t, we_t, skip, doc_c, doc_r):
    rows = mk.shape[0]
    return pl.pallas_call(
        mixer_kernel,
        out_shape=(
            jax.ShapeDtypeStruct((rows, XBC), F32),
            jax.ShapeDtypeStruct((rows, XBC), BF),
            jax.ShapeDtypeStruct((rows, INNER), F32),
            jax.ShapeDtypeStruct((NS, INNER), BF),
        ),
        in_specs=[VM] * 11,
        out_specs=(VM,) * 4,
        scratch_shapes=[pltpu.VMEM((rows, INNER), BF), pltpu.VMEM((rows, rows), F32)],
        compiler_params=params(),
    )(xe, mk, cw, cb, cum_t, cum, dt_t, we_t, skip, doc_c, doc_r)


def spread_heads():
    head = lax.broadcasted_iota(jnp.int32, (MH, INNER), 0)
    lane = lax.broadcasted_iota(jnp.int32, (MH, INNER), 1)
    return (lane // MP == head).astype(F32)


def wide(columns, spread_mat):
    return lax.dot_general(
        columns,
        spread_mat,
        (((1,), (0,)), ((), ())),
        precision=lax.Precision.HIGHEST,
        preferred_element_type=F32,
    )


def gate_kernel(mix, xo, state, din_t, gate, gain, att, mixed, branch):
    rows = mix.shape[0]
    spread_mat = spread_heads()

    @pl.loop(0, rows // 64)
    def _(i):
        r = pl.ds(pl.multiple_of(i * 64, 64), 64)
        carried = nn(xo[r, pl.ds(INNER + NS, NS)], state[...])
        m = mix[r, :] + carried * wide(din_t[r, :], spread_mat)
        mixed[r, :] = m
        gv = gate[r, :]
        gated = m * (gv * jax.nn.sigmoid(gv))
        factor = lax.rsqrt(jnp.mean(gated * gated, axis=1, keepdims=True) + norm_eps)
        branch[r, pl.ds(0, QUERY_WIDTH)] = att[r, :]
        branch[r, pl.ds(QUERY_WIDTH, INNER)] = (gated * factor * gain[...]).astype(BF)


def gate_out(mix, xo, state, din_t, gate, gain, att):
    rows = mix.shape[0]
    return pl.pallas_call(
        gate_kernel,
        out_shape=(
            jax.ShapeDtypeStruct((rows, INNER), F32),
            jax.ShapeDtypeStruct((rows, MIXOUT), BF),
        ),
        in_specs=[VM] * 7,
        out_specs=(VM,) * 2,
        compiler_params=params(),
    )(mix, xo, state, din_t, gate, gain, att)


def gate_back_kernel(grad, mixed, gate, gain, din_t, xo, state, dm, dgate, dgain, dstate, dc, dinc):
    rows = mixed.shape[0]
    spread_mat = spread_heads()
    dgain[...] = jnp.zeros_like(dgain)

    @pl.loop(0, rows // 64)
    def _(i):
        r = pl.ds(pl.multiple_of(i * 64, 64), 64)
        m, gv, gr = mixed[r, :], gate[r, :], grad[r, :]
        sig = jax.nn.sigmoid(gv)
        sil = gv * sig
        gated = m * sil
        factor = lax.rsqrt(jnp.mean(gated * gated, axis=1, keepdims=True) + norm_eps)
        w = gr * gain[...]
        dg = factor * (w - gated * factor * factor * jnp.mean(w * gated, axis=1, keepdims=True))
        dgain[...] += jnp.sum(gr * gated * factor, axis=0, keepdims=True)
        dgate[r, :] = (dg * m * (sig * (1.0 + gv * (1.0 - sig)))).astype(BF)
        d = dg * sil
        dm[r, :] = d.astype(BF)
        dinc[r, :] = (d * wide(din_t[r, :], spread_mat)).astype(BF)

    dstate[...] = tn(xo[:, pl.ds(INNER + NS, NS)], dinc[...]).astype(BF)
    dc[...] = nt(dinc[...], state[...])


def gate_back(grad, mixed, gate, gain, din_t, xo, state):
    rows = mixed.shape[0]
    return pl.pallas_call(
        gate_back_kernel,
        out_shape=(
            jax.ShapeDtypeStruct((rows, INNER), BF),
            jax.ShapeDtypeStruct((rows, INNER), BF),
            jax.ShapeDtypeStruct((1, INNER), F32),
            jax.ShapeDtypeStruct((NS, INNER), BF),
            jax.ShapeDtypeStruct((rows, NS), F32),
        ),
        in_specs=[VM] * 7,
        out_specs=(VM,) * 5,
        scratch_shapes=[pltpu.VMEM((rows, INNER), BF)],
        compiler_params=params(),
    )(grad, mixed, gate, gain, din_t, xo, state)


def mixer_back_kernel(
    xe, mk, cw, cum_t, cum, dt_t, we_t, skip, doc_c, doc_r, pre, xo, dm, dc_in, ds,
    dpre, dcw, dskip, xw, bias,
):
    rows = pre.shape[0]
    b_rows, c_rows = xo[:, pl.ds(INNER, NS)], xo[:, pl.ds(INNER + NS, NS)]
    cross = nt(b_rows, c_rows)
    s_at = lax.broadcasted_iota(jnp.int32, (rows, rows), 0)
    t_at = lax.broadcasted_iota(jnp.int32, (rows, rows), 1)
    bias[...] = jnp.where((doc_c[...] == doc_r[...]) & (s_at <= t_at), 0.0, large_negative)
    lanes = lax.broadcasted_iota(jnp.int32, (rows, 2 * MP), 1)

    def slope(sl):
        v = pre[:, sl]
        sig = jax.nn.sigmoid(v)
        return sig * (1.0 + v * (1.0 - sig))

    dcross = jnp.zeros((rows, rows), F32)
    for p in range(MH // 2):
        sl = pl.ds(p * 2 * MP, 2 * MP)
        xv = xo[:, sl].astype(F32)
        dt2, we2 = pair_columns(dt_t, p, lanes), pair_columns(we_t, p, lanes)
        xd = xv * dt2
        xw[:, sl] = (xd * we2).astype(BF)
        g = dm[:, sl]
        outs = []
        for k in (0, 1):
            h = 2 * p + k
            low = jnp.exp(jnp.minimum(cum[h : h + 1, :] - cum_t[:, h : h + 1], bias[...]))
            outs.append(nn((low * cross).astype(BF), g))
            part = jnp.where((lanes < MP) == (k == 0), xd, 0.0).astype(BF)
            dcross = dcross + nt(part, g) * low
        dxd = two(outs[0], outs[1], lanes) + we2 * nn(b_rows, ds[:, sl])
        gf = g.astype(F32)
        dskip[:, sl] = jnp.sum(gf * xv, axis=0, keepdims=True)
        dpre[:, sl] = (dxd * dt2 + skip[:, sl] * gf) * slope(sl)
    db16 = dcross.astype(BF)
    slb, slc = pl.ds(INNER, NS), pl.ds(INNER + NS, NS)
    dpre[:, slb] = (nn(db16, c_rows) + nt(xw[...], ds[...])) * slope(slb)
    dpre[:, slc] = (tn(db16, b_rows) + dc_in[...]) * slope(slc)
    for i in range(XBC // 256):
        sl = pl.ds(i * 256, 256)
        d = dpre[:, sl]
        for j in range(CONV):
            dcw[j : j + 1, sl] = jnp.sum(
                d * (xe[pl.ds(5 + j, rows), sl] * mk[:, j : j + 1]), axis=0, keepdims=True
            )
        dcw[CONV : CONV + 1, sl] = jnp.sum(d, axis=0, keepdims=True)


def mixer_back(xe, mk, cw, cum_t, cum, dt_t, we_t, skip, doc_c, doc_r, pre, xo, dm, dc_in, ds):
    rows = mk.shape[0]
    return pl.pallas_call(
        mixer_back_kernel,
        out_shape=(
            jax.ShapeDtypeStruct((rows, XBC), F32),
            jax.ShapeDtypeStruct((CONV + 1, XBC), F32),
            jax.ShapeDtypeStruct((1, INNER), F32),
        ),
        in_specs=[VM] * 15,
        out_specs=(VM,) * 3,
        scratch_shapes=[pltpu.VMEM((rows, INNER), BF), pltpu.VMEM((rows, rows), F32)],
        compiler_params=params(),
    )(xe, mk, cw, cum_t, cum, dt_t, we_t, skip, doc_c, doc_r, pre, xo, dm, dc_in, ds)


def doc_layout(lengths, token_positions):
    starts = jnp.cumsum(lengths) - lengths
    inside = token_positions[:, None] >= starts[None, :]
    document_index = jnp.sum(inside.astype(jnp.int32), axis=1) - 1
    begins = jnp.max(jnp.where(inside, starts[None, :], 0), axis=1)
    return (document_index, token_positions - begins)


def rope_tables(rel_pos):
    half_dim = HEAD_WIDTH // 2
    inv_freq = rope_base ** (-2.0 * jnp.arange(half_dim, dtype=jnp.float32) / HEAD_WIDTH)
    angles = rel_pos.astype(jnp.float32)[:, None] * inv_freq[None, :]
    return (jnp.cos(angles), jnp.sin(angles))


def apply_rotary(values, cosine_table, sine_table):
    half_dim = values.shape[-1] // 2
    lower_half = values[..., :half_dim]
    upper_half = values[..., half_dim:]
    cos_rows = cosine_table[:, None, :]
    sin_rows = sine_table[:, None, :]
    return jnp.concatenate(
        [
            lower_half * cos_rows - upper_half * sin_rows,
            upper_half * cos_rows + lower_half * sin_rows,
        ],
        axis=-1,
    )


def inverse_rotary(grads, cosine_table, sine_table):
    half_dim = grads.shape[-1] // 2
    lower_half = grads[..., :half_dim]
    upper_half = grads[..., half_dim:]
    cos_rows = cosine_table[:, None, :]
    sin_rows = sine_table[:, None, :]
    return jnp.concatenate(
        [
            lower_half * cos_rows + upper_half * sin_rows,
            upper_half * cos_rows - lower_half * sin_rows,
        ],
        axis=-1,
    )


def split_small(vector):
    widths = (D, D, INNER, CONV * XBC, XBC, MH)
    pieces = []
    offset = 0
    for span_width in widths:
        pieces.append(vector[offset : offset + span_width])
        offset += span_width
    return (pieces[0], pieces[1], pieces[2], pieces[3].reshape(CONV, XBC), pieces[4], pieces[5])


def norm_backward(grad_normed, values, factor, gain_vals):
    weighted = grad_normed * gain_vals
    grad_values = factor * (
        weighted - values * factor * factor * jnp.mean(weighted * values, axis=1, keepdims=True)
    )
    grad_gain = jnp.sum(grad_normed * values * factor, axis=0)
    return (grad_values, grad_gain)


def adamw_step(param_vals, grad_vals, first_vals, second_vals, weight_decay):
    first_new = beta_one * first_vals + (1.0 - beta_one) * grad_vals
    second_new = beta_two * second_vals + (1.0 - beta_two) * grad_vals * grad_vals
    update = (
        first_new
        / (1.0 - beta_one**STEP)
        / (jnp.sqrt(second_new / (1.0 - beta_two**STEP)) + adam_eps)
    )
    return (param_vals - learn_rate * (update + weight_decay * param_vals), first_new, second_new)


def adam_direction(grad_vals, first_vals, second_vals):
    first_new = beta_one * first_vals + (1.0 - beta_one) * grad_vals
    second_new = beta_two * second_vals + (1.0 - beta_two) * grad_vals * grad_vals
    update = (
        first_new
        / (1.0 - beta_one**STEP)
        / (jnp.sqrt(second_new / (1.0 - beta_two**STEP)) + adam_eps)
    )
    return (update, first_new, second_new)


def by_head(rows):
    tokens = rows.shape[0]
    return (
        rows.reshape(tokens, QUERY_HEADS, HEAD_WIDTH)
        .transpose(1, 0, 2)
        .reshape(QUERY_HEADS * tokens, HEAD_WIDTH)
    )


def shards(
    planes,
    hidden,
    out_grad,
    decay_log,
    doc_lengths,
    weights,
    first_moment,
    second_moment,
    small_params,
    small_first,
    small_second,
):
    local_rows = hidden.shape[1]
    count = 4 * planes
    ctx_index = lax.axis_index("ctx")
    first_pos = ctx_index * local_rows
    scale_qk = HEAD_WIDTH ** (-0.5)
    contract_last = (((1,), (1,)), ((), ()))
    gain_one, gain_two, gate_gain, conv_w, conv_bias, skip_gain = split_small(small_params)
    lengths = doc_lengths[0]
    token_positions = first_pos + jnp.arange(local_rows, dtype=jnp.int32)
    near_positions = first_pos + jnp.arange(-(CONV - 1), local_rows + CONV - 1, dtype=jnp.int32)
    near_doc = doc_layout(lengths, near_positions)[0]
    document_index, rel_pos = doc_layout(lengths, token_positions)
    doc_before = near_doc[CONV - 2]
    is_start = document_index != near_doc[CONV - 2 : CONV - 2 + local_rows]
    cosine_table, sine_table = rope_tables(rel_pos)
    begins = token_positions - rel_pos
    pos = jnp.stack([token_positions, begins])
    block = 512
    span = jnp.stack([jnp.min(begins) // block, (first_pos + local_rows - 1) // block + 1])

    tok_f = hidden[0].astype(jnp.float32)
    scale_one = lax.rsqrt(jnp.mean(tok_f * tok_f, axis=1, keepdims=True) + norm_eps)
    normed_one = (tok_f * scale_one * gain_one).astype(jnp.bfloat16)
    own_b = weights.astype(jnp.bfloat16)
    mixer_w = gather_rows(own_b[:, : MIXIN + MIXOUT], planes, 0).reshape(D, MIXIN + MIXOUT)
    mlp_w = lax.all_gather(own_b[:, MIXIN + MIXOUT :], ("ctx", "fsdp"), axis=0, tiled=True)
    projected = jnp.dot(normed_one, mixer_w[:, :MIXIN], preferred_element_type=jnp.float32)
    query_rows = apply_rotary(
        projected[:, :QUERY_WIDTH].reshape(local_rows, QUERY_HEADS, HEAD_WIDTH),
        cosine_table,
        sine_table,
    ).astype(jnp.bfloat16)
    key_rows = apply_rotary(
        projected[:, QUERY_WIDTH : QUERY_WIDTH + KEY_WIDTH].reshape(
            local_rows, KEY_VALUE_HEADS, HEAD_WIDTH
        ),
        cosine_table,
        sine_table,
    ).reshape(local_rows, KEY_WIDTH)
    kv_rows = jnp.concatenate(
        [key_rows, projected[:, QUERY_WIDTH + KEY_WIDTH : QUERY_WIDTH + 2 * KEY_WIDTH]], axis=1
    ).astype(jnp.bfloat16)
    gate_in = projected[:, QUERY_WIDTH + 2 * KEY_WIDTH : QUERY_WIDTH + 2 * KEY_WIDTH + INNER]
    xbc_b = projected[:, QUERY_WIDTH + 2 * KEY_WIDTH + INNER :].astype(jnp.bfloat16)
    query_heads = by_head(query_rows.reshape(local_rows, QUERY_WIDTH) * jnp.bfloat16(scale_qk))

    log_decay = decay_log[0]
    cum = jnp.cumsum(log_decay, axis=1)
    steps_in = jnp.where(is_start[None, :], 1.0, jnp.sqrt(-jnp.expm1(2.0 * log_decay)))
    decay_in = jnp.where((document_index == doc_before)[None, :], jnp.exp(cum), 0.0)
    same_end = (document_index == document_index[-1])[None, :]
    to_end = jnp.where(same_end, jnp.exp(jnp.minimum(cum[:, -1:] - cum, 0.0)), 0.0)
    cum_t, dt_t, we_t, din_t = cum.T, steps_in.T, to_end.T, decay_in.T
    own_decay = jnp.zeros((8, 128), jnp.float32).at[0, :MH].set(decay_in[:, -1])

    kv_all, edge_in, decays = spread(planes, kv_rows, xbc_b[local_rows - 16 :], own_decay, 1)
    decays = jnp.repeat(decays[:, 0, :MH], MP, axis=1)
    kv_flat = kv_all.reshape(count * local_rows, 2 * KEY_WIDTH)

    same_doc = jnp.stack(
        [near_doc[j : j + local_rows] == document_index for j in range(CONV)], axis=1
    ).astype(jnp.float32)
    xe = jnp.concatenate(
        [
            jnp.zeros((9 - CONV, XBC), jnp.float32),
            edge_in[17 - CONV :].astype(jnp.float32),
            xbc_b.astype(jnp.float32),
        ],
        axis=0,
    )
    skip_wide = jnp.repeat(skip_gain, MP)[None, :]
    doc_c, doc_r = document_index[:, None], document_index[None, :]
    pre, xo, mix_local, state_out = mixer(
        xe, same_doc, conv_w, conv_bias[None, :], cum_t, cum, dt_t, we_t, skip_wide, doc_c, doc_r
    )
    state_in = relay(planes, False, state_out, decays, 2)
    attended, log_sums = attend(span, query_heads, kv_flat, pos, block)
    mixed, branch = gate_out(
        mix_local, xo, state_in, din_t, gate_in, gate_gain[None, :], attended
    )

    resid_one = tok_f + lax.dot_general(
        branch, mixer_w[:, MIXIN:], contract_last, preferred_element_type=jnp.float32
    )
    scale_two = lax.rsqrt(jnp.mean(resid_one * resid_one, axis=1, keepdims=True) + norm_eps)
    normed_two = (resid_one * scale_two * gain_two).astype(jnp.bfloat16)
    gate_up = jnp.dot(normed_two, mlp_w[:, : 2 * FF], preferred_element_type=jnp.float32)
    gate_part = gate_up[:, :FF]
    up_part = gate_up[:, FF:]
    sigma_gate = jax.nn.sigmoid(gate_part)
    silu_gate = gate_part * sigma_gate
    hidden_mid = (silu_gate * up_part).astype(jnp.bfloat16)
    block_out = resid_one + lax.dot_general(
        hidden_mid, mlp_w[:, 2 * FF :], contract_last, preferred_element_type=jnp.float32
    )
    out_hidden = block_out.astype(jnp.bfloat16)[None]
    grad_out = out_grad[0]
    grad_mid = jnp.dot(grad_out, mlp_w[:, 2 * FF :], preferred_element_type=jnp.float32)
    silu_slope = sigma_gate * (1.0 + gate_part * (1.0 - sigma_gate))
    grad_gate_up = jnp.concatenate(
        [grad_mid * up_part * silu_slope, grad_mid * silu_gate], axis=1
    ).astype(jnp.bfloat16)
    grad_normed_two = lax.dot_general(
        grad_gate_up, mlp_w[:, : 2 * FF], contract_last, preferred_element_type=jnp.float32
    )
    grad_norm_two, grad_gain_two = norm_backward(grad_normed_two, resid_one, scale_two, gain_two)
    grad_resid_one = grad_out.astype(jnp.float32) + grad_norm_two
    grad_resid_b = grad_resid_one.astype(jnp.bfloat16)
    mlp_grads = scatter_rows(planes, normed_two.T, grad_gate_up, grad_out.T, hidden_mid, 3)

    grad_branch = jnp.dot(grad_resid_b, mixer_w[:, MIXIN:], preferred_element_type=jnp.float32)
    grad_attended = grad_branch[:, :QUERY_WIDTH].astype(jnp.bfloat16)
    grad_mixed, grad_gate_in, grad_gate_gain, grad_state, grad_c = gate_back(
        grad_branch[:, QUERY_WIDTH:], mixed, gate_in, gate_gain[None, :], din_t, xo, state_in
    )
    grad_state_out = relay(planes, True, grad_state, decays, 4)
    delta = jnp.sum(
        (grad_attended.astype(jnp.float32) * attended.astype(jnp.float32)).reshape(
            local_rows, QUERY_HEADS, HEAD_WIDTH
        ),
        axis=-1,
    ).T
    grad_query, kv_grads = attend_back(
        span, query_heads, by_head(grad_attended), kv_flat, pos, log_sums, delta, block
    )
    grad_pre, conv_grads, skip_grads = mixer_back(
        xe, same_doc, conv_w, cum_t, cum, dt_t, we_t, skip_wide, doc_c, doc_r,
        pre, xo, grad_mixed, grad_c, grad_state_out,
    )
    key_gradients, pre_next = fold(
        planes, kv_grads.reshape(count, local_rows, 2 * KEY_WIDTH), grad_pre[:8], 5
    )
    pre_ext = jnp.concatenate([grad_pre, pre_next[: CONV - 1]], axis=0)
    doc_next = near_doc[CONV - 1 :]
    grad_xbc = sum(
        conv_w[j][None, :]
        * pre_ext[CONV - 1 - j : CONV - 1 - j + local_rows]
        * (doc_next[CONV - 1 - j : CONV - 1 - j + local_rows] == document_index)[:, None]
        for j in range(CONV)
    )
    grad_q = inverse_rotary(
        grad_query.reshape(local_rows, QUERY_HEADS, HEAD_WIDTH), cosine_table, sine_table
    ).reshape(local_rows, QUERY_WIDTH)
    key_gradient = inverse_rotary(
        key_gradients[:, :KEY_WIDTH].reshape(local_rows, KEY_VALUE_HEADS, HEAD_WIDTH),
        cosine_table,
        sine_table,
    ).reshape(local_rows, KEY_WIDTH)
    grad_proj = jnp.concatenate(
        [
            grad_q.astype(jnp.bfloat16),
            key_gradient.astype(jnp.bfloat16),
            key_gradients[:, KEY_WIDTH:].astype(jnp.bfloat16),
            grad_gate_in,
            grad_xbc.astype(jnp.bfloat16),
        ],
        axis=1,
    )
    mixer_grads = scatter_rows(planes, normed_one.T, grad_proj, grad_resid_b.T, branch, 6)
    grad_normed_one = lax.dot_general(
        grad_proj, mixer_w[:, :MIXIN], contract_last, preferred_element_type=jnp.float32
    )
    grad_norm_one, grad_gain_one = norm_backward(grad_normed_one, tok_f, scale_one, gain_one)
    grad_hidden = (grad_resid_one + grad_norm_one)[None]
    small_local = jnp.concatenate(
        [
            grad_gain_one,
            grad_gain_two,
            grad_gate_gain[0],
            conv_grads.reshape(-1),
            jnp.sum(skip_grads.reshape(MH, MP), axis=1),
        ]
    )
    size = small_local.shape[0]
    padded = jnp.pad(small_local, (0, SMALL_ROWS * 128 - size)).reshape(SMALL_ROWS, 128)
    small_grads = total_small(planes, padded, 7).reshape(-1)[:size]
    grad_weights = jnp.concatenate([mixer_grads, mlp_grads], axis=1)
    new_weights, new_first, new_second = adamw_step(
        weights, grad_weights, first_moment, second_moment, decay_rate
    )
    small_step, small_first_new, small_second_new = adam_direction(
        small_grads, small_first, small_second
    )
    return (
        out_hidden,
        grad_hidden,
        grad_weights,
        new_weights,
        new_first,
        new_second,
        small_grads,
        small_step,
        small_first_new,
        small_second_new,
    )


def solution(mesh):
    placed = (
        P("fsdp", "ctx", None),
        P("fsdp", "ctx", None),
        P("fsdp", None, "ctx"),
        P("fsdp", None),
        P(("ctx", "fsdp"), None),
        P(("ctx", "fsdp"), None),
        P(("ctx", "fsdp"), None),
        P(),
        P(),
        P(),
    )
    return jax.shard_map(
        functools.partial(shards, mesh.shape["ctx"] // 4),
        mesh=mesh,
        in_specs=placed,
        out_specs=(
            P("fsdp", "ctx", None),
            P("fsdp", "ctx", None),
            P(("ctx", "fsdp"), None),
            P(("ctx", "fsdp"), None),
            P(("ctx", "fsdp"), None),
            P(("ctx", "fsdp"), None),
            P(),
            P(),
            P(),
            P(),
        ),
        check_vma=False,
    )
```

time: 1170 us -> 558 us (0.48)
  waiting for transfers between devices: 581 us -> 0.04 us
  Pallas kernels: 0 us -> 434 us
  matrix products: 237 us -> 34 us
  other arithmetic: 150 us -> 29 us
  blocking collectives: 73.7 us -> 0 us
  local copies, waits for them, and re-layouts: 92.3 us -> 38 us
    pallas_call x0 -> x14, Pallas kernels: none -> 434 us  [the longest x2 161 us: scatter_rows(): pl.pallas_call(functools.partial(scatter_kernel, planes), out_shape=jax.S...]
    reduce_scatter x2 -> x0, waiting for transfers between devices: 375 us -> none  [the longest x1 372 us: shards(): lax.psum_scatter(jnp.concatenate([row_product(normed_one, grad_proj), row...]
    dot_general x74 -> x0, matrix products: 197 us -> none  [the longest x16 29 us: block_scores(): jnp.einsum('tgqd,sgd->tgqs', grouped_query, key_tile.reshape(block_length...]
    all_gather x5 -> x0, waiting for transfers between devices: 163 us -> none  [the longest x1 99 us: shards(): lax.all_gather(own_b[:, :MIXIN + MIXOUT], ('ctx', 'fsdp'), axis=0, tiled=...]
    psum x1 -> x0, blocking collectives: 41.6 us -> none  [shards(): small_grads = lax.psum(small_local, ('ctx', 'fsdp'))]
    all_gather x1, waiting for transfers between devices: 40.9 us -> 0.02 us  [shards(): lax.all_gather(own_b[:, MIXIN + MIXOUT:], ('ctx', 'fsdp'), axis=0, tiled=...]
    reduce_sum x14 -> x4, other arithmetic: 41.7 us -> 3.03 us  [the longest x2 2.28 us: norm_backward(): grad_gain = jnp.sum(grad_normed * values * factor, axis=0)]
    dynamic_slice x32 -> x0, local copies, waits for them, and re-layouts: 35.4 us -> none  [shards(): lax.scan(absorb, (initial_accumulator, initial_maximum, initial_sum), (ke...]
  transfers between devices with their start and end apart: 10 -> 1, of which waited for: 8 -> 0; matrix products, arithmetic and copies ran while one was open for 21% -> 7% of each run, Pallas kernels for 0% -> 26%
where the time goes in v1:
time: 558 us; the launch traced here: 553 us
  Pallas kernels  434 us (78%)
  local copies, waits for them, and re-layouts  38 us (7%)
  matrix products  34 us (6%)
  other arithmetic  29 us (5%)
  between operations  17.8 us (3%)
    pallas_call x2, Pallas kernels, scatter_rows(): pl.pallas_call(functools.partial(scatter_kernel, planes), out_shape=jax.S...  161 us
    pallas_call x2, Pallas kernels, relay(): pl.pallas_call(functools.partial(relay_kernel, planes, reverse), out_shap...  86.9 us
    pallas_call x1, Pallas kernels, gather_rows(): pl.pallas_call(functools.partial(gather_kernel, planes), out_shape=jax.Sh...  76.8 us
    pallas_call x1, Pallas kernels, fold(): pl.pallas_call(functools.partial(fold_kernel, planes), out_shape=(jax.Sha...  27.6 us
    pallas_call x1, Pallas kernels, total_small(): pl.pallas_call(functools.partial(total_kernel, planes), out_shape=jax.Sha...  24.1 us
    pallas_call x1, Pallas kernels, spread(): pl.pallas_call(functools.partial(spread_kernel, planes), out_shape=(jax.S...  13.1 us
    unnamed x67, local copies, waits for them, and re-layouts  11.5 us
  transfers between devices with their start and end apart: 1, of which 0 were waited for; matrix products, arithmetic and copies ran while one was open for 7% of the time, Pallas kernels for 26%

profile of v1, /device:TPU:0, one launch (start us, length us, event | category | flops | bytes accessed | tf_op | source)
XLA Modules:
  0.0 553.1 jit_solution(1868031408904868008)
XLA Ops:
  9.7 76.8 %shard_map.177 = bf16[32,32,6144]{2,1,0:T(8,128)(2,1)} custom-call(bf16[32,6144]{1,0:T(8,128)(2,1)} %get-tuple-element.143.w_ref), custom_call_target="tpu_custom_call" | custom-call | tf_op jit(solution)/shard_map/pallas_call | solution.py:269
  86.9 7.9 %fusion.73 = (bf16[256,4096]{1,0:T(8,128)(2,1)S(1)}, f32[256,4096]{1,0:T(8,128)}) fusion(bf16[1024,6144]{1,0:T(8,128)(2,1)} %bitcast.91, bf16[1,256,1024]{1,2,0:T(8,128)(2,1)S(1)} %copy.127, f32[1024]{0:T(1024)S(1)} %get-tuple-element.161, f32[256]{0:T(256)S(1)} %add_rsqrt_fusion.1), kind=kOutput, calls=%fused_computation.154 | convolution fusion | flops 2149580800 | bytes 15209472 | tf_op jit(solution)/shard_map/dot_general | solution.py:1230
  97.8 2.7 slice.279.gate
  116.8 13.1 %shard_map.178 = (bf16[16,256,256]{2,1,0:T(8,128)(2,1)}, bf16[16,1792]{1,0:T(8,128)(2,1)}, f32[16,8,128]{2,1,0:T(8,128)}) custom-call(bf16[256,256]{1,0:T(8,128)(2,1)} %pad_maximum_fusion.5.kv_ref, bf16[16,1792]{1,0:T(8,128)(2,1)} %slice.274.edge_ref, f32[8,128]{1,0:T(8,128)} %scatter.4.dec_ref), custom_call_target="tpu_custom_call" | custom-call | tf_op jit(solution)/shard_map/pallas_call | solution.py:551
  138.1 8.4 %shard_map.179 = (f32[256,1792]{1,0:T(8,128)}, bf16[256,1792]{1,0:T(8,128)(2,1)}, f32[256,1536]{1,0:T(8,128)}, bf16[128,1536]{1,0:T(8,128)(2,1)}) custom-call(f32[264,1792]{1,0:T(8,128)} %pad_maximum_fusion.1.xe, f32[256,4]{1,0:T(8,128)} %convert_element_type.101.mk, f32[4,1792]{1,0:T(4,128)} %reshape.297.cw, f32[1,1792]{1,0:T(1,128)} %broadcast_in_dim.58.cb, ...), custom_call_target="tpu_custom_call" | custom-call | tf_op jit(solution)/shard_map/pallas_call | solution.py:925
  146.5 32.0 %shard_map.180 = bf16[16,8,1536]{2,1,0:T(8,128)(2,1)} custom-call(bf16[16,8,1536]{2,1,0:T(8,128)(2,1)} %bitcast.118, f32[16,1536]{1,0:T(8,128)} %reshape.299.dec_ref), custom_call_target="tpu_custom_call" | custom-call | tf_op jit(solution)/shard_map/pallas_call | solution.py:709
  179.7 6.4 %shard_map.181 = (bf16[256,512]{1,0:T(8,128)(2,1)}, f32[8,256]{1,0:T(8,128)}) custom-call(s32[2]{0:T(128)} %pad_add_fusion.2.span_ref, bf16[2048,64]{1,0:T(8,128)(2,1)} %bitcast.98, bf16[4096,256]{1,0:T(8,128)(2,1)} %bitcast.95, s32[2,256]{1,0:T(2,128)} %pad_add_fusion.1.pos_ref), custom_call_target="tpu_custom_call" | custom-call | tf_op jit(solution)/shard_map/pallas_call | solution.py:811
  186.1 6.3 %shard_map.182 = (f32[256,1536]{1,0:T(8,128)}, bf16[256,2048]{1,0:T(8,128)(2,1)}) custom-call(f32[256,1536]{1,0:T(8,128)} %get-tuple-element.46.mix, bf16[256,1792]{1,0:T(8,128)(2,1)} %get-tuple-element.47.xo, bf16[128,1536]{1,0:T(8,128)(2,1)} %bitcast.100, f32[256,24]{1,0:T(8,128)} %bitcast.111, f32[256,1536]{1,0:T(8,128)} %slice.279.gate, ...), custom_call_target="tpu_custom_call" | custom-call | tf_op jit(solution)/shard_map/pallas_call | solution.py:975
  192.4 3.8 multiply_reduce_fusion.2
  196.3 6.0 %fusion.2 = f32[256,4096]{1,0:T(8,128)S(1)} fusion(bf16[1024,6144]{1,0:T(8,128)(2,1)} %all-gather.2.cloned.1.call-done, f32[256,1024]{0,1:T(8,128)S(1)} %get-tuple-element.180, f32[1024]{0:T(1024)S(1)} %get-tuple-element.160, f32[256]{0:T(256)S(1)} %add_rsqrt_fusion), kind=kOutput, calls=%fused_computation.2 | convolution fusion | flops 2148270080 | bytes 13636608 | tf_op jit(solution)/shard_map/dot_general | solution.py:1290
  205.5 2.4 fusion
  210.1 3.5 fusion.12
  222.5 7.6 %shard_map.183 = (f32[256,512]{1,0:T(8,128)}, bf16[4096,256]{1,0:T(8,128)(2,1)}) custom-call(s32[2]{0:T(128)} %pad_add_fusion.2.span_ref, bf16[2048,64]{1,0:T(8,128)(2,1)} %bitcast.99, bf16[2048,64]{1,0:T(8,128)(2,1)} %bitcast.109, bf16[4096,256]{1,0:T(8,128)(2,1)} %bitcast.96, s32[2,256]{1,0:T(2,128)} %pad_add_fusion.1.pos_ref, ...), custom_call_target="tpu_custom_call" | custom-call | tf_op jit(solution)/shard_map/pallas_call | solution.py:869
  232.4 6.2 %shard_map.184 = (bf16[256,1536]{1,0:T(8,128)(2,1)}, bf16[256,1536]{1,0:T(8,128)(2,1)}, f32[1,1536]{1,0:T(1,128)}, bf16[128,1536]{1,0:T(8,128)(2,1)}, f32[256,128]{1,0:T(8,128)}) custom-call(f32[256,1536]{1,0:T(8,128)} %slice.292.grad, f32[256,1536]{1,0:T(8,128)} %get-tuple-element.57.mixed, f32[256,1536]{1,0:T(8,128)} %slice.279.gate, ...), custom_call_target="tpu_custom_call" | custom-call | tf_op jit(solution)/shard_map/pallas_call | solution.py:1014
  238.6 54.9 %shard_map.185 = bf16[16,8,1536]{2,1,0:T(8,128)(2,1)} custom-call(bf16[16,8,1536]{2,1,0:T(8,128)(2,1)} %bitcast.117, f32[16,1536]{1,0:T(8,128)} %reshape.299.dec_ref), custom_call_target="tpu_custom_call" | custom-call | tf_op jit(solution)/shard_map/pallas_call | solution.py:709
  293.5 9.6 %shard_map.186 = (f32[256,1792]{1,0:T(8,128)}, f32[5,1792]{1,0:T(8,128)}, f32[1,1536]{1,0:T(1,128)}) custom-call(f32[264,1792]{1,0:T(8,128)} %pad_maximum_fusion.1.xe, f32[256,4]{1,0:T(8,128)} %convert_element_type.101.mk, f32[4,1792]{1,0:T(4,128)} %reshape.297.cw, f32[256,24]{1,0:T(8,128)} %bitcast.105, f32[24,256]{1,0:T(8,128)} %copy.135.cum, ...), custom_call_target="tpu_custom_call" | custom-call | tf_op jit(solution)/shard_map/pallas_call | solution.py:1082
  304.6 27.6 %shard_map.187 = (f32[256,256]{1,0:T(8,128)}, f32[8,1792]{1,0:T(8,128)}) custom-call(bf16[16,256,256]{2,1,0:T(8,128)(2,1)} %bitcast.106, f32[8,1792]{1,0:T(8,128)} %slice.251.edge_ref), custom_call_target="tpu_custom_call" | custom-call | tf_op jit(solution)/shard_map/pallas_call | solution.py:649
  339.5 2.1 constant_dynamic-update-slice_fusion
  341.6 3.7 fusion.53.r1
  345.4 6.4 %fusion.4 = f32[256,1024]{0,1:T(8,128)S(1)} fusion(bf16[256,4096]{1,0:T(8,128)(2,1)} %fusion.53.r1, bf16[1024,6144]{1,0:T(8,128)(2,1)} %bitcast.94), kind=kOutput, calls=%fused_computation.4 | convolution fusion | flops 2147483648 | bytes 11534336 | tf_op jit(solution)/shard_map/dot_general | solution.py:1363
  355.5 24.1 %shard_map.190 = f32[104,128]{1,0:T(8,128)} custom-call(f32[104,128]{1,0:T(8,128)} %pad_bitcast_fusion.a_ref), custom_call_target="tpu_custom_call" | custom-call | tf_op jit(solution)/shard_map/pallas_call | solution.py:755
  379.6 79.5 %shard_map.188 = f32[32,6144]{1,0:T(8,128)} custom-call(bf16[1024,256]{1,0:T(8,128)(2,1)} %get-tuple-element.148.l1, bf16[256,4096]{1,0:T(8,128)(2,1)} %fusion.53.r1, bf16[1024,256]{1,0:T(8,128)(2,1)} %get-tuple-element.132.l2, bf16[256,2048]{1,0:T(8,128)(2,1)} %get-tuple-element.52.r2), custom_call_target="tpu_custom_call" | custom-call | tf_op jit(solution)/shard_map/pallas_call | solution.py:451
  459.2 81.6 %shard_map.189 = f32[32,6144]{1,0:T(8,128)} custom-call(bf16[1024,256]{1,0:T(8,128)(2,1)} %get-tuple-element.141.l1, bf16[256,4096]{1,0:T(8,128)(2,1)} %pad_maximum_fusion.r1, bf16[1024,256]{1,0:T(8,128)(2,1)} %bitcast.97, bf16[256,2048]{1,0:T(8,128)(2,1)} %copy-done.8), custom_call_target="tpu_custom_call" | custom-call | tf_op jit(solution)/shard_map/pallas_call | solution.py:451
  541.6 4.2 multiply_subtract_fusion
  (178 shorter events, 58.5 us)
Async XLA Ops:
  7.2 189.1 %all-gather.2.cloned.1.call-start = ((), (), s32[]{:S(2)}) async-start(), calls=%async_computation | async-start | bytes 12976128 | tf_op jit(solution)/shard_map/all_gather | solution.py:1229
  9.7 76.8 %copy-start.10 = (bf16[1,256,1024]{2,1,0:T(8,128)(2,1)S(1)}, bf16[1,256,1024]{2,1,0:T(8,128)(2,1)}, u32[]{:S(2)}) copy-start(bf16[1,256,1024]{2,1,0:T(8,128)(2,1)} %param.12) | copy-start | bytes 1572868
  9.7 77.2 %copy-start.15 = (f32[12568]{0:T(1024)S(1)}, f32[12568]{0:T(1024)}, u32[]{:S(2)}) copy-start(f32[12568]{0:T(1024)} %param.19) | copy-start | bytes 150820
  86.9 7.9 %copy-start.21 = (f32[256]{0:T(256)}, f32[256]{0:T(256)S(1)}, u32[]{:S(2)}) copy-start(f32[256]{0:T(256)S(1)} %add_rsqrt_fusion.1) | copy-start | bytes 3076
  86.9 9.8 %copy-start.16 = (f32[1,24,256]{2,1,0:T(8,128)S(1)}, f32[1,24,256]{2,1,0:T(8,128)}, u32[]{:S(2)}) copy-start(f32[1,24,256]{2,1,0:T(8,128)} %param.14) | copy-start | bytes 73732
  94.8 5.7 %copy-start.26 = (s32[1,2]{1,0:T(1,128)S(1)}, s32[1,2]{1,0:T(1,128)}, u32[]{:S(2)}) copy-start(s32[1,2]{1,0:T(1,128)} %param.15) | copy-start | bytes 28
  101.4 30.2 %copy-start.20 = (s32[256]{0:T(256)}, s32[256]{0:T(256)S(1)}, u32[]{:S(2)}) copy-start(s32[256]{0:T(256)S(1)} %get-tuple-element.181) | copy-start | bytes 3076
  104.0 27.7 %slice-start = ((f32[12568]{0:T(1024)}), f32[1536]{0:T(1024)S(1)}, s32[]{:S(2)}) async-start(f32[12568]{0:T(1024)} %param.19), calls=%async_computation.1 | async-start | bytes 16384 | tf_op jit(solution)/shard_map/slice | solution.py:1146
  106.6 26.0 %copy-start.2 = (f32[24,2,128]{0,2,1:T(8,128)}, f32[24,2,128]{0,2,1:T(8,128)S(1)}, u32[]{:S(2)}) copy-start(f32[24,2,128]{0,2,1:T(8,128)S(1)} %copy.131) | copy-start | bytes 73732
  111.2 22.3 %copy-start.7 = (f32[24,256]{0,1:T(8,128)}, f32[24,256]{0,1:T(8,128)S(1)}, u32[]{:S(2)}) copy-start(f32[24,256]{0,1:T(8,128)S(1)} %get-tuple-element.154) | copy-start | bytes 73732
  116.1 17.4 %copy-start.11 = (bf16[1,256,1024]{2,1,0:T(8,128)(2,1)S(1)}, bf16[1,256,1024]{2,1,0:T(8,128)(2,1)}, u32[]{:S(2)}) copy-start(bf16[1,256,1024]{2,1,0:T(8,128)(2,1)} %param.13) | copy-start | bytes 1572868
  133.8 75.2 %copy-start.1 = (bf16[1,256,1024]{1,2,0:T(8,128)(2,1)}, bf16[1,256,1024]{1,2,0:T(8,128)(2,1)S(1)}, u32[]{:S(2)}) copy-start(bf16[1,256,1024]{1,2,0:T(8,128)(2,1)S(1)} %copy.141) | copy-start | bytes 1572868
  196.3 6.0 %copy-start.12 = (bf16[1,256,1024]{2,1,0:T(8,128)(2,1)S(1)}, bf16[1,256,1024]{2,1,0:T(8,128)(2,1)}, u32[]{:S(2)}) copy-start(bf16[1,256,1024]{2,1,0:T(8,128)(2,1)} %param.13) | copy-start | bytes 1572868
  196.3 7.1 %copy-start.25 = (bf16[1024,6144]{1,0:T(8,128)(2,1)S(1)}, bf16[1024,6144]{1,0:T(8,128)(2,1)}, u32[]{:S(2)}) copy-start(bf16[1024,6144]{1,0:T(8,128)(2,1)} %all-gather.2.cloned.1.call-done) | copy-start | bytes 37748740
  205.5 10.9 %copy-start.8 = (bf16[256,2048]{1,0:T(8,128)(2,1)}, bf16[256,2048]{1,0:T(8,128)(2,1)S(1)}, u32[]{:S(2)}) copy-start(bf16[256,2048]{1,0:T(8,128)(2,1)S(1)} %get-tuple-element.140.r2) | copy-start | bytes 3145732
  304.6 37.0 %copy-start.4 = (f32[256,1792]{1,0:T(8,128)S(1)}, f32[256,1792]{1,0:T(8,128)}, u32[]{:S(2)}) copy-start(f32[256,1792]{1,0:T(8,128)} %get-tuple-element.61) | copy-start | bytes 5505028
  345.4 6.4 %copy-start.22 = (f32[256]{0:T(256)S(1)}, f32[256]{0:T(256)}, u32[]{:S(2)}) copy-start(f32[256]{0:T(256)} %copy-done.21) | copy-start | bytes 3076
  379.6 162.0 %copy-start.6 = (f32[32,12288]{1,0:T(8,128)S(1)}, f32[32,12288]{1,0:T(8,128)}, u32[]{:S(2)}) copy-start(f32[32,12288]{1,0:T(8,128)} %param.18) | copy-start | bytes 4718596
  459.2 81.7 %copy-start.14 = (f32[104,128]{1,0:T(8,128)S(1)}, f32[104,128]{1,0:T(8,128)}, u32[]{:S(2)}) copy-start(f32[104,128]{1,0:T(8,128)} %shard_map.190) | copy-start | bytes 159748
  459.2 81.7 %copy-start.18 = (f32[12568]{0:T(1024)S(1)}, f32[12568]{0:T(1024)}, u32[]{:S(2)}) copy-start(f32[12568]{0:T(1024)} %param.20) | copy-start | bytes 150820
  459.2 81.7 %copy-start.19 = (f32[12568]{0:T(1024)S(1)}, f32[12568]{0:T(1024)}, u32[]{:S(2)}) copy-start(f32[12568]{0:T(1024)} %param.21) | copy-start | bytes 150820
  459.2 82.4 %copy-start = (f32[32,12288]{1,0:T(8,128)S(1)}, f32[32,12288]{1,0:T(8,128)}, u32[]{:S(2)}) copy-start(f32[32,12288]{1,0:T(8,128)} %param.16) | copy-start | bytes 4718596
  459.2 82.4 %copy-start.3 = (f32[32,6144]{1,0:T(8,128)S(1)}, f32[32,6144]{1,0:T(8,128)}, u32[]{:S(2)}) copy-start(f32[32,6144]{1,0:T(8,128)} %shard_map.188) | copy-start | bytes 2359300
  459.2 82.4 %copy-start.5 = (f32[32,12288]{1,0:T(8,128)S(1)}, f32[32,12288]{1,0:T(8,128)}, u32[]{:S(2)}) copy-start(f32[32,12288]{1,0:T(8,128)} %param.17) | copy-start | bytes 4718596
  (5 other events, 9.8 us)
Sparse Core Ops, SparseCore 0:
  11.5 113.5 all-gather.1

commit v2 on v1

--- a/solution.py
+++ b/solution.py
@@ -25,6 +25,8 @@
 MIXIN = 4096
 MIXOUT = 2048
 SMALL_ROWS = 104
+TOKENS = 256
+PIECE = 512
 
 norm_eps = 1e-05
 rope_base = 100000000000.0
@@ -46,9 +48,9 @@
 
 def params(collective=None):
     if collective is None:
-        return pltpu.CompilerParams(vmem_limit_bytes=56 * 2**20)
+        return pltpu.CompilerParams(vmem_limit_bytes=62 * 2**20)
     return pltpu.CompilerParams(
-        collective_id=collective, has_side_effects=True, vmem_limit_bytes=56 * 2**20
+        collective_id=collective, has_side_effects=True, vmem_limit_bytes=62 * 2**20
     )
 
 
@@ -118,7 +120,7 @@
     pl.semaphore_wait(bar, peers)
 
 
-def greet_row(pc):
+def greet_row(pc, across=False):
     bar = pltpu.get_barrier_semaphore()
     n = 4 * pc.Z
 
@@ -128,7 +130,9 @@
             bar, inc=1, device_id=(lax.rem(pc.ctx + d, n), pc.y), device_id_type=MESH
         )
 
-    pl.semaphore_wait(bar, n - 1)
+    if across:
+        pl.semaphore_signal(bar, inc=1, device_id=pc.near("y"), device_id_type=MESH)
+    pl.semaphore_wait(bar, n - 1 + int(across))
 
 
 def rcopy(pc, src, dst, ssem, rsem, d):
@@ -276,189 +280,6 @@
     )(w)
 
 
-def scatter_scratch(planes, rows, columns):
-    h = columns // 2
-    return [
-        pltpu.VMEM((planes, 4, rows, columns), BF),
-        pltpu.VMEM((2, planes, 2, rows, h), BF),
-        pltpu.VMEM((2, planes, rows, h), BF),
-        pltpu.VMEM((2, 2, planes, rows, h), BF),
-        DMA((planes, 4)),
-        DMA((planes, 4)),
-        DMA((2, planes, 2)),
-        DMA((2, planes, 2)),
-        DMA((2, planes)),
-        DMA((2, planes)),
-        DMA((2, 2, planes)),
-        DMA((2, 2, planes)),
-    ]
-
-
-def scatter_steps(pc, make_plane, g_ref, out_ref, scratch):
-    rc, r2, r3, rz, cs, cr, s2, q2, s3, q3, sz, qz = scratch
-    Z, z, x, y, c = pc.Z, pc.z, pc.x, pc.y, pc.c
-    h = g_ref.shape[-1] // 2
-
-    def cols(p):
-        return pl.ds(p * h, h)
-
-    def other(q):
-        return (x if q < 2 else 1 - x), (y if q % 2 == 0 else 1 - y)
-
-    def ccopy(zz, q):
-        xx, yy = other(q)
-        return rcopy(
-            pc, g_ref.at[pc.shard(zz, xx, yy, 1 - c)], rc.at[zz, q], cs.at[zz, q], cr.at[zz, q], "c"
-        )
-
-    def copy2(p, zz, j):
-        q = (1 + 2 * j) if p == 0 else (2 + j)
-        return rcopy(
-            pc,
-            rc.at[zz, q, :, cols(p)],
-            r2.at[p, zz, j],
-            s2.at[p, zz, j],
-            q2.at[p, zz, j],
-            "y" if p == 0 else "x",
-        )
-
-    def copy3(p, zz):
-        q = 2 if p == 0 else 1
-        return rcopy(
-            pc, rc.at[zz, q, :, cols(p)], r3.at[p, zz], s3.at[p, zz], q3.at[p, zz], "x" if p == 0 else "y"
-        )
-
-    def copyz(p, zz, up):
-        u = int(up)
-        return rcopy(
-            pc,
-            rc.at[zz, 0, :, cols(p)],
-            rz.at[p, u, zz],
-            sz.at[p, u, zz],
-            qz.at[p, u, zz],
-            "u" if up else "d",
-        )
-
-    order = (3, 1, 2, 0)
-    for k in range(Z):
-        zz = pc.zord(k)
-        make_plane(zz)
-        for q in order:
-            ccopy(zz, q).start()
-        yield
-    for q in order:
-        for k in range(Z):
-            zz = pc.zord(k)
-            xx, yy = other(q)
-            ccopy(zz, q).wait_recv()
-            add_into(rc.at[zz, q], [g_ref.at[pc.shard(zz, xx, yy, c)], rc.at[zz, q]])
-            if q == 3:
-                copy2(0, zz, 1).start()
-                copy2(1, zz, 1).start()
-            if q == 1:
-                copy2(0, zz, 0).start()
-            if q == 2:
-                copy2(1, zz, 0).start()
-            yield
-    for k in range(Z):
-        zz = pc.zord(k)
-        for p in (0, 1):
-            copy2(p, zz, 1).wait_recv()
-            a = rc.at[zz, 2 if p == 0 else 1, :, cols(p)]
-            add_into(a, [a, r2.at[p, zz, 1]])
-            copy3(p, zz).start()
-        yield
-
-    def own(p, zz):
-        copy2(p, zz, 0).wait_recv()
-        copy3(p, zz).wait_recv()
-        a = rc.at[zz, 0, :, cols(p)]
-        return a, [a, r2.at[p, zz, 0], r3.at[p, zz]]
-
-    def chain(p, zz, up, more):
-        a, parts = own(p, zz)
-        add_into(a, parts)
-
-        @pl.when(more)
-        def _():
-            copyz(p, zz, up).wait_recv()
-            add_into(a, [a, rz.at[p, int(up), zz]])
-
-        copyz(p, zz, up).start()
-
-    for t in range(Z - 1):
-        for p in (0, 1):
-            below, above = t - (Z - 1 - z), Z - 1 - (t - z)
-            pl.when((below >= 0) & (below < z))(lambda: chain(p, below, False, pc.up))
-            pl.when((above > z) & (above < Z))(lambda: chain(p, above, True, pc.down))
-        yield
-    for p in (0, 1):
-        a, parts = own(p, z)
-        o = out_ref.at[:, cols(p)]
-        add_into(o, parts)
-
-        def last(u):
-            copyz(p, z, bool(u)).wait_recv()
-            add_into(o, [o, rz.at[p, u, z]])
-
-        pl.when(pc.up)(lambda: last(0))
-        pl.when(pc.down)(lambda: last(1))
-        yield
-    for zz in range(Z):
-        for q in range(4):
-            ccopy(zz, q).wait_send()
-        for p in (0, 1):
-            for j in (0, 1):
-                copy2(p, zz, j).wait_send()
-            copy3(p, zz).wait_send()
-            pl.when(zz < z)(lambda: copyz(p, zz, False).wait_send())
-            pl.when(zz > z)(lambda: copyz(p, zz, True).wait_send())
-
-
-def plane_maker(planes, pairs, g_ref):
-    rows = g_ref.shape[1]
-    depth = 8 * rows
-
-    def make_plane(zz):
-        base = 0
-        for left, right in pairs:
-            lhs = left[pl.ds(pl.multiple_of(zz * depth, depth), depth), :]
-            width = right.shape[1]
-
-            @pl.loop(0, width // 512)
-            def _(i):
-                at = pl.multiple_of(i * 512, 512)
-                tile = nn(lhs, right[:, pl.ds(at, 512)]).reshape(8, rows, 512).astype(BF)
-                g_ref[pl.ds(zz * 8, 8), :, pl.ds(pl.multiple_of(base + at, 512), 512)] = tile
-
-            base += width
-
-    return make_plane
-
-
-def scatter_kernel(planes, l1, r1, l2, r2, out_ref, g_ref, *scratch):
-    pc = Place(planes)
-    greet(pc)
-    for _ in scatter_steps(
-        pc, plane_maker(planes, ((l1, r1), (l2, r2)), g_ref), g_ref, out_ref, scratch
-    ):
-        pass
-
-
-def scatter_rows(planes, l1, r1, l2, r2, collective):
-    rows = l1.shape[0] // (8 * planes)
-    columns = r1.shape[1] + r2.shape[1]
-    return pl.pallas_call(
-        functools.partial(scatter_kernel, planes),
-        out_shape=jax.ShapeDtypeStruct((rows, columns), F32),
-        in_specs=[VM] * 4,
-        out_specs=VM,
-        scratch_shapes=[pltpu.VMEM((8 * planes, rows, columns), BF)]
-        + scatter_scratch(planes, rows, columns),
-        compiler_params=params(collective),
-    )(l1, r1, l2, r2)
-
-
 def spread_scratch(planes):
     n = 4 * planes
     return [DMA((planes,)), DMA((planes,)), DMA((planes, 2)), DMA((n,)), DMA((n,)), DMA((n,)), DMA((3,))]
@@ -562,21 +383,275 @@
     )(kv, edge, dec)
 
 
-def fold_kernel(planes, g_ref, edge_ref, out_ref, got_ref, rc, rx, rz, acc, *scratch):
-    cs, cr, xs, xr, zs, zr, one = scratch
+def scatter_scratch(planes, rows, widths):
+    columns = sum(widths)
+    w, h = columns // 4, columns // 8 * 3
+    half = 4 * planes * rows
+    return [
+        pltpu.VMEM((planes, 2, 2, rows, columns), BF),
+        pltpu.VMEM((2, planes, 2, rows, h), BF),
+        pltpu.VMEM((2, planes, rows, h), BF),
+        pltpu.VMEM((2, planes + 1, rows, h), BF),
+        pltpu.VMEM((planes + 1, 2, 2, rows, w), BF),
+        pltpu.VMEM((3, rows, w), BF),
+        pltpu.VMEM((len(widths), half, TOKENS), BF),
+        pltpu.VMEM((TOKENS, columns), BF),
+        DMA((len(widths),)),
+        DMA((len(widths),)),
+        DMA((columns // PIECE,)),
+        DMA((columns // PIECE,)),
+        DMA((2, planes, 2)),
+        DMA((2, planes, 2)),
+        DMA((2, planes)),
+        DMA((2, planes)),
+        DMA((3, planes)),
+        DMA((3, planes + 1)),
+        DMA((3,)),
+        DMA((3,)),
+    ]
+
+
+def scatter_steps(pc, pairs, out_ref, scratch):
+    g, r2, r3, rz, rw, rt, la, rb, as_, ar, bs, br, s2, q2, s3, q3, sz, qz, st, qt = scratch
+    Z, z, x, y, c = pc.Z, pc.z, pc.x, pc.y, pc.c
+    rows = g.shape[3]
+    w = g.shape[-1] // 4
+    h = g.shape[-1] // 8 * 3
+    depth = 4 * rows
+
+    def cols(p):
+        return pl.ds(0, w) if p == 2 else pl.ds(w + p * h, h)
+
+    pieces = []
+    base = 0
+    for i, (left, right) in enumerate(pairs):
+        for at in range(0, right.shape[1], PIECE):
+            pieces.append((i, at, base + at))
+        base += right.shape[1]
+
+    def acopy(i):
+        return rcopy(pc, pairs[i][0].at[1 - c], la.at[i], as_.at[i], ar.at[i], "c")
+
+    def bcopy(k):
+        i, at, to = pieces[k]
+        return rcopy(
+            pc, pairs[i][1].at[:, pl.ds(at, PIECE)], rb.at[:, pl.ds(to, PIECE)], bs.at[k], br.at[k], "c"
+        )
+
+    def make(zz, k, first):
+        i, at, to = pieces[k]
+        if first:
+            if at == 0:
+                acopy(i).wait_recv()
+            bcopy(k).wait_recv()
+        here = pl.ds(pl.multiple_of(zz * depth, depth), depth)
+        mine, theirs = pairs[i][0][c, here, :], la[i, here, :]
+        for t in range(0, PIECE, 512):
+            tile = nn(mine, pairs[i][1][:, pl.ds(at + t, 512)]) + nn(theirs, rb[:, pl.ds(to + t, 512)])
+            g[zz, :, :, :, pl.ds(to + t, 512)] = tile.reshape(2, 2, rows, 512).astype(BF)
+
+    def copy2(p, zz, j):
+        xx, yy = (x if j == 0 else 1 - x, 1 - y) if p == 0 else (1 - x, y if j == 0 else 1 - y)
+        return rcopy(
+            pc, g.at[zz, xx, yy, :, cols(p)], r2.at[p, zz, j], s2.at[p, zz, j], q2.at[p, zz, j],
+            "y" if p == 0 else "x",
+        )
+
+    def copy3(p, zz):
+        xx, yy = (1 - x, y) if p == 0 else (x, 1 - y)
+        return rcopy(
+            pc, g.at[zz, xx, yy, :, cols(p)], r3.at[p, zz], s3.at[p, zz], q3.at[p, zz],
+            "x" if p == 0 else "y",
+        )
+
+    def views(p, zz, slot):
+        if p == 2:
+            return g.at[zz, :, :, :, cols(p)], rw.at[slot]
+        return g.at[zz, x, y, :, cols(p)], rz.at[p, slot]
+
+    def sendz(p, zz, up):
+        slot = jnp.where(zz == z + 1, Z, zz) if up else zz
+        src, dst = views(p, zz, slot)
+        return rcopy(pc, src, dst, sz.at[p, zz], qz.at[p, slot], "u" if up else "d")
+
+    def gotz(p, slot):
+        src, dst = views(p, 0, slot)
+        rcopy(pc, src, dst, sz.at[p, 0], qz.at[p, slot], "c").wait_recv()
+
+    def add_plane(zz, slots):
+        for xx in (0, 1):
+            for yy in (0, 1):
+                a = g.at[zz, xx, yy, :, cols(2)]
+                add_into(a, [a] + [rw.at[k, xx, yy] for k in slots])
+
+    def at_time(t, f):
+        below, above = t - (Z - 1 - z), Z - 1 - (t - z)
+        pl.when((below >= 0) & (below < z))(lambda: f(below, False, pc.up))
+        pl.when((above > z) & (above < Z))(lambda: f(above, True, pc.down))
+
+    def chain_first(zz, up, more):
+        @pl.when(more)
+        def _():
+            gotz(2, zz)
+            add_plane(zz, [zz])
+
+        sendz(2, zz, up).start()
+
+    def tail(k):
+        if k < 2:
+            return rcopy(pc, g.at[z, k, 1 - y, :, cols(2)], rt.at[k], st.at[k], qt.at[k], "y")
+        return rcopy(pc, g.at[z, 1 - x, y, :, cols(2)], rt.at[2], st.at[2], qt.at[2], "x")
+
+    for i in range(len(pairs)):
+        acopy(i).start()
+        for k in range(len(pieces)):
+            if pieces[k][0] == i:
+                bcopy(k).start()
+    yield
+    ends = {w + h: 0, w + 2 * h: 1}
+    for k in range(Z + 1):
+        if k < Z:
+            zz = pc.zord(k)
+            for n in range(len(pieces)):
+                make(zz, n, k == 0)
+                end = pieces[n][2] + PIECE
+                if end == w and k == 0 and Z > 1:
+                    at_time(0, chain_first)
+                if end in ends:
+                    copy2(ends[end], zz, 1).start()
+            yield
+        if k > 0:
+            zz = pc.zord(k - 1)
+            for p in (0, 1):
+                copy2(p, zz, 1).wait_recv()
+                a = g.at[(zz,) + ((1 - x, y) if p == 0 else (x, 1 - y)) + (slice(None), cols(p))]
+                add_into(a, [a, r2.at[p, zz, 1]])
+                copy3(p, zz).start()
+            for p in (0, 1):
+                copy2(p, zz, 0).start()
+            if 0 < k - 1 < Z - 1:
+                at_time(k - 1, chain_first)
+            yield
+
+    def own(p, zz):
+        copy2(p, zz, 0).wait_recv()
+        copy3(p, zz).wait_recv()
+        a = g.at[zz, x, y, :, cols(p)]
+        return a, [a, r2.at[p, zz, 0], r3.at[p, zz]]
+
+    def chain(p, zz, up, more):
+        a, parts = own(p, zz)
+
+        @pl.when(more)
+        def _():
+            gotz(p, zz)
+            add_into(a, parts + [rz.at[p, zz]])
+
+        @pl.when(jnp.logical_not(more))
+        def _():
+            add_into(a, parts)
+
+        sendz(p, zz, up).start()
+
+    def gather_plane(slot):
+        gotz(2, slot)
+        add_plane(z, [slot])
+
+    pl.when(pc.up)(lambda: gather_plane(z))
+    pl.when(pc.down)(lambda: gather_plane(Z))
+    for k in (0, 1):
+        tail(k).start()
+    yield
+    for t in range(Z - 1):
+        for p in (0, 1):
+            at_time(t, functools.partial(chain, p))
+        if t == 0:
+            for k in (0, 1):
+                tail(k).wait_recv()
+                a = g.at[z, k, y, :, cols(2)]
+                add_into(a, [a, rt.at[k]])
+            tail(2).start()
+        yield
+    tail(2).wait_recv()
+    add_into(out_ref.at[:, cols(2)], [g.at[z, x, y, :, cols(2)], rt.at[2]])
+    for p in (0, 1):
+        a, parts = own(p, z)
+        o = out_ref.at[:, cols(p)]
+        add_into(o, parts)
+
+        def last(slot):
+            gotz(p, slot)
+            add_into(o, [o, rz.at[p, slot]])
+
+        pl.when(pc.up)(lambda: last(z))
+        pl.when(pc.down)(lambda: last(Z))
+        yield
+    for i in range(len(pairs)):
+        acopy(i).wait_send()
+    for k in range(len(pieces)):
+        bcopy(k).wait_send()
+    for k in range(3):
+        tail(k).wait_send()
+    for zz in range(Z):
+        for p in (0, 1):
+            for j in (0, 1):
+                copy2(p, zz, j).wait_send()
+            copy3(p, zz).wait_send()
+        for p in (0, 1, 2):
+            pl.when(zz < z)(lambda: sendz(p, zz, False).wait_send())
+            pl.when(zz > z)(lambda: sendz(p, zz, True).wait_send())
+
+
+def scatter_kernel(planes, count, *refs):
     pc = Place(planes)
+    greet(pc)
+    pairs = tuple(zip(refs[:count], refs[count : 2 * count]))
+    for _ in scatter_steps(pc, pairs, refs[2 * count], refs[2 * count + 1 :]):
+        pass
+
+
+def scatter_rows(planes, lefts, rights, collective):
+    rows = lefts[0].shape[1] // (4 * planes)
+    widths = [r.shape[1] for r in rights]
+    return pl.pallas_call(
+        functools.partial(scatter_kernel, planes, len(lefts)),
+        out_shape=jax.ShapeDtypeStruct((rows, sum(widths)), F32),
+        in_specs=[VM] * (2 * len(lefts)),
+        out_specs=VM,
+        scratch_shapes=scatter_scratch(planes, rows, widths),
+        compiler_params=params(collective),
+    )(*lefts, *rights)
+
+
+def by_core(rows, planes):
+    tokens = rows.shape[0]
+    each = D // (8 * planes)
+    cut = rows.T.reshape(2 * planes, 2, 2 * each, tokens)
+    return cut.transpose(1, 0, 2, 3).reshape(2, D // 2, tokens)
+
+
+def fold_scratch(planes, rows, columns):
+    return [
+        pltpu.VMEM((planes, 2, rows, columns), BF),
+        pltpu.VMEM((planes, rows, columns), BF),
+        pltpu.VMEM((planes, rows, columns), BF),
+        pltpu.VMEM((planes, 2, rows, columns), BF),
+        DMA((planes, 2)),
+        DMA((planes, 2)),
+        DMA((planes,)),
+        DMA((planes,)),
+        DMA((planes,)),
+        DMA((planes,)),
+    ]
+
+
+def fold_steps(pc, block, out_ref, scratch):
+    rc, rx, rz, acc, cs, cr, xs, xr, zs, zr = scratch
     Z, z, x, c = pc.Z, pc.z, pc.x, pc.c
-    n = 4 * Z
-    me = pc.ctx
-    greet_row(pc)
-    edge = rcopy(pc, edge_ref, got_ref, one.at[0], one.at[1], (lax.rem(me + n - 1, n), pc.y))
-    pl.when(me > 0)(lambda: edge.start())
 
     def ccopy(zz, q):
         xx = x if q == 0 else 1 - x
-        return rcopy(
-            pc, g_ref.at[pc.spot(zz, xx, 1 - c)], rc.at[zz, q], cs.at[zz, q], cr.at[zz, q], "c"
-        )
+        return rcopy(pc, block(pc.spot(zz, xx, 1 - c)), rc.at[zz, q], cs.at[zz, q], cr.at[zz, q], "c")
 
     def xcopy(zz):
         return rcopy(pc, acc.at[zz, 1], rx.at[zz], xs.at[zz], xr.at[zz], "x")
@@ -594,39 +669,30 @@
 
     def b(zz):
         ccopy(zz, 1).wait_recv()
-        add_into(acc.at[zz, 1], [g_ref.at[pc.spot(zz, 1 - x, c)], rc.at[zz, 1]], 128)
+        add_into(acc.at[zz, 1], [block(pc.spot(zz, 1 - x, c)), rc.at[zz, 1]], 128)
         xcopy(zz).start()
 
     def m(zz):
         ccopy(zz, 0).wait_recv()
-        add_into(acc.at[zz, 0], [g_ref.at[pc.spot(zz, x, c)], rc.at[zz, 0]], 128)
+        add_into(acc.at[zz, 0], [block(pc.spot(zz, x, c)), rc.at[zz, 0]], 128)
 
     def e(zz):
         xcopy(zz).wait_recv()
+
+        def finish(parts):
+            @pl.when(zz < z)
+            def _():
+                add_into(acc.at[zz, 0], parts, 128)
+                zcopy(zz).start()
+
+            pl.when(zz == z)(lambda: add_into(out_ref, parts, 128))
 
         @pl.when(pc.up)
         def _():
             zcopy(zz).wait_recv()
-
-            @pl.when(zz < z)
-            def _():
-                add_into(acc.at[zz, 0], [acc.at[zz, 0], rx.at[zz], rz.at[zz]], 128)
-                zcopy(zz).start()
-
-            @pl.when(zz == z)
-            def _():
-                add_into(out_ref, [acc.at[zz, 0], rx.at[zz], rz.at[zz]], 128)
-
-        @pl.when(jnp.logical_not(pc.up))
-        def _():
-            @pl.when(zz < z)
-            def _():
-                add_into(acc.at[zz, 0], [acc.at[zz, 0], rx.at[zz]], 128)
-                zcopy(zz).start()
-
-            @pl.when(zz == z)
-            def _():
-                add_into(out_ref, [acc.at[zz, 0], rx.at[zz]], 128)
+            finish([acc.at[zz, 0], rx.at[zz], rz.at[zz]])
+
+        pl.when(jnp.logical_not(pc.up))(lambda: finish([acc.at[zz, 0], rx.at[zz]]))
 
     def w(zz):
         ccopy(zz, 1).wait_send()
@@ -634,48 +700,22 @@
         xcopy(zz).wait_send()
         pl.when(zz < z)(lambda: zcopy(zz).wait_send())
 
-    for f in (a, b, m, e, w):
+    for f in (a, b, m, e):
         each(f)
-    pl.when(me > 0)(lambda: edge.wait_send())
-    pl.when(me < n - 1)(lambda: edge.wait_recv())
-
-    @pl.when(me == n - 1)
-    def _():
-        got_ref[...] = jnp.zeros_like(got_ref)
-
-
-def fold(planes, grads, edge, collective):
-    n, rows, columns = grads.shape
-    return pl.pallas_call(
-        functools.partial(fold_kernel, planes),
-        out_shape=(
-            jax.ShapeDtypeStruct((rows, columns), F32),
-            jax.ShapeDtypeStruct(edge.shape, edge.dtype),
-        ),
-        in_specs=[VM] * 2,
-        out_specs=(VM,) * 2,
-        scratch_shapes=[
-            pltpu.VMEM((planes, 2, rows, columns), BF),
-            pltpu.VMEM((planes, rows, columns), BF),
-            pltpu.VMEM((planes, rows, columns), BF),
-            pltpu.VMEM((planes, 2, rows, columns), BF),
-            DMA((planes, 2)),
-            DMA((planes, 2)),
-            DMA((planes,)),
-            DMA((planes,)),
-            DMA((planes,)),
-            DMA((planes,)),
-            DMA((2,)),
-        ],
-        compiler_params=params(collective),
-    )(grads, edge)
-
-
-def relay_kernel(planes, reverse, s_ref, dec_ref, out_ref, got, part, ss, sr, bs, br):
-    pc = Place(planes)
+        yield
+    each(w)
+
+
+def relay_scratch(planes):
     n = 4 * planes
+    piece = pltpu.VMEM((n, NS // n, INNER), BF)
+    return [piece, piece, DMA((n,)), DMA((n,)), DMA((n,)), DMA((n,))]
+
+
+def relay_steps(pc, reverse, s_ref, dec_ref, out_ref, scratch):
+    got, part, ss, sr, bs, br = scratch
+    n = 4 * pc.Z
     me = pc.ctx
-    greet_row(pc)
 
     def to(d):
         return lax.rem(me + d, n)
@@ -688,6 +728,7 @@
 
     pl.loop(1, n)(lambda d: there(d).start())
     got[me] = s_ref[me]
+    yield
     pl.loop(1, n)(lambda d: there(d).wait_recv())
     total = jnp.zeros(got.shape[1:], F32)
     for k in range(n):
@@ -696,11 +737,21 @@
         total = total * dec_ref[pl.ds(j, 1), :] + got[j].astype(F32)
     pl.loop(1, n)(lambda d: back(d).start())
     out_ref[me] = part[me]
+    yield
+    pl.loop(1, n)(lambda d: back(d).wait_recv())
+    yield
 
     @pl.loop(1, n)
     def _(d):
         there(d).wait_send()
-        back(d).wait()
+        back(d).wait_send()
+
+
+def relay_kernel(planes, reverse, s_ref, dec_ref, out_ref, *scratch):
+    pc = Place(planes)
+    greet_row(pc)
+    for _ in relay_steps(pc, reverse, s_ref, dec_ref, out_ref, scratch):
+        pass
 
 
 def relay(planes, reverse, state, decays, collective):
@@ -711,38 +762,43 @@
         out_shape=jax.ShapeDtypeStruct(piece.shape, BF),
         in_specs=[VM] * 2,
         out_specs=VM,
-        scratch_shapes=[pltpu.VMEM(piece.shape, BF), pltpu.VMEM(piece.shape, BF)]
-        + [DMA((n,))] * 4,
+        scratch_shapes=relay_scratch(planes),
         compiler_params=params(collective),
     )(piece, decays)
     return out.reshape(NS, INNER)
 
 
-def total_kernel(planes, a_ref, out_ref, rx, rz, ss, sr, zs, zr):
-    pc = Place(planes)
+def total_scratch(planes):
+    shape = (SMALL_ROWS, 128)
+    return [
+        pltpu.VMEM((6,) + shape, F32),
+        pltpu.VMEM((planes,) + shape, F32),
+        DMA((3,)),
+        DMA((3,)),
+        DMA((planes,)),
+        DMA((planes,)),
+    ]
+
+
+def plane_peers(pc):
+    return [pc.dev(lax.rem(pc.z + d, pc.Z), pc.x, pc.y, pc.c) for d in range(1, pc.Z)]
+
+
+def total_steps(pc, out_ref, scratch):
+    rx, rz, ss, sr, zs, zr = scratch
     Z, z = pc.Z, pc.z
-    bar = pltpu.get_barrier_semaphore()
-
-    def plane(d):
-        return pc.dev(lax.rem(z + d, Z), pc.x, pc.y, pc.c)
-
-    for d in "cxy":
-        pl.semaphore_signal(bar, inc=1, device_id=pc.near(d), device_id_type=MESH)
-    for d in range(1, Z):
-        pl.semaphore_signal(bar, inc=1, device_id=plane(d), device_id_type=MESH)
-    pl.semaphore_wait(bar, 2 + Z)
-    out_ref[...] = a_ref[...]
     for i, d in enumerate("cxy"):
-        src = rx.at[2 * i]
-        src[...] = out_ref[...]
-        cp = rcopy(pc, src, rx.at[2 * i + 1], ss.at[i], sr.at[i], d)
+        rx[2 * i] = out_ref[...]
+        cp = rcopy(pc, rx.at[2 * i], rx.at[2 * i + 1], ss.at[i], sr.at[i], d)
         cp.start()
+        yield
         cp.wait()
         out_ref[...] = out_ref[...] + rx[2 * i + 1]
     rz[z] = out_ref[...]
-    copies = [rcopy(pc, rz.at[z], rz.at[z], zs.at[d], zr.at[d], plane(d)) for d in range(1, Z)]
+    copies = [rcopy(pc, rz.at[z], rz.at[z], zs.at[d], zr.at[d], to) for d, to in enumerate(plane_peers(pc))]
     for cp in copies:
         cp.start()
+    yield
     for cp in copies:
         cp.wait()
     total = rz[0]
@@ -751,27 +807,29 @@
     out_ref[...] = total
 
 
-def total_small(planes, a, collective):
-    return pl.pallas_call(
-        functools.partial(total_kernel, planes),
-        out_shape=jax.ShapeDtypeStruct(a.shape, F32),
-        in_specs=[VM],
-        out_specs=VM,
-        scratch_shapes=[
-            pltpu.VMEM((6,) + a.shape, F32),
-            pltpu.VMEM((planes,) + a.shape, F32),
-            DMA((3,)),
-            DMA((3,)),
-            DMA((planes,)),
-            DMA((planes,)),
-        ],
-        compiler_params=params(collective),
-    )(a)
-
-
 def visible(start, block, pos_ref):
     kpos = start + lax.broadcasted_iota(jnp.int32, (block, pos_ref.shape[1]), 0)
     return (kpos <= pos_ref[0:1, :]) & (kpos >= pos_ref[1:2, :])
+
+
+def split_heads(src, dst, scale=None):
+    rows = src.shape[0]
+    for h in range(QUERY_HEADS):
+        v = src[:, pl.ds(h * HEAD_WIDTH, HEAD_WIDTH)]
+        dst[pl.ds(h * rows, rows), :] = v if scale is None else v * scale
+
+
+def swap_halves(v):
+    width = v.shape[1]
+    lane = lax.broadcasted_iota(jnp.int32, v.shape, 1)
+    low = lax.rem(lane, HEAD_WIDTH) < HEAD_WIDTH // 2
+    ahead = pltpu.roll(v, width - HEAD_WIDTH // 2, 1)
+    behind = pltpu.roll(v, HEAD_WIDTH // 2, 1)
+    return jnp.where(low, ahead, behind)
+
+
+def rotate(v, cos_ref, sin_ref):
+    return v * cos_ref[...] + swap_halves(v) * sin_ref[...]
 
 
 def attend_kernel(block, span_ref, q_ref, kv_ref, pos_ref, o_ref, lse_ref, m_ref, l_ref, acc_ref):
@@ -782,22 +840,31 @@
 
     @pl.loop(span_ref[0], span_ref[1])
     def _(j):
-        start = pl.multiple_of(j * block, block)
-        ok = visible(start, block, pos_ref)
-        for h in range(QUERY_HEADS):
-            g = h // (QUERY_HEADS // KEY_VALUE_HEADS)
-            keys = kv_ref[pl.ds(start, block), pl.ds(g * HEAD_WIDTH, HEAD_WIDTH)]
-            vals = kv_ref[pl.ds(start, block), pl.ds(KEY_WIDTH + g * HEAD_WIDTH, HEAD_WIDTH)]
-            s = jnp.where(ok, nt(keys, q_ref[pl.ds(h * rows, rows), :]), large_negative)
-            m0 = m_ref[h : h + 1, :]
-            m1 = jnp.maximum(m0, jnp.max(s, axis=0, keepdims=True))
-            p = jnp.where(ok, jnp.exp(s - m1), 0.0)
-            a = jnp.exp(m0 - m1)
-            l_ref[h : h + 1, :] = l_ref[h : h + 1, :] * a + jnp.sum(p, axis=0, keepdims=True)
-            m_ref[h : h + 1, :] = m1
-            r = pl.ds(h * HEAD_WIDTH, HEAD_WIDTH)
-            acc_ref[r, :] = acc_ref[r, :] * a + tn(vals, p.astype(BF))
-
+        attend_block(j, block, q_ref, kv_ref, pos_ref, m_ref, l_ref, acc_ref)
+
+    attend_end(o_ref, lse_ref, m_ref, l_ref, acc_ref)
+
+
+def attend_block(j, block, q_ref, kv_ref, pos_ref, m_ref, l_ref, acc_ref):
+    rows = pos_ref.shape[1]
+    start = pl.multiple_of(j * block, block)
+    ok = visible(start, block, pos_ref)
+    for h in range(QUERY_HEADS):
+        g = h // (QUERY_HEADS // KEY_VALUE_HEADS)
+        keys = kv_ref[pl.ds(start, block), pl.ds(g * HEAD_WIDTH, HEAD_WIDTH)]
+        vals = kv_ref[pl.ds(start, block), pl.ds(KEY_WIDTH + g * HEAD_WIDTH, HEAD_WIDTH)]
+        s = jnp.where(ok, nt(keys, q_ref[pl.ds(h * rows, rows), :]), large_negative)
+        m0 = m_ref[h : h + 1, :]
+        m1 = jnp.maximum(m0, jnp.max(s, axis=0, keepdims=True))
+        p = jnp.where(ok, jnp.exp(s - m1), 0.0)
+        a = jnp.exp(m0 - m1)
+        l_ref[h : h + 1, :] = l_ref[h : h + 1, :] * a + jnp.sum(p, axis=0, keepdims=True)
+        m_ref[h : h + 1, :] = m1
+        r = pl.ds(h * HEAD_WIDTH, HEAD_WIDTH)
+        acc_ref[r, :] = acc_ref[r, :] * a + tn(vals, p.astype(BF))
+
+
+def attend_end(o_ref, lse_ref, m_ref, l_ref, acc_ref):
     lse_ref[...] = m_ref[...] + jnp.log(l_ref[...])
     inv = 1.0 / l_ref[...]
     for h in range(QUERY_HEADS):
@@ -825,58 +892,29 @@
     )(span, q, kv, pos)
 
 
-def attend_back_kernel(
-    block, span_ref, q_ref, do_ref, kv_ref, pos_ref, lse_ref, dl_ref, dq_ref, dkv_ref, acc_ref
-):
+def attend_back_block(j, block, q_ref, do_ref, kv_ref, pos_ref, lse_ref, dl_ref, dkv_ref, acc_ref):
     rows = pos_ref.shape[1]
-    acc_ref[...] = jnp.zeros_like(acc_ref)
-
-    def blank(j):
-        dkv_ref[pl.ds(pl.multiple_of(j * block, block), block), :] = jnp.zeros((block, 256), BF)
-
-    pl.loop(0, span_ref[0])(blank)
-    pl.loop(span_ref[1], kv_ref.shape[0] // block)(blank)
-
-    @pl.loop(span_ref[0], span_ref[1])
-    def _(j):
-        start = pl.multiple_of(j * block, block)
-        ok = visible(start, block, pos_ref)
-        at = pl.ds(start, block)
-        dks, dvs = [], []
-        for g in range(KEY_VALUE_HEADS):
-            keys = kv_ref[at, pl.ds(g * HEAD_WIDTH, HEAD_WIDTH)]
-            vals = kv_ref[at, pl.ds(KEY_WIDTH + g * HEAD_WIDTH, HEAD_WIDTH)]
-            dk = dv = None
-            for h in range(4 * g, 4 * g + 4):
-                q = q_ref[pl.ds(h * rows, rows), :]
-                do = do_ref[pl.ds(h * rows, rows), :]
-                p = jnp.where(ok, jnp.exp(nt(keys, q) - lse_ref[h : h + 1, :]), 0.0)
-                ds = (p * (nt(vals, do) - dl_ref[h : h + 1, :])).astype(BF)
-                r = pl.ds(h * HEAD_WIDTH, HEAD_WIDTH)
-                acc_ref[r, :] += tn(keys, ds)
-                a, b = nn(ds, q), nn(p.astype(BF), do)
-                dk = a if dk is None else dk + a
-                dv = b if dv is None else dv + b
-            dks.append(dk)
-            dvs.append(dv)
-        dkv_ref[at, :] = jnp.concatenate(dks + dvs, axis=1).astype(BF)
-
-    dq_ref[...] = acc_ref[...].T * (HEAD_WIDTH**-0.5)
-
-
-def attend_back(span, q, do, kv, pos, lse, delta, block):
-    rows = pos.shape[1]
-    return pl.pallas_call(
-        functools.partial(attend_back_kernel, block),
-        out_shape=(
-            jax.ShapeDtypeStruct((rows, QUERY_WIDTH), F32),
-            jax.ShapeDtypeStruct((kv.shape[0], 2 * KEY_WIDTH), BF),
-        ),
-        in_specs=[SM] + [VM] * 6,
-        out_specs=(VM, VM),
-        scratch_shapes=[pltpu.VMEM((QUERY_WIDTH, rows), F32)],
-        compiler_params=params(),
-    )(span, q, do, kv, pos, lse, delta)
+    start = pl.multiple_of(j * block, block)
+    ok = visible(start, block, pos_ref)
+    at = pl.ds(start, block)
+    dks, dvs = [], []
+    for g in range(KEY_VALUE_HEADS):
+        keys = kv_ref[at, pl.ds(g * HEAD_WIDTH, HEAD_WIDTH)]
+        vals = kv_ref[at, pl.ds(KEY_WIDTH + g * HEAD_WIDTH, HEAD_WIDTH)]
+        dk = dv = None
+        for h in range(4 * g, 4 * g + 4):
+            q = q_ref[pl.ds(h * rows, rows), :]
+            do = do_ref[pl.ds(h * rows, rows), :]
+            p = jnp.where(ok, jnp.exp(nt(keys, q) - lse_ref[h : h + 1, :]), 0.0)
+            ds = (p * (nt(vals, do) - dl_ref[h : h + 1, :])).astype(BF)
+            r = pl.ds(h * HEAD_WIDTH, HEAD_WIDTH)
+            acc_ref[r, :] += tn(keys, ds)
+            a, b = nn(ds, q), nn(p.astype(BF), do)
+            dk = a if dk is None else dk + a
+            dv = b if dv is None else dv + b
+        dks.append(dk)
+        dvs.append(dv)
+    dkv_ref[at, :] = jnp.concatenate(dks + dvs, axis=1).astype(BF)
 
 
 def two(left, right, lanes):
@@ -896,7 +934,7 @@
         acc = jnp.broadcast_to(cb[:, sl], (rows, 256))
         for j in range(CONV):
             acc = acc + cw[j : j + 1, sl] * (xe[pl.ds(5 + j, rows), sl] * mk[:, j : j + 1])
-        pre[:, sl] = acc
+        pre[:, sl] = acc.astype(BF)
         act = acc * jax.nn.sigmoid(acc)
         xo[:, sl] = act.astype(BF)
         if i < INNER // 256:
@@ -925,7 +963,7 @@
     return pl.pallas_call(
         mixer_kernel,
         out_shape=(
-            jax.ShapeDtypeStruct((rows, XBC), F32),
+            jax.ShapeDtypeStruct((rows, XBC), BF),
             jax.ShapeDtypeStruct((rows, XBC), BF),
             jax.ShapeDtypeStruct((rows, INNER), F32),
             jax.ShapeDtypeStruct((NS, INNER), BF),
@@ -943,14 +981,14 @@
     return (lane // MP == head).astype(F32)
 
 
+def exact(a, b, dims):
+    return lax.dot_general(
+        a, b, (dims, ((), ())), precision=lax.Precision.HIGHEST, preferred_element_type=F32
+    )
+
+
 def wide(columns, spread_mat):
-    return lax.dot_general(
-        columns,
-        spread_mat,
-        (((1,), (0,)), ((), ())),
-        precision=lax.Precision.HIGHEST,
-        preferred_element_type=F32,
-    )
+    return exact(columns, spread_mat, ((1,), (0,)))
 
 
 def gate_kernel(mix, xo, state, din_t, gate, gain, att, mixed, branch):
@@ -962,7 +1000,7 @@
         r = pl.ds(pl.multiple_of(i * 64, 64), 64)
         carried = nn(xo[r, pl.ds(INNER + NS, NS)], state[...])
         m = mix[r, :] + carried * wide(din_t[r, :], spread_mat)
-        mixed[r, :] = m
+        mixed[r, :] = m.astype(BF)
         gv = gate[r, :]
         gated = m * (gv * jax.nn.sigmoid(gv))
         factor = lax.rsqrt(jnp.mean(gated * gated, axis=1, keepdims=True) + norm_eps)
@@ -975,7 +1013,7 @@
     return pl.pallas_call(
         gate_kernel,
         out_shape=(
-            jax.ShapeDtypeStruct((rows, INNER), F32),
+            jax.ShapeDtypeStruct((rows, INNER), BF),
             jax.ShapeDtypeStruct((rows, MIXOUT), BF),
         ),
         in_specs=[VM] * 7,
@@ -984,54 +1022,31 @@
     )(mix, xo, state, din_t, gate, gain, att)
 
 
-def gate_back_kernel(grad, mixed, gate, gain, din_t, xo, state, dm, dgate, dgain, dstate, dc, dinc):
-    rows = mixed.shape[0]
-    spread_mat = spread_heads()
-    dgain[...] = jnp.zeros_like(dgain)
-
-    @pl.loop(0, rows // 64)
-    def _(i):
-        r = pl.ds(pl.multiple_of(i * 64, 64), 64)
-        m, gv, gr = mixed[r, :], gate[r, :], grad[r, :]
-        sig = jax.nn.sigmoid(gv)
-        sil = gv * sig
-        gated = m * sil
-        factor = lax.rsqrt(jnp.mean(gated * gated, axis=1, keepdims=True) + norm_eps)
-        w = gr * gain[...]
-        dg = factor * (w - gated * factor * factor * jnp.mean(w * gated, axis=1, keepdims=True))
-        dgain[...] += jnp.sum(gr * gated * factor, axis=0, keepdims=True)
-        dgate[r, :] = (dg * m * (sig * (1.0 + gv * (1.0 - sig)))).astype(BF)
-        d = dg * sil
-        dm[r, :] = d.astype(BF)
-        dinc[r, :] = (d * wide(din_t[r, :], spread_mat)).astype(BF)
-
-    dstate[...] = tn(xo[:, pl.ds(INNER + NS, NS)], dinc[...]).astype(BF)
-    dc[...] = nt(dinc[...], state[...])
-
-
-def gate_back(grad, mixed, gate, gain, din_t, xo, state):
-    rows = mixed.shape[0]
-    return pl.pallas_call(
-        gate_back_kernel,
-        out_shape=(
-            jax.ShapeDtypeStruct((rows, INNER), BF),
-            jax.ShapeDtypeStruct((rows, INNER), BF),
-            jax.ShapeDtypeStruct((1, INNER), F32),
-            jax.ShapeDtypeStruct((NS, INNER), BF),
-            jax.ShapeDtypeStruct((rows, NS), F32),
-        ),
-        in_specs=[VM] * 7,
-        out_specs=(VM,) * 5,
-        scratch_shapes=[pltpu.VMEM((rows, INNER), BF)],
-        compiler_params=params(),
-    )(grad, mixed, gate, gain, din_t, xo, state)
-
-
-def mixer_back_kernel(
-    xe, mk, cw, cum_t, cum, dt_t, we_t, skip, doc_c, doc_r, pre, xo, dm, dc_in, ds,
-    dpre, dcw, dskip, xw, bias,
+GATE_AT = QUERY_WIDTH + 2 * KEY_WIDTH
+XBC_AT = GATE_AT + INNER
+
+
+def gate_back_rows(i, grad, mixed, gate, gain, din_t, spread_mat, dm, dproj, dgain, dinc):
+    r = pl.ds(pl.multiple_of(i * 64, 64), 64)
+    m, gv, gr = mixed[r, :].astype(F32), gate[r, :], grad[r, pl.ds(QUERY_WIDTH, INNER)]
+    sig = jax.nn.sigmoid(gv)
+    sil = gv * sig
+    gated = m * sil
+    factor = lax.rsqrt(jnp.mean(gated * gated, axis=1, keepdims=True) + norm_eps)
+    w = gr * gain[...]
+    dg = factor * (w - gated * factor * factor * jnp.mean(w * gated, axis=1, keepdims=True))
+    dgain[...] += jnp.sum(gr * gated * factor, axis=0, keepdims=True)
+    dproj[r, pl.ds(GATE_AT, INNER)] = (dg * m * (sig * (1.0 + gv * (1.0 - sig)))).astype(BF)
+    d = dg * sil
+    dm[r, :] = d.astype(BF)
+    dinc[r, :] = (d * wide(din_t[r, :], spread_mat)).astype(BF)
+
+
+def mixer_back_steps(
+    xe, mk, cw, cum_t, cum, dt_t, we_t, skip, doc_c, doc_r, pre, xo, dm, dc_in, ds, dpre, dcw, dskip, xw, bias
 ):
     rows = pre.shape[0]
+    here = pl.ds(0, rows)
     b_rows, c_rows = xo[:, pl.ds(INNER, NS)], xo[:, pl.ds(INNER + NS, NS)]
     cross = nt(b_rows, c_rows)
     s_at = lax.broadcasted_iota(jnp.int32, (rows, rows), 0)
@@ -1040,7 +1055,7 @@
     lanes = lax.broadcasted_iota(jnp.int32, (rows, 2 * MP), 1)
 
     def slope(sl):
-        v = pre[:, sl]
+        v = pre[:, sl].astype(F32)
         sig = jax.nn.sigmoid(v)
         return sig * (1.0 + v * (1.0 - sig))
 
@@ -1062,14 +1077,17 @@
         dxd = two(outs[0], outs[1], lanes) + we2 * nn(b_rows, ds[:, sl])
         gf = g.astype(F32)
         dskip[:, sl] = jnp.sum(gf * xv, axis=0, keepdims=True)
-        dpre[:, sl] = (dxd * dt2 + skip[:, sl] * gf) * slope(sl)
+        dpre[here, sl] = (dxd * dt2 + skip[:, sl] * gf) * slope(sl)
+        if p % 4 == 3:
+            yield
     db16 = dcross.astype(BF)
     slb, slc = pl.ds(INNER, NS), pl.ds(INNER + NS, NS)
-    dpre[:, slb] = (nn(db16, c_rows) + nt(xw[...], ds[...])) * slope(slb)
-    dpre[:, slc] = (tn(db16, b_rows) + dc_in[...]) * slope(slc)
+    dpre[here, slb] = (nn(db16, c_rows) + nt(xw[...], ds[...])) * slope(slb)
+    dpre[here, slc] = (tn(db16, b_rows) + dc_in[...]) * slope(slc)
+    yield
     for i in range(XBC // 256):
         sl = pl.ds(i * 256, 256)
-        d = dpre[:, sl]
+        d = dpre[here, sl]
         for j in range(CONV):
             dcw[j : j + 1, sl] = jnp.sum(
                 d * (xe[pl.ds(5 + j, rows), sl] * mk[:, j : j + 1]), axis=0, keepdims=True
@@ -1077,20 +1095,230 @@
         dcw[CONV : CONV + 1, sl] = jnp.sum(d, axis=0, keepdims=True)
 
 
-def mixer_back(xe, mk, cw, cum_t, cum, dt_t, we_t, skip, doc_c, doc_r, pre, xo, dm, dc_in, ds):
-    rows = mk.shape[0]
+def back_kernel(planes, count, block, *refs):
+    lefts, rights, refs = refs[:count], refs[count : 2 * count], refs[2 * count :]
+    if count:
+        branch = rights[2]
+    else:
+        branch, refs = refs[0], refs[1:]
+    (
+        grad, mixed, gate, gain, din_t, xo, state, q_in, kv, pos, lse, cos_w, sin_w, decays,
+        xe, mk, mk_next, cw, cum_t, cum, dt_t, we_t, skip, doc_c, doc_r, pre,
+    ) = refs[:26]
+    refs = refs[26:]
+    if count:
+        scattered, refs = refs[0], refs[1:]
+    dproj, dgain, dcw, dskip = refs[:4]
+    (
+        dm, dinc, dc, dstate, dsnew, flat, qh, doh, dl, acc, dkv, dkv_own, dpre, edge, bias, esem
+    ) = refs[4:20]
+    refs = refs[20:]
+    relay_refs, refs = refs[:6], refs[6:]
+    fold_refs, refs = refs[:10], refs[10:]
+    pc = Place(planes)
+    n = 4 * planes
+    rows = mixed.shape[0]
+    greet_row(pc, count > 0)
+    side = (
+        scatter_steps(pc, tuple(zip(lefts, rights)), scattered, refs) if count else iter(())
+    )
+
+    def pump():
+        next(side, None)
+
+    pump()
+    spread_mat = spread_heads()
+    dgain[...] = jnp.zeros_like(dgain)
+    pl.loop(0, rows // 64)(
+        lambda i: gate_back_rows(i, grad, mixed, gate, gain, din_t, spread_mat, dm, dproj, dgain, dinc)
+    )
+    ds0 = tn(xo[:, pl.ds(INNER + NS, NS)], dinc[...]).astype(BF)
+    dc[...] = nt(dinc[...], state[...])
+    dstate[...] = ds0.reshape(dstate.shape)
+    states = relay_steps(pc, True, dstate, decays, dsnew, relay_refs)
+    next(states)
+    for _ in range(planes):
+        pump()
+    split_heads(q_in, qh, jnp.asarray(HEAD_WIDTH**-0.5, BF))
+    go = grad[:, pl.ds(0, QUERY_WIDTH)].astype(BF)
+    head = lax.broadcasted_iota(jnp.int32, (QUERY_HEADS, QUERY_WIDTH), 0)
+    lane = lax.broadcasted_iota(jnp.int32, (QUERY_HEADS, QUERY_WIDTH), 1)
+    for h in range(QUERY_HEADS):
+        doh[pl.ds(h * rows, rows), :] = go[:, h * HEAD_WIDTH : (h + 1) * HEAD_WIDTH]
+    dl[...] = exact(
+        (lane // HEAD_WIDTH == head).astype(F32),
+        go.astype(F32) * branch[:, pl.ds(0, QUERY_WIDTH)].astype(F32),
+        ((1,), (1,)),
+    )
+    acc[...] = jnp.zeros_like(acc)
+    total = kv.shape[0] // block
+    seen = (pc.ctx * rows + rows + block - 1) // block
+    parts = 4
+    each = total // parts
+
+    @pl.loop(seen, (pc.z + 1) * 4 * rows // block)
+    def _(j):
+        dkv[pl.ds(pl.multiple_of(j * block, block), block), :] = jnp.zeros((block, 2 * KEY_WIDTH), BF)
+
+    for k in range(parts):
+        lo = each * k
+        pl.loop(jnp.minimum(lo, seen), jnp.minimum(lo + each, seen))(
+            lambda j: attend_back_block(j, block, qh, doh, kv, pos, lse, dl, dkv, acc)
+        )
+        pump()
+        if k == 1:
+            next(states)
+    folds = fold_steps(
+        pc, lambda s: dkv.at[pl.ds(pl.multiple_of(s * rows, rows), rows), :], dkv_own, fold_refs
+    )
+    next(folds)
+    for t in range(QUERY_WIDTH // 128):
+        dq = acc[pl.ds(t * 128, 128), :].T * (HEAD_WIDTH**-0.5)
+        dproj[:, pl.ds(t * 128, 128)] = rotate(dq, cos_w, sin_w).astype(BF)
+    next(states)
+    flat[...] = dsnew[...].reshape(flat.shape)
+    next(folds)
+    mixing = mixer_back_steps(
+        xe, mk, cw, cum_t, cum, dt_t, we_t, skip, doc_c, doc_r, pre, xo, dm, dc, flat, dpre, dcw, dskip, dinc, bias
+    )
+    next(mixing)
+    next(folds)
+    pump()
+    next(mixing)
+    pump()
+    next(mixing)
+    next(folds)
+    pump()
+    next(mixing)
+    prior = rcopy(pc, dpre.at[pl.ds(0, 8), :], edge, esem.at[0], esem.at[1], (lax.rem(pc.ctx + n - 1, n), pc.y))
+    pl.when(pc.ctx > 0)(lambda: prior.start())
+    for _ in mixing:
+        pass
+    pump()
+    for _ in folds:
+        pass
+    dproj[:, pl.ds(QUERY_WIDTH, KEY_WIDTH)] = rotate(dkv_own[:, pl.ds(0, KEY_WIDTH)], cos_w, sin_w).astype(BF)
+    dproj[:, pl.ds(QUERY_WIDTH + KEY_WIDTH, KEY_WIDTH)] = dkv_own[:, pl.ds(KEY_WIDTH, KEY_WIDTH)].astype(BF)
+    pl.when(pc.ctx < n - 1)(lambda: prior.wait_recv())
+
+    @pl.when(pc.ctx == n - 1)
+    def _():
+        edge[...] = jnp.zeros_like(edge)
+
+    dpre[pl.ds(rows, 8), :] = edge[...]
+    for i in range(XBC // 256):
+        sl = pl.ds(i * 256, 256)
+        total_grad = jnp.zeros((rows, 256), F32)
+        for j in range(CONV):
+            total_grad = total_grad + cw[j : j + 1, sl] * (
+                dpre[pl.ds(CONV - 1 - j, rows), sl] * mk_next[:, j : j + 1]
+            )
+        dproj[:, pl.ds(XBC_AT + i * 256, 256)] = total_grad.astype(BF)
+    for _ in states:
+        pass
+    pl.when(pc.ctx > 0)(lambda: prior.wait_send())
+    for _ in side:
+        pass
+
+
+def back(planes, lefts, rights, args, block, collective):
+    count = len(lefts)
+    n = 4 * planes
+    rows = args[-1].shape[0]
+    keys = n * rows
+    outs = [
+        jax.ShapeDtypeStruct((rows, MIXIN), BF),
+        jax.ShapeDtypeStruct((1, INNER), F32),
+        jax.ShapeDtypeStruct((CONV + 1, XBC), F32),
+        jax.ShapeDtypeStruct((1, INNER), F32),
+    ]
+    scratch = [
+        pltpu.VMEM((rows, INNER), BF),
+        pltpu.VMEM((rows, INNER), BF),
+        pltpu.VMEM((rows, NS), F32),
+        pltpu.VMEM((n, NS // n, INNER), BF),
+        pltpu.VMEM((n, NS // n, INNER), BF),
+        pltpu.VMEM((NS, INNER), BF),
+        pltpu.VMEM((QUERY_HEADS * rows, HEAD_WIDTH), BF),
+        pltpu.VMEM((QUERY_HEADS * rows, HEAD_WIDTH), BF),
+        pltpu.VMEM((QUERY_HEADS, rows), F32),
+        pltpu.VMEM((QUERY_WIDTH, rows), F32),
+        pltpu.VMEM((keys, 2 * KEY_WIDTH), BF),
+        pltpu.VMEM((rows, 2 * KEY_WIDTH), F32),
+        pltpu.VMEM((rows + 8, XBC), F32),
+        pltpu.VMEM((8, XBC), F32),
+        pltpu.VMEM((rows, rows), F32),
+        DMA((2,)),
+    ]
+    scratch += relay_scratch(planes) + fold_scratch(planes, rows, 2 * KEY_WIDTH)
+    if count:
+        widths = [r.shape[1] for r in rights]
+        each = lefts[0].shape[1] // n
+        outs = [jax.ShapeDtypeStruct((each, sum(widths)), F32)] + outs
+        scratch += scatter_scratch(planes, each, widths)
     return pl.pallas_call(
-        mixer_back_kernel,
+        functools.partial(back_kernel, planes, count, block),
+        out_shape=tuple(outs),
+        in_specs=[VM] * (2 * count + len(args)),
+        out_specs=(VM,) * len(outs),
+        scratch_shapes=scratch,
+        compiler_params=params(collective),
+    )(*lefts, *rights, *args)
+
+
+def last_kernel(planes, left, dproj, w_ref, tok, scale, gain, dres, small, scattered, dhid, totals, dn, *scratch):
+    pc = Place(planes)
+    peers = plane_peers(pc)
+    bar = pltpu.get_barrier_semaphore()
+    for d in [pc.near(k) for k in "cxy"] + peers:
+        pl.semaphore_signal(bar, inc=1, device_id=d, device_id_type=MESH)
+    pl.semaphore_wait(bar, 3 + len(peers))
+    rows = dproj.shape[0]
+    side = scatter_steps(pc, ((left, dproj),), scattered, scratch[6:])
+    next(side)
+    for i in range(D // 256):
+        dn[:, pl.ds(i * 256, 256)] = nt(dproj[...], w_ref[pl.ds(i * 256, 256), :])
+        if i == 0:
+            next(side)
+    for _ in range(planes - 1):
+        next(side)
+    totals[...] = small[...]
+    for i in range(rows // 64):
+        r = pl.ds(i * 64, 64)
+        v, g, f = tok[r, :].astype(F32), dn[r, :], scale[r, :]
+        w = g * gain[...]
+        dhid[r, :] = dres[r, :] + f * (w - v * f * f * jnp.mean(w * v, axis=1, keepdims=True))
+        part = jnp.sum(g * v * f, axis=0, keepdims=True)
+        for t in range(D // 128):
+            totals[t : t + 1, :] = totals[t : t + 1, :] + part[:, t * 128 : (t + 1) * 128]
+    sums = total_steps(pc, totals, scratch[:6])
+    next(sums)
+    for _ in range(3):
+        next(side)
+        next(sums)
+    for _ in side:
+        next(sums, None)
+    for _ in sums:
+        pass
+
+
+def last(planes, left, dproj, w, tok, scale, gain, dres, small, collective):
+    rows = dproj.shape[0]
+    each = left.shape[1] // (4 * planes)
+    return pl.pallas_call(
+        functools.partial(last_kernel, planes),
         out_shape=(
-            jax.ShapeDtypeStruct((rows, XBC), F32),
-            jax.ShapeDtypeStruct((CONV + 1, XBC), F32),
-            jax.ShapeDtypeStruct((1, INNER), F32),
+            jax.ShapeDtypeStruct((each, MIXIN), F32),
+            jax.ShapeDtypeStruct((rows, D), F32),
+            jax.ShapeDtypeStruct((SMALL_ROWS, 128), F32),
         ),
-        in_specs=[VM] * 15,
+        in_specs=[VM] * 8,
         out_specs=(VM,) * 3,
-        scratch_shapes=[pltpu.VMEM((rows, INNER), BF), pltpu.VMEM((rows, rows), F32)],
-        compiler_params=params(),
-    )(xe, mk, cw, cum_t, cum, dt_t, we_t, skip, doc_c, doc_r, pre, xo, dm, dc_in, ds)
+        scratch_shapes=[pltpu.VMEM((rows, D), F32)]
+        + total_scratch(planes)
+        + scatter_scratch(planes, each, [MIXIN]),
+        compiler_params=params(collective),
+    )(left, dproj, w, tok, scale, gain, dres, small)
 
 
 def doc_layout(lengths, token_positions):
@@ -1309,75 +1537,51 @@
     grad_norm_two, grad_gain_two = norm_backward(grad_normed_two, resid_one, scale_two, gain_two)
     grad_resid_one = grad_out.astype(jnp.float32) + grad_norm_two
     grad_resid_b = grad_resid_one.astype(jnp.bfloat16)
-    mlp_grads = scatter_rows(planes, normed_two.T, grad_gate_up, grad_out.T, hidden_mid, 3)
 
     grad_branch = jnp.dot(grad_resid_b, mixer_w[:, MIXIN:], preferred_element_type=jnp.float32)
-    grad_attended = grad_branch[:, :QUERY_WIDTH].astype(jnp.bfloat16)
-    grad_mixed, grad_gate_in, grad_gate_gain, grad_state, grad_c = gate_back(
-        grad_branch[:, QUERY_WIDTH:], mixed, gate_in, gate_gain[None, :], din_t, xo, state_in
-    )
-    grad_state_out = relay(planes, True, grad_state, decays, 4)
-    delta = jnp.sum(
-        (grad_attended.astype(jnp.float32) * attended.astype(jnp.float32)).reshape(
-            local_rows, QUERY_HEADS, HEAD_WIDTH
-        ),
-        axis=-1,
-    ).T
-    grad_query, kv_grads = attend_back(
-        span, query_heads, by_head(grad_attended), kv_flat, pos, log_sums, delta, block
-    )
-    grad_pre, conv_grads, skip_grads = mixer_back(
-        xe, same_doc, conv_w, cum_t, cum, dt_t, we_t, skip_wide, doc_c, doc_r,
-        pre, xo, grad_mixed, grad_c, grad_state_out,
-    )
-    key_gradients, pre_next = fold(
-        planes, kv_grads.reshape(count, local_rows, 2 * KEY_WIDTH), grad_pre[:8], 5
-    )
-    pre_ext = jnp.concatenate([grad_pre, pre_next[: CONV - 1]], axis=0)
-    doc_next = near_doc[CONV - 1 :]
-    grad_xbc = sum(
-        conv_w[j][None, :]
-        * pre_ext[CONV - 1 - j : CONV - 1 - j + local_rows]
-        * (doc_next[CONV - 1 - j : CONV - 1 - j + local_rows] == document_index)[:, None]
-        for j in range(CONV)
-    )
-    grad_q = inverse_rotary(
-        grad_query.reshape(local_rows, QUERY_HEADS, HEAD_WIDTH), cosine_table, sine_table
-    ).reshape(local_rows, QUERY_WIDTH)
-    key_gradient = inverse_rotary(
-        key_gradients[:, :KEY_WIDTH].reshape(local_rows, KEY_VALUE_HEADS, HEAD_WIDTH),
-        cosine_table,
-        sine_table,
-    ).reshape(local_rows, KEY_WIDTH)
-    grad_proj = jnp.concatenate(
+    same_next = jnp.stack(
         [
-            grad_q.astype(jnp.bfloat16),
-            key_gradient.astype(jnp.bfloat16),
-            key_gradients[:, KEY_WIDTH:].astype(jnp.bfloat16),
-            grad_gate_in,
-            grad_xbc.astype(jnp.bfloat16),
+            near_doc[2 * (CONV - 1) - j : 2 * (CONV - 1) - j + local_rows] == document_index
+            for j in range(CONV)
         ],
         axis=1,
-    )
-    mixer_grads = scatter_rows(planes, normed_one.T, grad_proj, grad_resid_b.T, branch, 6)
-    grad_normed_one = lax.dot_general(
-        grad_proj, mixer_w[:, :MIXIN], contract_last, preferred_element_type=jnp.float32
-    )
-    grad_norm_one, grad_gain_one = norm_backward(grad_normed_one, tok_f, scale_one, gain_one)
-    grad_hidden = (grad_resid_one + grad_norm_one)[None]
+    ).astype(jnp.float32)
+    cos_wide = jnp.tile(cosine_table, (1, 4))
+    sin_back = jnp.tile(jnp.concatenate([sine_table, -sine_table], axis=1), (1, 2))
+    lefts = [by_core(v, planes) for v in (normed_two, grad_out, grad_resid_b)]
+    rights = [grad_gate_up, hidden_mid, branch]
+    args = (
+        grad_branch, mixed, gate_in, gate_gain[None, :], din_t, xo, state_in,
+        query_rows.reshape(local_rows, QUERY_WIDTH), kv_flat, pos, log_sums, cos_wide, sin_back, decays,
+        xe, same_doc, same_next, conv_w, cum_t, cum, dt_t, we_t, skip_wide, doc_c, doc_r, pre,
+    )
+    if planes <= 4:
+        early, grad_proj, gate_gain_grads, conv_grads, skip_grads = back(
+            planes, lefts, rights, args, block, 3
+        )
+    else:
+        early = scatter_rows(planes, lefts, rights, 4)
+        grad_proj, gate_gain_grads, conv_grads, skip_grads = back(planes, [], [], (branch,) + args, block, 3)
     small_local = jnp.concatenate(
         [
-            grad_gain_one,
+            jnp.zeros((D,), jnp.float32),
             grad_gain_two,
-            grad_gate_gain[0],
+            gate_gain_grads[0],
             conv_grads.reshape(-1),
             jnp.sum(skip_grads.reshape(MH, MP), axis=1),
         ]
     )
     size = small_local.shape[0]
     padded = jnp.pad(small_local, (0, SMALL_ROWS * 128 - size)).reshape(SMALL_ROWS, 128)
-    small_grads = total_small(planes, padded, 7).reshape(-1)[:size]
-    grad_weights = jnp.concatenate([mixer_grads, mlp_grads], axis=1)
+    mixin_grads, grad_hidden, totals = last(
+        planes, by_core(normed_one, planes), grad_proj, mixer_w[:, :MIXIN], hidden[0], scale_one,
+        gain_one[None, :], grad_resid_one, padded, 5,
+    )
+    grad_hidden = grad_hidden[None]
+    small_grads = totals.reshape(-1)[:size]
+    grad_weights = jnp.concatenate(
+        [mixin_grads, early[:, 3 * FF :], early[:, : 3 * FF]], axis=1
+    )
     new_weights, new_first, new_second = adamw_step(
         weights, grad_weights, first_moment, second_moment, decay_rate
     )

time: 558 us -> 461 us (0.83)
  Pallas kernels: 434 us -> 336 us
    pallas_call x2 -> x1, Pallas kernels: 86.9 us -> 32 us  [relay(): pl.pallas_call(functools.partial(relay_kernel, planes, reverse), out_shap...]
    pallas_call x7 -> x2, Pallas kernels: 236 us -> 194 us  [the longest x1 133 us: back(): pl.pallas_call(functools.partial(back_kernel, planes, count, block), out_...]
    unnamed x67 -> x70, local copies, waits for them, and re-layouts: 11.5 us -> 3.7 us
    dot_general x1 -> x0, matrix products: 6.38 us -> none  [shards(): lax.dot_general(grad_proj, mixer_w[:, :MIXIN], contract_last, preferred_e...]
    transpose x0 -> x8, local copies, waits for them, and re-layouts: none -> 5.6 us  [the longest x4 3.34 us: by_core(): return cut.transpose(1, 0, 2, 3).reshape(2, D // 2, tokens)]
  transfers between devices with their start and end apart: 1 -> 1, of which waited for: 0 -> 0; matrix products, arithmetic and copies ran while one was open for 7% -> 12% of each run, Pallas kernels for 26% -> 31%
where the time goes in v2:
time: 461 us; the launch traced here: 455 us
  Pallas kernels  336 us (73%)
  local copies, waits for them, and re-layouts  42.7 us (9%)
  matrix products  32.7 us (7%)
  other arithmetic  25.8 us (6%)
  between operations  17.7 us (4%)
    pallas_call x1, Pallas kernels, back(): pl.pallas_call(functools.partial(back_kernel, planes, count, block), out_...  133 us
    pallas_call x1, Pallas kernels, gather_rows(): pl.pallas_call(functools.partial(gather_kernel, planes), out_shape=jax.Sh...  76.8 us
    pallas_call x1, Pallas kernels, last(): pl.pallas_call(functools.partial(last_kernel, planes), out_shape=(jax.Sha...  60.9 us
    pallas_call x1, Pallas kernels, relay(): pl.pallas_call(functools.partial(relay_kernel, planes, reverse), out_shap...  32 us
    pallas_call x1, Pallas kernels, spread(): pl.pallas_call(functools.partial(spread_kernel, planes), out_shape=(jax.S...  12.7 us
  transfers between devices with their start and end apart: 1, of which 0 were waited for; matrix products, arithmetic and copies ran while one was open for 12% of the time, Pallas kernels for 31%

profile of v2, /device:TPU:0, one launch (start us, length us, event | category | flops | bytes accessed | tf_op | source)
XLA Modules:
  0.0 455.1 jit_solution(4819545299980427650)
XLA Ops:
  9.7 76.8 %shard_map.177 = bf16[32,32,6144]{2,1,0:T(8,128)(2,1)} custom-call(bf16[32,6144]{1,0:T(8,128)(2,1)} %get-tuple-element.81.w_ref), custom_call_target="tpu_custom_call" | custom-call | tf_op jit(solution)/shard_map/pallas_call | solution.py:273
  87.3 7.9 %fusion.47 = (bf16[256,4096]{1,0:T(8,128)(2,1)S(1)}, f32[256,4096]{1,0:T(8,128)}) fusion(bf16[1024,6144]{1,0:T(8,128)(2,1)} %bitcast.92, f32[1024]{0:T(1024)S(1)} %get-tuple-element.89, f32[256]{0:T(256)S(1)} %add_rsqrt_fusion.1, bf16[1,256,1024]{2,1,0:T(8,128)(2,1)S(1)} %copy-done.1), kind=kOutput, calls=%fused_computation.112 | convolution fusion | flops 2149580800 | bytes 15209472 | tf_op jit(solution)/shard_map/dot_general | solution.py:1458
  98.3 2.7 slice.204.gate.refs_8_
  106.1 8.1 %slice.194.w_ref = bf16[1024,4096]{1,0:T(8,128)(2,1)} slice(bf16[1024,6144]{1,0:T(8,128)(2,1)} %bitcast.93), slice={[0:1024], [0:4096]} | slice | bytes 16777216 | tf_op jit(solution)/shard_map/slice | solution.py:1458
  118.2 1.9 slice_compare_fusion.2
  126.5 12.7 %shard_map.178 = (bf16[16,256,256]{2,1,0:T(8,128)(2,1)}, bf16[16,1792]{1,0:T(8,128)(2,1)}, f32[16,8,128]{2,1,0:T(8,128)}) custom-call(bf16[256,256]{1,0:T(8,128)(2,1)} %pad_maximum_fusion.3.kv_ref, bf16[16,1792]{1,0:T(8,128)(2,1)} %slice.199.edge_ref, f32[8,128]{1,0:T(8,128)} %scatter.4.dec_ref), custom_call_target="tpu_custom_call" | custom-call | tf_op jit(solution)/shard_map/pallas_call | solution.py:372
  152.9 8.5 %shard_map.179 = (bf16[256,1792]{1,0:T(8,128)(2,1)}, bf16[256,1792]{1,0:T(8,128)(2,1)}, f32[256,1536]{1,0:T(8,128)}, bf16[128,1536]{1,0:T(8,128)(2,1)}) custom-call(f32[264,1792]{1,0:T(8,128)} %pad_maximum_fusion.1.xe.refs_20_, f32[256,4]{1,0:T(8,128)} %convert_element_type.70.mk.refs_21_, f32[4,1792]{1,0:T(4,128)} %reshape.320.cw.refs_23_, ...), custom_call_target="tpu_custom_call" | custom-call | tf_op jit(solution)/shard_map/pallas_call | solution.py:963
  161.4 32.0 %shard_map.180 = bf16[16,8,1536]{2,1,0:T(8,128)(2,1)} custom-call(bf16[16,8,1536]{2,1,0:T(8,128)(2,1)} %bitcast.123, f32[16,1536]{1,0:T(8,128)} %reshape.322.dec_ref.refs_19_), custom_call_target="tpu_custom_call" | custom-call | tf_op jit(solution)/shard_map/pallas_call | solution.py:760
  194.6 6.5 %shard_map.181 = (bf16[256,512]{1,0:T(8,128)(2,1)}, f32[8,256]{1,0:T(8,128)}) custom-call(s32[2]{0:T(128)} %pad_add_fusion.1.span_ref, bf16[2048,64]{1,0:T(8,128)(2,1)} %bitcast.107, bf16[4096,256]{1,0:T(8,128)(2,1)} %bitcast.96, s32[2,256]{1,0:T(2,128)} %pad_add_fusion.pos_ref.refs_15_), custom_call_target="tpu_custom_call" | custom-call | tf_op jit(solution)/shard_map/pallas_call | solution.py:878
  201.1 6.0 %shard_map.182 = (bf16[256,1536]{1,0:T(8,128)(2,1)}, bf16[256,2048]{1,0:T(8,128)(2,1)}) custom-call(f32[256,1536]{1,0:T(8,128)} %get-tuple-element.42.mix, bf16[256,1792]{1,0:T(8,128)(2,1)} %get-tuple-element.43.xo.refs_11_, bf16[128,1536]{1,0:T(8,128)(2,1)} %bitcast.99, f32[256,24]{1,0:T(8,128)} %bitcast.116, f32[256,1536]{1,0:T(8,128)} %slice.204.gate.refs_8_, ...), custom_call_target="tpu_custom_call" | custom-call | tf_op jit(solution)/shard_map/pallas_call | solution.py:1013
  207.1 3.9 multiply_reduce_fusion.2
  211.1 6.2 %fusion.2 = f32[256,4096]{1,0:T(8,128)S(1)} fusion(bf16[1024,6144]{1,0:T(8,128)(2,1)} %all-gather.2.cloned.1.call-done, f32[256,1024]{1,0:T(8,128)S(1)} %get-tuple-element.110, f32[1024]{0:T(1024)S(1)} %copy-done.22, f32[256]{0:T(256)S(1)} %add_rsqrt_fusion), kind=kOutput, calls=%fused_computation.2 | convolution fusion | flops 2148270080 | bytes 13636608 | tf_op jit(solution)/shard_map/dot_general | solution.py:1518
  218.3 3.0 multiply_convert_fusion.1
  221.3 1.6 pad_maximum_fusion.refs_3_
  222.9 2.6 multiply_reduce_fusion
  225.5 2.7 convert_bitcast_fusion
  228.2 1.6 copy.124
  231.8 4.7 %fusion.8.refs_6_ = f32[256,2048]{1,0:T(8,128)} fusion(bf16[1024,6144]{1,0:T(8,128)(2,1)} %bitcast.95, f32[256,1024]{1,0:T(8,128)S(1)} %get-tuple-element.73.dres), kind=kOutput, calls=%fused_computation.8 | convolution fusion | flops 1074003968 | bytes 7340032 | tf_op jit(solution)/shard_map/dot_general | solution.py:1541
  236.5 132.9 %shard_map.183 = (f32[32,8192]{1,0:T(8,128)}, bf16[256,4096]{1,0:T(8,128)(2,1)}, f32[1,1536]{1,0:T(1,128)}, f32[5,1792]{1,0:T(8,128)}, f32[1,1536]{1,0:T(1,128)}) custom-call(bf16[2,512,256]{2,1,0:T(8,128)(2,1)} %bitcast.108, bf16[2,512,256]{2,1,0:T(8,128)(2,1)} %bitcast.106, bf16[2,512,256]{2,1,0:T(8,128)(2,1)} %bitcast.109, ...), custom_call_target="tpu_custom_call" | custom-call | tf_op jit(solution)/shard_map/pallas_call | solution.py:1259
  369.4 2.1 slice.191
  374.5 60.9 %shard_map.184 = (f32[32,4096]{1,0:T(8,128)}, f32[256,1024]{1,0:T(8,128)}, f32[104,128]{1,0:T(8,128)}) custom-call(bf16[2,512,256]{2,1,0:T(8,128)(2,1)} %bitcast.110, bf16[256,4096]{1,0:T(8,128)(2,1)} %get-tuple-element.52.dproj, bf16[1024,4096]{1,0:T(8,128)(2,1)} %slice.194.w_ref, bf16[256,1024]{1,0:T(8,128)(2,1)} %bitcast.98, f32[256,1]{1,0:T(8,128)} %copy.136.scale, ...), custom_call_target="tpu_custom_call" | custom-call | tf_op jit(solution)/shard_map/pallas_call | solution.py:1308
  435.4 1.5 add_divide_fusion.1
  436.9 5.4 %multiply_subtract_fusion = (f32[32,12288]{1,0:T(8,128)}, f32[32,12288]{1,0:T(8,128)}, f32[32,12288]{1,0:T(8,128)}, f32[32,12288]{1,0:T(8,128)}) fusion(f32[32,12288]{1,0:T(8,128)S(1)} %copy-done, f32[32,12288]{1,0:T(8,128)} %param.17, f32[32,12288]{1,0:T(8,128)} %param.18, f32[32,6144]{1,0:T(8,128)} %slice.191, f32[32,2048]{1,0:T(8,128)S(1)} %slice.190, ...), kind=kLoop, calls=%fused_computation.22 | loop fusion | flops 6684672 | bytes 12582912 | tf_op jit(solution)/shard_map/sub | solution.py:1396
  442.4 4.5 fusion.22
  (174 shorter events, 41.1 us)
Async XLA Ops:
  7.2 203.9 %all-gather.2.cloned.1.call-start = ((), (), s32[]{:S(2)}) async-start(), calls=%async_computation | async-start | bytes 12976128 | tf_op jit(solution)/shard_map/all_gather | solution.py:1457
  9.7 76.8 %copy-start.1 = (bf16[1,256,1024]{2,1,0:T(8,128)(2,1)S(1)}, bf16[1,256,1024]{2,1,0:T(8,128)(2,1)}, u32[]{:S(2)}) copy-start(bf16[1,256,1024]{2,1,0:T(8,128)(2,1)} %param.12) | copy-start | bytes 1572868
  9.7 77.0 %copy-start.15 = (f32[12568]{0:T(1024)S(1)}, f32[12568]{0:T(1024)}, u32[]{:S(2)}) copy-start(f32[12568]{0:T(1024)} %param.19) | copy-start | bytes 150820
  86.7 8.5 %copy-start.23 = (f32[256]{0:T(256)}, f32[256]{0:T(256)S(1)}, u32[]{:S(2)}) copy-start(f32[256]{0:T(256)S(1)} %add_rsqrt_fusion.1) | copy-start | bytes 3076
  87.3 7.9 %copy-start.18 = (f32[1024]{0:T(1024)}, f32[1024]{0:T(1024)S(1)}, u32[]{:S(2)}) copy-start(f32[1024]{0:T(1024)S(1)} %get-tuple-element.89) | copy-start | bytes 12292
  87.3 9.9 %copy-start.13 = (f32[1,24,256]{2,1,0:T(8,128)S(1)}, f32[1,24,256]{2,1,0:T(8,128)}, u32[]{:S(2)}) copy-start(f32[1,24,256]{2,1,0:T(8,128)} %param.14) | copy-start | bytes 73732
  95.2 6.3 %copy-start.31 = (s32[1,2]{1,0:T(1,128)S(1)}, s32[1,2]{1,0:T(1,128)}, u32[]{:S(2)}) copy-start(s32[1,2]{1,0:T(1,128)} %param.15) | copy-start | bytes 28
  101.8 12.4 %copy-start.25 = (s32[256]{0:T(256)}, s32[256]{0:T(256)S(1)}, u32[]{:S(2)}) copy-start(s32[256]{0:T(256)S(1)} %get-tuple-element.63) | copy-start | bytes 3076
  116.2 26.3 %copy-start.3 = (f32[24,2,128]{0,2,1:T(8,128)}, f32[24,2,128]{0,2,1:T(8,128)S(1)}, u32[]{:S(2)}) copy-start(f32[24,2,128]{0,2,1:T(8,128)S(1)} %copy.114) | copy-start | bytes 73732
  116.9 8.9 %copy-start.20 = (s32[256]{0:T(256)}, s32[256]{0:T(256)S(1)}, u32[]{:S(2)}) copy-start(s32[256]{0:T(256)S(1)} %broadcast_add_fusion.2) | copy-start | bytes 3076
  120.9 21.7 %copy-start.6 = (f32[24,256]{0,1:T(8,128)}, f32[24,256]{0,1:T(8,128)S(1)}, u32[]{:S(2)}) copy-start(f32[24,256]{0,1:T(8,128)S(1)} %get-tuple-element.87) | copy-start | bytes 73732
  126.5 17.1 %copy-start.4 = (bf16[1,256,1024]{2,1,0:T(8,128)(2,1)S(1)}, bf16[1,256,1024]{2,1,0:T(8,128)(2,1)}, u32[]{:S(2)}) copy-start(bf16[1,256,1024]{2,1,0:T(8,128)(2,1)} %param.13) | copy-start | bytes 1572868
  142.6 4.5 copy-start.21
  142.6 5.3 %copy-start.24 = (f32[256]{0:T(256)S(1)}, f32[256]{0:T(256)}, u32[]{:S(2)}) copy-start(f32[256]{0:T(256)} %copy-done.23) | copy-start | bytes 3076
  143.6 5.1 %copy-start.29 = (pred[256]{0:T(512)(128)(4,1)S(1)}, pred[256]{0:T(512)(128)(4,1)}, u32[]{:S(2)}) copy-start(pred[256]{0:T(512)(128)(4,1)} %get-tuple-element.91) | copy-start | bytes 772
  152.9 41.1 %copy-start.26 = (s32[256]{0:T(256)S(1)}, s32[256]{0:T(256)}, u32[]{:S(2)}) copy-start(s32[256]{0:T(256)} %copy-done.25) | copy-start | bytes 3076
  211.0 11.9 %copy-start.9 = (f32[256,1024]{1,0:T(8,128)}, f32[256,1024]{1,0:T(8,128)S(1)}, u32[]{:S(2)}) copy-start(f32[256,1024]{1,0:T(8,128)S(1)} %get-tuple-element.110) | copy-start | bytes 3145732
  211.0 7.3 %copy-start.30 = (bf16[1024,6144]{1,0:T(8,128)(2,1)S(1)}, bf16[1024,6144]{1,0:T(8,128)(2,1)}, u32[]{:S(2)}) copy-start(bf16[1024,6144]{1,0:T(8,128)(2,1)} %all-gather.2.cloned.1.call-done) | copy-start | bytes 37748740
  374.5 60.9 %copy-start.16 = (f32[12568]{0:T(1024)S(1)}, f32[12568]{0:T(1024)}, u32[]{:S(2)}) copy-start(f32[12568]{0:T(1024)} %param.20) | copy-start | bytes 150820
  374.5 60.9 %copy-start.17 = (f32[12568]{0:T(1024)S(1)}, f32[12568]{0:T(1024)}, u32[]{:S(2)}) copy-start(f32[12568]{0:T(1024)} %param.21) | copy-start | bytes 150820
  374.5 62.4 %copy-start = (f32[32,12288]{1,0:T(8,128)S(1)}, f32[32,12288]{1,0:T(8,128)}, u32[]{:S(2)}) copy-start(f32[32,12288]{1,0:T(8,128)} %param.16) | copy-start | bytes 4718596
  436.9 5.4 %copy-start.7 = (bf16[256,2048]{1,0:T(8,128)(2,1)S(1)}, bf16[256,2048]{1,0:T(8,128)(2,1)}, u32[]{:S(2)}) copy-start(bf16[256,2048]{1,0:T(8,128)(2,1)} %get-tuple-element.78.refs_4_) | copy-start | bytes 3145732
  436.9 5.4 %copy-start.10 = (f32[256,1024]{1,0:T(8,128)S(1)}, f32[256,1024]{1,0:T(8,128)}, u32[]{:S(2)}) copy-start(f32[256,1024]{1,0:T(8,128)} %copy-done.9) | copy-start | bytes 3145732
  442.4 4.5 copy-start.8
  (9 other events, 30.1 us)
Sparse Core Ops, SparseCore 0:
  10.9 113.2 all-gather.1
